TPU v7x, 32 devices: a whole 2x2x4 slice. The times are simulated.
32 devices in a mesh: dp: 8 (over z, x), blk: 4 (over y, core).
Axes of the slice: x: 2, y: 2, z: 4, core: 2. Of those that a mesh axis runs over, the one named last changes fastest.
Arguments:
- inputs: bfloat16 [8, 1536, 768], P('dp', 'blk'), may hold values from -6 to 6
- clip_ids: int32 [8, 1536], P('dp', 'blk'), may hold values from 0 to 5, as said below
- ln1_gain: bfloat16 [768], P(('dp', 'blk')), may hold values from 0.5 to 1.5
- ln1_bias: bfloat16 [768], P(('dp', 'blk')), may hold values from -4 to 4
- w_qkv: bfloat16 [768, 2304], P(('dp', 'blk')), may hold values from -0.21875 to 0.21875
- qv_bias: bfloat16 [1536], P(('dp', 'blk')), may hold values from -6 to 6
- w_out: bfloat16 [768, 768], P(('dp', 'blk')), may hold values from -6 to 6
- out_bias: bfloat16 [768], P(('dp', 'blk')), may hold values from -4 to 4
- ln2_gain: bfloat16 [768], P(('dp', 'blk')), may hold values from 0.5 to 1.5
- ln2_bias: bfloat16 [768], P(('dp', 'blk')), may hold values from -4 to 4
- w_up: bfloat16 [768, 3072], P(('dp', 'blk')), may hold values from -0.21875 to 0.21875
- up_bias: bfloat16 [3072], P(('dp', 'blk')), may hold values from -4 to 4
- w_down: bfloat16 [3072, 768], P(('dp', 'blk')), may hold values from -0.109375 to 0.109375
- down_bias: bfloat16 [768], P(('dp', 'blk')), may hold values from -4 to 4
- out_grad: bfloat16 [8, 1536, 768], P('dp', 'blk'), may hold values from -6 to 6
Outputs:
- output: bfloat16 [8, 1536, 768], P('dp', 'blk')
- input_grad: float32 [8, 1536, 768], P('dp', 'blk')
- ln1_gain_grad: float32 [768], P(('dp', 'blk'))
- ln1_bias_grad: float32 [768], P(('dp', 'blk'))
- w_qkv_grad: float32 [768, 2304], P(('dp', 'blk'))
- qv_bias_grad: float32 [1536], P(('dp', 'blk'))
- w_out_grad: float32 [768, 768], P(('dp', 'blk'))
- out_bias_grad: float32 [768], P(('dp', 'blk'))
- ln2_gain_grad: float32 [768], P(('dp', 'blk'))
- ln2_bias_grad: float32 [768], P(('dp', 'blk'))
- w_up_grad: float32 [768, 3072], P(('dp', 'blk'))
- up_bias_grad: float32 [3072], P(('dp', 'blk'))
- w_down_grad: float32 [3072, 768], P(('dp', 'blk'))
- down_bias_grad: float32 [768], P(('dp', 'blk'))
Inputs may be any that keep to these rules, and one draw needn't show every extreme that they name: `clip_ids`: in each sequence the clip numbers start at 0 and rise by 0 or 1 from one patch to the next. One sequence holds three clips or fewer, one of which begins among its first 192 patches and ends among its last 192; every other sequence holds exactly six clips, the k-th boundary within 64 patches of k * 256.
All inputs are finite; a program needn't handle non-finite values.
Results may differ from a plain program's by a relative error of at most 0.014.
Values may be sent and summed in bfloat16 or wider, within the bound.
No kernel may reach another device: no remote copies, remote signals or barrier semaphores. Data moves between devices by JAX's collectives and lax.ppermute only.
A program may use at most 192 MiB of HBM per device.

v0:
```python
import functools
import itertools
import math

import jax
import jax.numpy as jnp
from jax import lax
from jax.experimental import pallas as pl
from jax.experimental.pallas import tpu as pltpu
from jax.sharding import PartitionSpec as P

HEAD_DIM = 64
NORM_EPS = 1e-06
LOG2E = math.log2(math.e)
f32 = jnp.float32
bf16 = jnp.bfloat16
AXES = ("dp", "blk")


def mm(a, b, dims=((1,), (0,))):
    return lax.dot_general(a, b, (dims, ((), ())), preferred_element_type=f32)


SMALL = pl.CostEstimate(flops=1000, bytes_accessed=1000, transcendentals=0)


class Grid:
    def __init__(self, dp, blk):
        self.size = {"z": dp // 2, "x": 2, "q": blk // 2, "c": 2}
        self.z, self.x, self.q = dp // 2, 2, blk // 2
        self.chips = self.z * 2 * self.q
        me_dp, me_blk = lax.axis_index("dp"), lax.axis_index("blk")
        self.me = {"z": me_dp // 2, "x": me_dp % 2, "q": me_blk // 2, "c": me_blk % 2}
        self.place = jnp.stack([self.me[a] for a in ("z", "x", "q", "c")]).astype(jnp.int32)

    def flat(self, at):
        return ((at["z"] * self.x + at["x"]) * self.q + at["q"]) * 2 + at["c"]

    def shift(self, value, axis, step):
        pairs = []
        for z in range(self.z):
            for x in range(self.x):
                for q in range(self.q):
                    for c in range(2):
                        at = {"z": z, "x": x, "q": q, "c": c}
                        to = dict(at)
                        to[axis] = (at[axis] + step) % self.size[axis]
                        pairs.append((self.flat(at), self.flat(to)))
        return lax.ppermute(value, AXES, pairs)

    def chip(self, place, dz, dx, dq):
        z = -1 - dz if dz < 0 else lax.rem(place[0] + (self.z - dz), self.z)
        x = lax.rem(place[1] + (self.x - dx), self.x)
        q = lax.rem(place[2] + (self.q - dq), self.q)
        return (z * self.x + x) * self.q + q

    def relative(self, place, chip, near=False):
        z, x, q = chip // (self.x * self.q), chip // self.q % self.x, chip % self.q
        dx = lax.rem(x + self.x - place[1], self.x)
        dq = lax.rem(q + self.q - place[2], self.q)
        if near:
            z = lax.rem(z + self.z - place[0], self.z)
        return dx * self.q + dq, z

    def along(self, value, axis):
        return [self.shift(value, axis, k) for k in range(1, self.size[axis])]

    def line(self, value, others):
        return jnp.stack([value] + others)

    def corner_pieces(self, over, sides):
        half = self.z // 2
        return [
            (self.shift(over[:half], "q", k), self.shift(side[half:], "x", 1))
            for k, side in enumerate(sides, 1)
        ]

    def found(self, line, over, sides, corners, plain=False):
        half = self.z // 2
        zs = [-1 - z if plain else z for z in range(self.z)]
        out = [(line, [(z, 0, 0) for z in zs]), (over, [(z, 1, 0) for z in zs])]
        for k, (side, (a, b)) in enumerate(zip(sides, corners), 1):
            out.append((side, [(z, 0, k) for z in zs]))
            out.append((a, [(z, 1, k) for z in zs[:half]]))
            out.append((b, [(z, 1, k) for z in zs[half:]]))
        return out

    def found_last(self, plane, others):
        at = [(x, q) for x in range(2) for q in range(self.q)]
        return [(p, [(z, x, q) for x, q in at]) for z, p in enumerate([plane] + others)]


    def corners(self, value, first=()):
        half = self.z // 2
        over = value[self.q]
        late, sides = [], []
        for k in range(1, self.q):
            corner = value[self.q + k]
            got = behind(self.shift(corner[:half], "x", 1), first)
            late.append(behind(self.shift(corner[half:], "q", k), first))
            side = value[k]
            sides.append(jnp.concatenate([total_of(side[:half], got).astype(bf16), side[half:]]))
        over = jnp.concatenate([over[:half], total_of(over[half:], *late).astype(bf16)])
        return over, sides

    def edges(self, value, over, sides, first=()):
        parts = [self.shift(over, "x", 1)]
        parts += [self.shift(s, "q", k) for k, s in enumerate(sides, 1)]
        parts = behind(parts, first)
        return total_of(value[0], *parts).astype(bf16)

    def column(self, own):
        return total_of(*self.exchange(own))

    def column_near(self, own):
        return total_of(own[0], *(self.shift(own[k], "z", k) for k in range(1, self.z)))

    def groups(self, axes):
        names = ("z", "x", "q", "c")
        rest = [n for n in names if n not in axes]
        out = []
        for fixed in itertools.product(*(range(self.size[n]) for n in rest)):
            at = dict(zip(rest, fixed))
            out.append(
                [
                    self.flat({**at, **dict(zip(axes, v))})
                    for v in itertools.product(*(range(self.size[n]) for n in axes))
                ]
            )
        return out

    def exchange(self, blocks):
        return lax.all_to_all(
            blocks, AXES, 0, 0, axis_index_groups=self.groups(("z",)), tiled=True
        )

    def gather_chips(self, value):
        return lax.all_gather(
            value, AXES, axis=0, axis_index_groups=self.groups(("z", "x", "q")), tiled=True
        )


def total_of(*values):
    return sum(v.astype(f32) for v in values)


def lock(*values):
    return lax.optimization_barrier(values)


def behind(value, *others):
    return lax.optimization_barrier((value, others))[0]


def call(kernel, place, operands, **kw):
    spec = pltpu.PrefetchScalarGridSpec(
        num_scalar_prefetch=1,
        grid=kw.pop("grid"),
        in_specs=kw.pop("in_specs"),
        out_specs=kw.pop("out_specs"),
        scratch_shapes=kw.pop("scratch_shapes", []),
    )
    return pl.pallas_call(
        kernel,
        grid_spec=spec,
        compiler_params=pltpu.CompilerParams(vmem_limit_bytes=kw.pop("mib") * 2**20),
        **kw,
    )(place, *operands)


class Pieces:
    def __init__(self, grid, found):
        self.grid = grid
        self.found = found
        self.arrays = [f[0] for f in found]
        self.count = sum(f[0].shape[0] for f in found)

    def copies(self, place, refs, sem, moves):
        out = []
        for ref, (piece, at_chips) in zip(refs, self.found):
            for i, distance in enumerate(at_chips):
                chip = self.grid.chip(place, *distance)
                for at, rows, col, cols, to in moves:
                    source = ref.at[i, pl.ds(at, rows), pl.ds(col, cols)]
                    out.append(pltpu.make_async_copy(source, to(chip), sem.at[len(out)]))
        return out


class Whole:
    def __init__(self, arrays):
        self.arrays = arrays
        self.count = 1


def pick(grid, found, first, lanes):
    arrays = [f[0][:, first:, :lanes] for f in found]
    rows = arrays[0].shape[1]

    def kernel(place, *refs):
        for ref, (piece, at_chips) in zip(refs[:-1], found):
            for i, distance in enumerate(at_chips):
                refs[-1][grid.chip(place, *distance)] = ref[i]

    return call(
        kernel,
        grid.place,
        arrays,
        grid=(1,),
        in_specs=[pl.BlockSpec(a.shape, lambda i, s: (0, 0, 0)) for a in arrays],
        out_specs=pl.BlockSpec((grid.chips, rows, lanes), lambda i, s: (0, 0, 0)),
        out_shape=jax.ShapeDtypeStruct((grid.chips, rows, lanes), bf16),
        cost_estimate=SMALL,
        mib=8,
        name="pick",
    )


def vectors_kernel(place, small_ref, out_ref):
    rows, width = small_ref.shape[0], out_ref.shape[1]
    chips = rows // 16
    m = lax.broadcasted_iota(jnp.int32, (128, width), 0)
    j = lax.broadcasted_iota(jnp.int32, (128, width), 1)
    small = small_ref[...]
    narrow, wide = width // chips, 2 * width // chips
    spread = lambda n: mm(small, ((j % n) == m).astype(bf16)).reshape(chips, 16, width)
    one = lax.broadcasted_iota(jnp.int32, (chips, 16, width), 2)
    chip = lax.broadcasted_iota(jnp.int32, (chips, 16, width), 0)
    a, b = spread(narrow), spread(wide)
    plain = jnp.sum(jnp.where(one // narrow == chip, a, 0.0), axis=0)
    low = jnp.sum(jnp.where(one // wide == chip, b, 0.0), axis=0)
    high = jnp.sum(jnp.where(one // wide + chips // 2 == chip, b, 0.0), axis=0)
    out_ref[...] = jnp.concatenate(
        [plain[0:6], low[6:7], high[6:7], low[7:8], high[7:8], plain[0:6]], axis=0
    )


def vectors_of(grid, small, width):
    rows = small.shape[0]
    return call(
        vectors_kernel,
        grid.place,
        [small],
        grid=(1,),
        in_specs=[pl.BlockSpec((rows, 128), lambda i, s: (0, 0))],
        out_specs=pl.BlockSpec((16, width), lambda i, s: (0, 0)),
        out_shape=jax.ShapeDtypeStruct((16, width), f32),
        cost_estimate=SMALL,
        mib=8,
        name="vectors",
    )


def first_lanes(head):
    lane = lax.broadcasted_iota(jnp.int32, (1, 2 * HEAD_DIM), 1)
    return lane < HEAD_DIM if head == 0 else lane >= HEAD_DIM


def chunk_of(rows):
    return 1536 if rows % 1536 == 0 else rows


def attn_fwd_kernel(q_ref, k_ref, v_ref, hot_ref, pen_ref, o_ref, ob_ref, lse_ref):
    total_keys = k_ref.shape[0]
    chunk = chunk_of(total_keys)
    steps = total_keys // chunk
    query_rows = q_ref.shape[0]
    query, hot = q_ref[...], hot_ref[...]
    outs = []
    for head in range(2):
        sel = first_lanes(head)
        q_aug = jnp.where(sel, query, hot)

        def scores(rows):
            k_aug = jnp.where(sel, k_ref[rows, :], pen_ref[rows, :])
            return mm(k_aug, q_aug, ((1,), (1,)))

        def weigh(rows, s, top):
            p = jnp.exp2(s - top)
            added = mm(v_ref[rows, :], p.astype(bf16), ((0,), (0,)))
            return jnp.sum(p, axis=0, keepdims=True), added

        if steps == 1:
            s = scores(slice(0, chunk))
            top = jnp.max(s, axis=0, keepdims=True)
            total, acc = weigh(slice(0, chunk), s, top)
        else:

            def step(i, carry):
                top, total, acc = carry
                rows = pl.ds(pl.multiple_of(i * chunk, chunk), chunk)
                s = scores(rows)
                new_top = jnp.maximum(top, jnp.max(s, axis=0, keepdims=True))
                more, added = weigh(rows, s, new_top)
                fade = jnp.exp2(top - new_top)
                return new_top, total * fade + more, acc * fade + added

            top, total, acc = lax.fori_loop(
                0,
                steps,
                step,
                (
                    jnp.full((1, query_rows), -1e30, f32),
                    jnp.zeros((1, query_rows), f32),
                    jnp.zeros((2 * HEAD_DIM, query_rows), f32),
                ),
            )
        outs.append((acc / total)[head * HEAD_DIM : (head + 1) * HEAD_DIM])
        lse_ref[0, head : head + 1, :] = top + jnp.log2(total)
    out = jnp.concatenate(outs, axis=0).T
    o_ref[...] = out
    ob_ref[...] = out.astype(bf16)


def attn_fwd(queries, keys, values, hot, pen, start, pairs):
    rows, width = queries.shape[0], pairs * 128
    total_keys = keys.shape[0]
    pairs = width // 128
    block = 256 if rows % 256 == 0 else rows
    cost = SMALL
    return pl.pallas_call(
        attn_fwd_kernel,
        grid=(pairs, rows // block),
        in_specs=[
            pl.BlockSpec((block, 128), lambda p, i: (i, p + start)),
            pl.BlockSpec((total_keys, 128), lambda p, i: (0, p + start)),
            pl.BlockSpec((total_keys, 128), lambda p, i: (0, p + start)),
            pl.BlockSpec((block, 128), lambda p, i: (i, 0)),
            pl.BlockSpec((total_keys, 128), lambda p, i: (0, 0)),
        ],
        out_specs=[
            pl.BlockSpec((block, 128), lambda p, i: (i, p)),
            pl.BlockSpec((block, 128), lambda p, i: (i, p)),
            pl.BlockSpec((1, 2, block), lambda p, i: (p, 0, i)),
        ],
        out_shape=[
            jax.ShapeDtypeStruct((rows, width), f32),
            jax.ShapeDtypeStruct((rows, width), bf16),
            jax.ShapeDtypeStruct((pairs, 2, rows), f32),
        ],
        compiler_params=pltpu.CompilerParams(vmem_limit_bytes=16 * 2**20),
        cost_estimate=cost,
        name="attn_fwd",
    )(queries, keys, values, hot, pen)


def attn_bwd_kernel(
    q_ref, k_ref, v_ref, hot_ref, pen_ref, o_ref, do_ref, lse_ref, dq_ref, dk_ref, dv_ref, dk_acc, dv_acc
):
    total_keys = k_ref.shape[0]
    chunk = chunk_of(total_keys)
    steps = total_keys // chunk
    at, last = pl.program_id(1), pl.num_programs(1) - 1
    query, hot, grad = q_ref[...], hot_ref[...], do_ref[...]

    @pl.when(at == 0)
    def _():
        dk_acc[...] = jnp.zeros_like(dk_acc)
        dv_acc[...] = jnp.zeros_like(dv_acc)

    flipped = (grad.astype(f32) * o_ref[...]).T
    zero = jnp.zeros_like(query)

    def step(rows):
        keys, values, pen = k_ref[rows, :], v_ref[rows, :], pen_ref[rows, :]
        dq = None
        dk = dk_acc[rows, :]
        dv = dv_acc[rows, :]
        for head in range(2):
            sel = first_lanes(head)
            delta = jnp.sum(
                flipped[head * HEAD_DIM : (head + 1) * HEAD_DIM], axis=0, keepdims=True
            )
            k_aug = jnp.where(sel, keys, pen)
            s = mm(k_aug, jnp.where(sel, query, hot), ((1,), (1,)))
            p = jnp.exp2(s - lse_ref[0, head : head + 1, :])
            grad_h = jnp.where(sel, grad, zero)
            dp = mm(values, grad_h, ((1,), (1,)))
            ds = (p * (dp - delta)).astype(bf16)
            dv = dv + mm(p.astype(bf16), grad_h)
            dk = dk + mm(ds, jnp.where(sel, query, zero))
            part = mm(keys, ds, ((0,), (0,)))
            part = part[head * HEAD_DIM : (head + 1) * HEAD_DIM]
            dq = part if dq is None else jnp.concatenate([dq, part], axis=0)
        dk_acc[rows, :] = dk
        dv_acc[rows, :] = dv
        return dq

    if steps == 1:
        dq = step(slice(0, chunk))
    else:
        dq = lax.fori_loop(
            0,
            steps,
            lambda i, total: total + step(pl.ds(pl.multiple_of(i * chunk, chunk), chunk)),
            jnp.zeros((2 * HEAD_DIM, query.shape[0]), f32),
        )
    dq_ref[...] = (dq.T * HEAD_DIM**-0.5).astype(bf16)

    @pl.when(at == last)
    def _():
        dk_ref[...] = (dk_acc[...] * (1.0 / LOG2E)).astype(bf16)
        dv_ref[...] = dv_acc[...].astype(bf16)


def attn_bwd(queries, keys, values, hot, pen, attended, d_attended, lse, start, pairs):
    rows = queries.shape[0]
    total_keys = keys.shape[0]
    block = 256 if rows % 256 == 0 else rows
    by_query = pl.BlockSpec((block, 128), lambda p, i: (i, p + start))
    own = pl.BlockSpec((block, 128), lambda p, i: (i, p))
    by_key = pl.BlockSpec((total_keys, 128), lambda p, i: (0, p + start))
    to_query = pl.BlockSpec((block, 128), lambda p, i: (i, p))
    to_key = pl.BlockSpec((total_keys, 128), lambda p, i: (0, p))
    width = pairs * 128
    cost = SMALL
    return pl.pallas_call(
        attn_bwd_kernel,
        grid=(pairs, rows // block),
        in_specs=[
            by_query,
            by_key,
            by_key,
            pl.BlockSpec((block, 128), lambda p, i: (i, 0)),
            pl.BlockSpec((total_keys, 128), lambda p, i: (0, 0)),
            own,
            by_query,
            pl.BlockSpec((1, 2, block), lambda p, i: (p, 0, i)),
        ],
        out_specs=[to_query, to_key, to_key],
        out_shape=[
            jax.ShapeDtypeStruct((rows, width), bf16),
            jax.ShapeDtypeStruct((total_keys, width), bf16),
            jax.ShapeDtypeStruct((total_keys, width), bf16),
        ],
        scratch_shapes=[pltpu.VMEM((total_keys, 128), f32), pltpu.VMEM((total_keys, 128), f32)],
        compiler_params=pltpu.CompilerParams(vmem_limit_bytes=24 * 2**20),
        cost_estimate=cost,
        name="attn_bwd",
    )(queries, keys, values, hot, pen, attended, d_attended, lse)


def halves(place, mine, other):
    first = place[3] == 0
    return jnp.where(first, mine, other), jnp.where(first, other, mine)


def load_all(copies):
    for c in copies:
        c.start()
    for c in copies:
        c.wait()


def qkv_kernel(weights, moves, place, n1_ref, vec_ref, *refs):
    pieces, (q_ref, k_ref, v_ref, h1t_ref, w_out, w_s, sem) = refs[:-7], refs[-7:]
    half = q_ref.shape[1]
    width = n1_ref.shape[1]
    step = pl.program_id(0)

    @pl.when(step == 0)
    def _():
        if isinstance(weights, Pieces):
            load_all(weights.copies(place, pieces, sem, moves(w_s)))
        else:
            load_all([pltpu.make_async_copy(pieces[0], w_s.at[0], sem.at[0])])
        w_out[...] = w_s[...]

    h1 = (n1_ref[...] * vec_ref[0:1, :] + vec_ref[1:2, :]).astype(bf16)
    low, high = vec_ref[6:8, :half], vec_ref[6:8, half:]
    bias = jnp.where(place[3] == 0, low, high)
    w = w_s[...].reshape(width, 3 * half)

    @pl.when(step < 2)
    def _():
        q = mm(h1, w[:, :half]) + bias[0:1]
        q_ref[...] = (q * (LOG2E * HEAD_DIM**-0.5)).astype(bf16)

    kv = mm(h1, w[:, half:])
    k_ref[...] = kv[:, :half].astype(bf16)
    v_ref[...] = (kv[:, half:] + bias[1:2]).astype(bf16)
    h1t_ref[...] = h1.T


def project_qkv(grid, n1, vec, weights, local):
    rows, width = n1.shape
    half = width // 2
    if isinstance(weights, Pieces):
        r = width // grid.chips
        moves = lambda w: [(0, r, 0, 3 * half, lambda chip: w.at[chip])]
        shape = (grid.chips, r, 3 * half)
    else:
        moves = None
        shape = (1, width, 3 * half)
    q, k, v, h1t, w = call(
        functools.partial(qkv_kernel, weights, moves),
        grid.place,
        [n1, vec] + weights.arrays,
        grid=(rows // local,),
        in_specs=[
            pl.BlockSpec((local, width), lambda i, s: (i, 0)),
            pl.BlockSpec(vec.shape, lambda i, s: (0, 0)),
        ]
        + [pl.BlockSpec(memory_space=pl.ANY)] * len(weights.arrays),
        out_specs=[
            pl.BlockSpec((local, half), lambda i, s: (jnp.minimum(i, 1), 0)),
            pl.BlockSpec((local, half), lambda i, s: (i, 0)),
            pl.BlockSpec((local, half), lambda i, s: (i, 0)),
            pl.BlockSpec((width, local), lambda i, s: (0, i)),
            pl.BlockSpec(shape, lambda i, s: (0, 0, 0)),
        ],
        out_shape=[
            jax.ShapeDtypeStruct((2 * local, half), bf16),
            jax.ShapeDtypeStruct((rows, half), bf16),
            jax.ShapeDtypeStruct((rows, half), bf16),
            jax.ShapeDtypeStruct((width, rows), bf16),
            jax.ShapeDtypeStruct(shape, bf16),
        ],
        scratch_shapes=[pltpu.VMEM(shape, bf16), pltpu.SemaphoreType.DMA((weights.count,))],
        cost_estimate=SMALL,
        mib=20,
        name="qkv",
    )
    return q, k, v, h1t, w.reshape(width, 3 * half)


def mean_of(v):
    return jnp.mean(v, axis=-1, keepdims=True)


def join(refs):
    return jnp.concatenate([r[...] for r in refs], axis=1)


def out_kernel(n, place, x_ref, w_ref, vec_ref, *refs):
    (after_ref, h2_ref, n2_ref, rstd_ref) = refs[2 * n :]
    a, b = halves(place, join(refs[:n]), join(refs[n : 2 * n]))
    after = x_ref[...].astype(f32) + mm(a, w_ref[0]) + mm(b, w_ref[1]) + vec_ref[2:3, :]
    after_ref[...] = after
    centered = after - mean_of(after)
    rstd = lax.rsqrt(mean_of(centered * centered) + NORM_EPS)
    n2 = centered * rstd
    n2_ref[...] = n2
    rstd_ref[...] = jnp.broadcast_to(rstd, rstd_ref.shape)
    h2_ref[...] = (n2 * vec_ref[3:4, :] + vec_ref[4:5, :]).astype(bf16)


def project_out(grid, x, mine, other, w, vec):
    rows, width = mine[0].shape[0], x.shape[1]
    block = 256 if rows % 256 == 0 else rows
    line = lambda n: pl.BlockSpec((block, n), lambda i, s: (i, 0))
    return call(
        functools.partial(out_kernel, len(mine)),
        grid.place,
        [x, w, vec] + mine + other,
        grid=(rows // block,),
        in_specs=[
            line(width),
            pl.BlockSpec(w.shape, lambda i, s: (0, 0, 0)),
            pl.BlockSpec(vec.shape, lambda i, s: (0, 0)),
        ]
        + [line(v.shape[1]) for v in mine + other],
        out_specs=[line(width), line(width), line(width), line(128)],
        out_shape=[
            jax.ShapeDtypeStruct((rows, width), f32),
            jax.ShapeDtypeStruct((rows, width), bf16),
            jax.ShapeDtypeStruct((rows, width), f32),
            jax.ShapeDtypeStruct((rows, 128), f32),
        ],
        cost_estimate=SMALL,
        mib=16,
        name="out_proj",
    )


def norm_back(grad, normed, rstd, gain):
    e = grad * gain
    return (e - mean_of(e) - normed * mean_of(e * normed)) * rstd


def sum_rows(v):
    return jnp.sum(v, axis=0, keepdims=True)


def out_back_kernel(
    place, mine_ref, got_ref, dy_ref, n2_ref, rstd_ref, vec_ref, w_ref, after_ref, branch_ref, datt_ref, sums_ref
):
    d_h2 = mine_ref[...] + got_ref[...].astype(f32)
    dy = dy_ref[...].astype(f32)
    n2 = n2_ref[...]
    d_after = dy + norm_back(d_h2, n2, rstd_ref[:, 0:1], vec_ref[3:4, :])
    after_ref[...] = d_after
    branch = d_after.astype(bf16)
    branch_ref[...] = branch
    datt_ref[...] = mm(branch, w_ref[0], ((1,), (1,))).astype(bf16)
    rows = [sum_rows(branch.astype(f32)), sum_rows(d_h2 * n2), sum_rows(d_h2), sum_rows(dy)]
    sums = jnp.concatenate(rows + [jnp.zeros((4, dy.shape[1]), f32)], axis=0) * 0.5

    @pl.when(pl.program_id(0) == 0)
    def _():
        sums_ref[...] = jnp.zeros_like(sums_ref)

    sums_ref[...] += sums


def out_back(grid, mine, got, dy, n2, rstd, vec, w):
    rows, width = mine.shape
    block = 256 if rows % 256 == 0 else rows
    line = lambda n: pl.BlockSpec((block, n), lambda i, s: (i, 0))
    return call(
        out_back_kernel,
        grid.place,
        [mine, got, dy, n2, rstd, vec, w],
        grid=(rows // block,),
        in_specs=[
            line(width),
            line(width),
            line(width),
            line(width),
            line(128),
            pl.BlockSpec(vec.shape, lambda i, s: (0, 0)),
            pl.BlockSpec((1,) + w.shape[1:], lambda i, s: (s[3], 0, 0)),
        ],
        out_specs=[
            line(width),
            line(width),
            line(width // 2),
            pl.BlockSpec((8, width), lambda i, s: (0, 0)),
        ],
        out_shape=[
            jax.ShapeDtypeStruct((rows, width), f32),
            jax.ShapeDtypeStruct((rows, width), bf16),
            jax.ShapeDtypeStruct((rows, width // 2), bf16),
            jax.ShapeDtypeStruct((8, width), f32),
        ],
        cost_estimate=SMALL,
        mib=20,
        name="out_back",
    )


def store_rows(grid, place, ref, value, first, shard, to, tail=()):
    for i in range(value.shape[0] // shard):
        column, z = grid.relative(place, first + i, True)
        at = (column, z) + tail + (pl.ds(to, shard),) + (slice(None),)
        ref[at] = value[i * shard : (i + 1) * shard]


def out_grad_kernel(grid, fast, n, place, d_ref, *refs):
    g_ref = refs[-1]
    parts = halves(place, join(refs[:n]), join(refs[n : 2 * n]))
    for i, part in enumerate(parts):
        g = mm(part, d_ref[...], ((0,), (0,))).astype(bf16)
        if fast:
            shard = 2 * g.shape[0] // grid.chips
            store_rows(grid, place, g_ref, g, i * g.shape[0] // shard, shard, 0)
        else:
            g_ref[i] = g


def out_gradient(grid, fast, mine, other, branch):
    rows, half = branch.shape[0], branch.shape[1] // 2
    shape = (2 * grid.q, grid.z, 2 * half // grid.chips, half) if fast else (2, half, half)
    return call(
        functools.partial(out_grad_kernel, grid, fast, len(mine)),
        grid.place,
        [branch] + mine + other,
        grid=(1,),
        in_specs=[pl.BlockSpec((rows, half), lambda i, s: (0, s[3]))]
        + [pl.BlockSpec(v.shape, lambda i, s: (0, 0)) for v in mine + other],
        out_specs=pl.BlockSpec(shape, lambda i, s: (0,) * len(shape)),
        out_shape=jax.ShapeDtypeStruct(shape, bf16),
        cost_estimate=SMALL,
        mib=8,
        name="w_out_grad",
    )


def vector_rows(chips, sums1, sums2, ups):
    width = sums1.shape[1]
    narrow, wide = width // chips, 2 * width // chips
    plain = jnp.concatenate([sums1[0:2], sums2[0:4], sums1[0:2]], axis=0)

    def fold(value, n, chip):
        lane = lax.broadcasted_iota(jnp.int32, (chips, 8, width), 2)
        value = jnp.where(lane // n == chip, value, 0.0).reshape(chips * 8, width)
        m = lax.broadcasted_iota(jnp.int32, (width, 128), 1)
        j = lax.broadcasted_iota(jnp.int32, (width, 128), 0)
        return mm(value.astype(bf16), (j % n == m).astype(bf16)).reshape(chips, 8, 128)

    chip = lax.broadcasted_iota(jnp.int32, (chips, 8, width), 0)
    a = fold(jnp.broadcast_to(plain[None], (chips, 8, width)), narrow, chip)
    low = jnp.concatenate([sums1[2:3], ups[0:1]] * 4, axis=0)
    high = jnp.concatenate([sums1[3:4], ups[1:2]] * 4, axis=0)
    both = jnp.where(chip < chips // 2, low[None], high[None])
    b = fold(both, wide, chip % (chips // 2))
    row = lax.broadcasted_iota(jnp.int32, (chips, 8, 128), 1)
    return jnp.where(row < 6, a, b).astype(bf16)


def qkv_grad_kernel(grid, fast, pairs, more, place, h1t_ref, dq_ref, dk_ref, dv_ref, *refs):
    g_ref = refs[-1]
    chip_rows = dq_ref.shape[0]
    if more:
        rows = vector_rows(grid.chips, *(r[...] for r in refs[:-1]))
        shard = h1t_ref.shape[0] // grid.chips
        rows = jnp.concatenate([rows, jnp.zeros_like(rows)], axis=1)
        for i in range(grid.chips):
            column, z = grid.relative(place, i, True)
            g_ref[column, z, 0, pl.ds(shard, 16), 0:128] = rows[i]
            g_ref[column, z, 0, pl.ds(shard, 16), 128:384] = jnp.zeros((16, 256), bf16)
    for p in range(pairs):
        cols = slice(p * 128, (p + 1) * 128)
        gq = mm(h1t_ref[:, :chip_rows], dq_ref[:, cols])
        gk = mm(h1t_ref[...], dk_ref[:, cols])
        gv = mm(h1t_ref[...], dv_ref[:, cols])
        g = jnp.concatenate([gq, gk, gv], axis=1).astype(bf16)
        if fast:
            store_rows(grid, place, g_ref, g, 0, g.shape[0] // grid.chips, 0, (p,))
        else:
            g_ref[p] = g


def qkv_gradient(grid, fast, h1t, dq, dk, dv, *more):
    width, rows = h1t.shape
    pairs = dq.shape[1] // 128
    if fast:
        shape = (2 * grid.q, grid.z, pairs, width // grid.chips + (16 if more else 0), 384)
    else:
        shape = (pairs, width, 384)
    whole = lambda v: pl.BlockSpec(v.shape, lambda i, s: (0, 0))
    return call(
        functools.partial(qkv_grad_kernel, grid, fast, pairs, len(more)),
        grid.place,
        [h1t, dq, dk, dv] + list(more),
        grid=(1,),
        in_specs=[whole(v) for v in (h1t, dq, dk, dv) + more],
        out_specs=pl.BlockSpec(shape, lambda i, s: (0,) * len(shape)),
        out_shape=jax.ShapeDtypeStruct(shape, bf16),
        cost_estimate=SMALL,
        mib=16,
        name="w_qkv_grad",
    )


def input_back_kernel(parts, place, *refs):
    grads, (w_ref, n1_ref, mine_ref, other_ref, sums_ref) = refs[: 3 * parts], refs[3 * parts :]
    step = pl.program_id(0)
    dq, dk, dv = (
        jnp.concatenate([grads[3 * p + i][...] for p in range(parts)], axis=1) for i in range(3)
    )
    half = dq.shape[1]
    width = n1_ref.shape[1]
    dq = jnp.where(step < 2, dq, jnp.zeros_like(dq))
    d = mm(jnp.concatenate([dq, dk, dv], axis=1), w_ref[...], ((1,), (1,)))
    block, core = step // 2, step % 2

    @pl.when(core == place[3])
    def _():
        mine_ref[block] = d

    @pl.when(core != place[3])
    def _():
        other_ref[block] = d.astype(bf16)

    none = jnp.zeros((1, half), f32)

    def spread(v):
        v = sum_rows(v.astype(f32))
        first = place[3] == 0
        return jnp.concatenate([jnp.where(first, v, none), jnp.where(first, none, v)], axis=1)

    rows = [sum_rows(d * n1_ref[...]), sum_rows(d), spread(dq), spread(dv)]
    sums = jnp.concatenate(rows + [jnp.zeros((4, width), f32)], axis=0)

    @pl.when(step == 0)
    def _():
        sums_ref[...] = jnp.zeros_like(sums_ref)

    sums_ref[...] += sums


def input_back(grid, grads, w, n1, local):
    rows, width = n1.shape
    flat = [g for part in grads for g in part]
    specs = []
    for dq, dk, dv in grads:
        n = dq.shape[1]
        specs.append(pl.BlockSpec((local, n), lambda i, s: (jnp.minimum(i, 1), 0)))
        specs += [pl.BlockSpec((local, n), lambda i, s: (i, 0))] * 2
    shape = (grid.q, local, width)
    return call(
        functools.partial(input_back_kernel, len(grads)),
        grid.place,
        flat + [w, n1],
        grid=(rows // local,),
        in_specs=specs
        + [
            pl.BlockSpec(w.shape, lambda i, s: (0, 0)),
            pl.BlockSpec((local, width), lambda i, s: (i, 0)),
        ],
        out_specs=[
            pl.BlockSpec(shape, lambda i, s: (0, 0, 0)),
            pl.BlockSpec(shape, lambda i, s: (0, 0, 0)),
            pl.BlockSpec((8, width), lambda i, s: (0, 0)),
        ],
        out_shape=[
            jax.ShapeDtypeStruct(shape, f32),
            jax.ShapeDtypeStruct(shape, bf16),
            jax.ShapeDtypeStruct((8, width), f32),
        ],
        cost_estimate=SMALL,
        mib=24,
        name="input_back",
    )


def finish_kernel(n_got, place, *refs):
    mine_ref, got_ref = refs[:2]
    sides = refs[2 : 2 + n_got]
    n1_ref, rstd_ref, after_ref, vec_ref, out_ref = refs[2 + n_got :]
    d = mine_ref[0] + got_ref[0].astype(f32)
    for s in sides:
        d = d + s[...].astype(f32)
    out_ref[...] = after_ref[...] + norm_back(d, n1_ref[...], rstd_ref[...], vec_ref[0:1, :])


def finish(grid, mine, got, sides, n1, rstd1, d_after, vec):
    _, rows, width = mine.shape
    first = pl.BlockSpec((1, rows, width), lambda i, s: (0, 0, 0))
    own = lambda n: pl.BlockSpec((rows, n), lambda i, s: (s[3], 0))
    return call(
        functools.partial(finish_kernel, len(sides)),
        grid.place,
        [mine, got] + sides + [n1, rstd1, d_after, vec],
        grid=(1,),
        in_specs=[first, first]
        + [pl.BlockSpec((rows, width), lambda i, s: (0, 0))] * len(sides)
        + [own(width), own(1), own(width), pl.BlockSpec(vec.shape, lambda i, s: (0, 0))],
        out_specs=pl.BlockSpec((rows, width), lambda i, s: (0, 0)),
        out_shape=jax.ShapeDtypeStruct((rows, width), f32),
        cost_estimate=SMALL,
        mib=20,
        name="finish",
    )


def ff_kernel(grid, ups, downs, place, h2_ref, dy_ref, vec_ref, *refs):
    fast = isinstance(ups, Pieces)
    n_up, n = len(ups.arrays), len(ups.arrays) + len(downs.arrays)
    pieces, refs = refs[:n], refs[n:]
    if fast:
        g_ref, refs = refs[0], refs[1:]
    else:
        (gdown_ref, gup_ref), refs = refs[:2], refs[2:]
    gbias_ref, out_ref, dh_ref, dhb_ref, act_s, dhid_s, h2t_s, up_s, down_s, sem, down_sem = refs
    step = pl.program_id(0)
    rows, width = h2_ref.shape
    units = act_s.shape[1]
    part = 256 if rows % 256 == 0 else rows

    @pl.when(step == 0)
    def _():
        if fast:
            r = up_s.shape[2]
            copies = ups.copies(
                place,
                pieces[:n_up],
                sem,
                [
                    (0, r, 0, width, lambda chip: up_s.at[0, chip]),
                    (r, r, 0, width, lambda chip: up_s.at[1, chip]),
                ],
            )
        else:
            tile = pl.ds(0, units), pl.ds(units, units)
            copies = [
                pltpu.make_async_copy(pieces[0].at[:, tile[i]], up_s.at[i, 0], sem.at[i])
                for i in range(2)
            ]
        copies.append(pltpu.make_async_copy(pieces[n_up], down_s, down_sem.at[0]))
        for c in copies:
            c.start()
        h2t_s[...] = h2_ref[...].T
        for c in copies:
            c.wait()

    w_up = up_s[step].reshape(width, units)
    d = down_s.shape[0] // 2
    w_down = down_s[pl.ds(step * d, d)]
    bias = jnp.where(step == 0, vec_ref[8:9, :], vec_ref[9:10, :])
    for at in range(0, rows, part):
        here = slice(at, at + part)
        for col in range(0, units, 256):
            cols = slice(col, col + 256)
            hidden = mm(h2_ref[here, :], w_up[:, cols]) + bias[:, cols]
            phi = 0.5 * (1.0 + lax.erf(hidden * (0.5**0.5)))
            dens = jnp.exp(-0.5 * hidden * hidden) * (1.0 / math.sqrt(2.0 * math.pi))
            act_s[here, cols] = (hidden * phi).astype(bf16)
            d_act = mm(dy_ref[here, :], w_down[cols, :], ((1,), (1,)))
            dhid_s[here, cols] = (d_act * (phi + hidden * dens)).astype(bf16)
    act, d_hidden = act_s[...], dhid_s[...]
    gdown = mm(act, dy_ref[...], ((0,), (0,))).astype(bf16)
    gup = mm(h2t_s[...], d_hidden).astype(bf16)
    gbias_ref[0] = sum_rows(d_hidden.astype(f32))
    out = mm(act, w_down)
    dh = mm(d_hidden, w_up, ((1,), (1,)))
    if fast:
        down_shard = 2 * units // grid.chips
        up_shard = width // grid.chips
        half = grid.chips // 2
        for i in range(half):
            column, z = grid.relative(place, step * half + i)
            g_ref[column, z, 0:down_shard, :] = gdown[i * down_shard : (i + 1) * down_shard]
        for i in range(grid.chips):
            column, z = grid.relative(place, i)
            to = pl.multiple_of(down_shard + step * up_shard, 16)
            g_ref[column, z, pl.ds(to, up_shard), :] = gup[i * up_shard : (i + 1) * up_shard]
    else:
        gdown_ref[...] = gdown
        gup_ref[...] = gup

    @pl.when(step == 0)
    def _():
        out_ref[...] = out
        dh_ref[...] = dh

    @pl.when(step == 1)
    def _():
        out_ref[...] += out
        total = dh_ref[...] + dh
        dh_ref[...] = total
        dhb_ref[...] = total.astype(bf16)


def feed_forward(grid, h2, dy, ups, downs, vec, units):
    fast = isinstance(ups, Pieces)
    rows, width = h2.shape
    tile = units // 2
    chips = grid.chips
    whole = pl.BlockSpec((rows, width), lambda j, s: (0, 0))
    cols = pl.BlockSpec((width, tile), lambda j, s: (0, j))
    lines = pl.BlockSpec((tile, width), lambda j, s: (j, 0))
    if fast:
        shape = (2 * grid.q, grid.z, (units + width * 2) // chips, width)
        g_specs = [pl.BlockSpec(shape, lambda j, s: (0, 0, 0, 0))]
        g_shapes = [jax.ShapeDtypeStruct(shape, bf16)]
        up_shape = (2, chips, width // chips, tile)
    else:
        g_specs = [lines, cols]
        g_shapes = [
            jax.ShapeDtypeStruct((units, width), bf16),
            jax.ShapeDtypeStruct((width, units), bf16),
        ]
        up_shape = (2, 1, width, tile)
    return call(
        functools.partial(ff_kernel, grid, ups, downs),
        grid.place,
        [h2, dy, vec] + ups.arrays + downs.arrays,
        grid=(2,),
        in_specs=[whole, whole, pl.BlockSpec(vec.shape, lambda j, s: (0, 0))]
        + [pl.BlockSpec(memory_space=pl.ANY)] * len(ups.arrays + downs.arrays),
        out_specs=g_specs
        + [pl.BlockSpec((1, 1, tile), lambda j, s: (j, 0, 0)), whole, whole, whole],
        out_shape=g_shapes
        + [
            jax.ShapeDtypeStruct((2, 1, tile), f32),
            jax.ShapeDtypeStruct((rows, width), f32),
            jax.ShapeDtypeStruct((rows, width), f32),
            jax.ShapeDtypeStruct((rows, width), bf16),
        ],
        scratch_shapes=[
            pltpu.VMEM((rows, tile), bf16),
            pltpu.VMEM((rows, tile), bf16),
            pltpu.VMEM((width, rows), bf16),
            pltpu.VMEM(up_shape, bf16),
            pltpu.VMEM((units, width), bf16),
            pltpu.SemaphoreType.DMA((2 * ups.count,)),
            pltpu.SemaphoreType.DMA((downs.count,)),
        ],
        cost_estimate=SMALL,
        mib=40,
        name="feed_forward",
    )


def in_order(first, mine, other):
    return jnp.stack([jnp.where(first, mine, other), jnp.where(first, other, mine)])


def body(
    dp,
    blk,
    inputs,
    clip_ids,
    ln1_gain,
    ln1_bias,
    w_qkv,
    qv_bias,
    w_out,
    out_bias,
    ln2_gain,
    ln2_bias,
    w_up,
    up_bias,
    w_down,
    down_bias,
    out_grad,
):
    grid = Grid(dp, blk)
    core = grid.me["c"]
    first = core == 0
    chips = grid.chips
    width = inputs.shape[2]
    half = width // 2
    local = inputs.shape[1]
    chip_rows = 2 * local
    units = w_up.shape[1] // 2
    shard = w_qkv.shape[0]
    per_chip = units // chips
    fast = shard % 8 == 0 and per_chip % 16 == 0
    swap = lambda v: grid.shift(v, "c", 1)
    at_core = lambda v, dim=0: lax.dynamic_index_in_dim(v, core, dim, keepdims=False)
    not_core = lambda v, dim=0: lax.dynamic_index_in_dim(v, 1 - core, dim, keepdims=False)

    pad = jnp.zeros((16, width), bf16).at[0, :local].set(clip_ids[0].astype(bf16))
    mine = jnp.concatenate([inputs[0], pad], axis=0)
    dy_mine = out_grad[0]
    if fast:
        put = lambda v, n: jnp.zeros((128,), bf16).at[:n].set(v)
        place_at = lambda v: jnp.where(first, jnp.pad(v, (0, v.size)), jnp.pad(v, (v.size, 0)))
        vecs = [ln1_gain, ln1_bias, out_bias, ln2_gain, ln2_bias, down_bias, qv_bias]
        rows = jnp.stack([jnp.pad(place_at(v), (0, 128 - 2 * v.size)) for v in vecs])
        up_row = put(up_bias, per_chip)[None]
        blank = jnp.zeros((8, 128), bf16)
        mine_small = jnp.concatenate([rows, up_row, blank])
        their_small = jnp.concatenate([rows, jnp.zeros_like(up_row), blank])
        widen = lambda v: jnp.pad(v, ((0, 0), (0, 3 * half - 128)))
        split = w_qkv.reshape(shard, 3, 2, half)
        my_qkv = at_core(split, 2).reshape(shard, 3 * half)
        to_qkv = not_core(split, 2).reshape(shard, 3 * half)
        up_split = w_up.reshape(shard, chips, 2, per_chip)
        out_split = w_out.reshape(shard, 2, half)
        my_up = at_core(up_split, 2).reshape(shard, units)
        to_up = not_core(up_split, 2).reshape(shard, units)
        my_out, to_out = at_core(out_split, 1), not_core(out_split, 1)
        got = swap(jnp.concatenate([to_qkv, widen(their_small)]))
        pair = in_order(first, my_qkv, got[:shard])
        small_chip = mine_small + got[shard:, :128]
        qkv_piece = jnp.concatenate([pair.reshape(2 * shard, 3 * half), widen(small_chip)])

        full_down = grid.gather_chips(w_down)
        downs = Whole([full_down])
        qkv_piece, x_sent = lock(qkv_piece, mine)
        qkv_z = grid.along(qkv_piece, "z")
        x_far = grid.along(x_sent, "q")
        x_near = swap(x_sent)
        got = swap(jnp.concatenate([to_up, to_out], axis=1))
        up_pair = in_order(first, my_up, got[:, :units]).reshape(2 * shard, units)
        up_piece = jnp.concatenate([up_pair[:, :width], up_pair[:, width:]])
        out_piece = in_order(first, my_out, got[:, units:]).reshape(2 * shard, half)
        cut = 2 * shard * 2 // 3 // 16 * 16
        low = jnp.pad(out_piece[cut:], ((0, 2 * cut - 2 * shard), (0, 0)))
        up_piece = jnp.concatenate([up_piece, jnp.concatenate([out_piece[:cut], low], axis=1)])

        qkv_z, x_far, x_near, up_piece = lock(qkv_z, x_far, x_near, up_piece)
        qkv_line = grid.line(qkv_piece, qkv_z)
        qkv_over, qkv_sides = grid.shift(qkv_line, "x", 1), grid.along(qkv_line, "q")
        up_line = grid.exchange(jnp.broadcast_to(up_piece, (grid.z,) + up_piece.shape))
        x_both = [(mine, x_near)] + [(v, swap(v)) for v in x_far]
        dy_near = swap(dy_mine)

        qkv_over, qkv_sides, x_both, dy_near = lock(qkv_over, qkv_sides, x_both, dy_near)
        found = grid.found(
            qkv_line, qkv_over, qkv_sides, grid.corner_pieces(qkv_over, qkv_sides)
        )
        qkv_weights = Pieces(grid, found)
        small_all = pick(grid, found, 2 * shard, 128)
        vec = vectors_of(grid, small_all.reshape(chips * 16, 128), width)
    else:
        whole = lambda v: lax.all_gather(v, AXES, axis=0, tiled=True)
        full_qkv = at_core(whole(w_qkv).reshape(width, 3, 2, half), 2).reshape(width, 3 * half)
        qkv_weights = Whole([full_qkv])
        full_out = whole(w_out)
        full_up = at_core(whole(w_up).reshape(width, chips, 2, per_chip), 2).reshape(width, units)
        full_down = at_core(whole(w_down).reshape(chips, 2, per_chip, width), 1).reshape(
            units, width
        )
        ups, downs = Whole([full_up]), Whole([full_down])
        up_all = at_core(whole(up_bias).reshape(chips, 2, per_chip), 1).reshape(2, width)
        singles = [ln1_gain, ln1_bias, out_bias, ln2_gain, ln2_bias, down_bias]
        vec = jnp.concatenate(
            [whole(v)[None] for v in singles]
            + [whole(qv_bias).reshape(2, width), up_all, jnp.zeros((6, width), bf16)]
        ).astype(f32)
        x_both = [(v, swap(v)) for v in [mine] + grid.along(mine, "q")]
        dy_near = swap(dy_mine)

    both = [in_order(first, *v) for v in x_both]
    token_rows = jnp.concatenate([b[:, :local].reshape(chip_rows, width) for b in both])
    clips = jnp.concatenate([b[:, local, :local].reshape(chip_rows) for b in both])
    x_all = token_rows.astype(f32)
    centered = x_all - mean_of(x_all)
    rstd1 = lax.rsqrt(mean_of(centered * centered) + NORM_EPS)
    n1 = centered * rstd1
    lane = lax.broadcasted_iota(jnp.int32, (1, 128), 1) % HEAD_DIM
    same = clips[:, None].astype(jnp.int32) == lane
    hot = same[:chip_rows].astype(bf16)
    pen = jnp.where(same | (lane >= 8), 0.0, -1e30).astype(bf16)
    dy = in_order(first, dy_mine, dy_near).reshape(chip_rows, width)

    queries, keys, values, h1t, full_qkv = project_qkv(grid, n1, vec, qkv_weights, local)
    pairs = half // 128
    forward = lambda q, a, n: attn_fwd(q, keys, values, hot, pen, a, n)
    if fast:
        queries, up_line = lock(queries, up_line)
        up_over, up_sides = grid.shift(up_line, "x", 1), grid.along(up_line, "q")
    parts = [forward(queries, 0, pairs - 1)]
    if fast:
        up_over, up_sides = behind((up_over, up_sides), parts[0])
        queries = behind(queries, up_over, up_sides)
        corners = grid.corner_pieces(up_over, up_sides)
        found = grid.found(up_line, up_over, up_sides, corners, True)
        ups = Pieces(grid, found)
        out_all = pick(grid, found, 4 * shard, width)
        low = out_all[:, : 2 * shard - cut, half:]
        out_cols = jnp.concatenate([out_all[:, :, :half], low], axis=1).reshape(width, half)
        full_out = jnp.concatenate(list(in_order(first, out_cols, swap(out_cols))), axis=1)
    parts.append(forward(queries, pairs - 1, 1))
    att_mine = [p[1] for p in parts]
    att_other = [swap(v) for v in att_mine]
    out_rows = full_out.reshape(2, half, width)
    after, h2, n2, rstd2 = project_out(grid, token_rows, att_mine, att_other, out_rows, vec)

    *g_ff, gbias, ff_out, dh, dh_b = feed_forward(grid, h2, dy, ups, downs, vec, units)
    d_after, d_branch, d_att, sums2 = out_back(grid, dh, swap(dh_b), dy, n2, rstd2, vec, out_rows)
    g_out = out_gradient(grid, fast, att_mine, att_other, d_branch)

    def back(d, i):
        att, _, lse = parts[i]
        start = i * (pairs - 1)
        return attn_bwd(queries, keys, values, hot, pen, att, d, lse, start, att.shape[1] // 128)

    by_core = lambda v: v.reshape(2, local, width)
    up_sums = gbias.reshape(2, width)
    if fast:
        ff_over, ff_sides = grid.corners(g_ff[0], (d_att, g_out))
        d_att = behind(d_att, ff_over, ff_sides)
    grads = [back(d_att, 0)]
    g_first = qkv_gradient(grid, fast, h1t, *grads[0])
    if fast:
        g_first = jnp.concatenate([g_first, g_out[:, :, None]], axis=2)
    d_att, g_first = lock(d_att, g_first)
    grads.append(back(d_att, 1))
    if fast:
        first_over, first_sides = grid.corners(g_first, grads[1])
        ff_own = grid.edges(g_ff[0], ff_over, ff_sides, grads[1])
        grads, ff_own, first_over, first_sides = lock(grads, ff_own, first_over, first_sides)
    d_mine, d_other, sums1 = input_back(grid, grads, full_qkv, n1, local)
    d_got = swap(d_other)
    if fast:
        g_last = qkv_gradient(grid, fast, h1t, *grads[1], sums1, sums2, up_sums)
        ff = grid.column(ff_own)
    else:
        g_last = qkv_gradient(grid, fast, h1t, *grads[1])
    sent = [
        (d_mine[k] + d_got[k].astype(f32)).astype(bf16) for k in range(1, grid.q)
    ]
    if fast:
        first_own = grid.edges(g_first, first_over, first_sides, g_last)
        sent, g_last, first_own = lock(sent, g_last, first_own)
    got = [grid.shift(s, "q", grid.q - k) for k, s in enumerate(sent, 1)]
    ff_out = behind(ff_out, sent)
    out_got = swap(not_core(by_core(ff_out)).astype(bf16)).astype(f32)
    result = at_core(by_core(ff_out)) + out_got + at_core(by_core(after)) + vec[5:6]
    output = result.astype(bf16)[None]
    input_grad = finish(grid, d_mine, d_got, got, n1, rstd1, d_after, vec)[None]

    if fast:
        last_over, last_sides = grid.corners(g_last)
        last_own = grid.edges(g_last, last_over, last_sides, ff)
        g_first, g_last = grid.column_near(first_own), grid.column_near(last_own)
        mine, g_last = g_last[:, 2 * shard :, :128], g_last[:, : 2 * shard]
        w_down_g = ff[:per_chip]
        up_chip = ff[per_chip:].reshape(2, 2, shard, width)
        up_other = swap(not_core(up_chip, 1).astype(bf16)).astype(f32)
        up_both = in_order(first, at_core(up_chip, 1), up_other)
        w_up_g = jnp.transpose(
            up_both.reshape(2, 2, shard, chips // 2, per_chip), (2, 1, 3, 0, 4)
        ).reshape(shard, 2 * units)

        def across(v):
            v = v.reshape(v.shape[0], 2, shard, half)
            other = swap(not_core(v, 1).astype(bf16)).astype(f32)
            return in_order(first, at_core(v, 1), other)

        g_first, g_last = across(g_first), across(g_last)
        early = pairs - 1
        w_out_g = jnp.concatenate([g_first[0, early], g_first[1, early]], axis=1)
        per_pair = jnp.concatenate([g_first[:, :early], g_last], axis=1)
        per_pair = per_pair.reshape(2, pairs, shard, 3, 128)
        w_qkv_g = jnp.transpose(per_pair, (2, 3, 0, 1, 4)).reshape(shard, 6 * half)
        mine = mine[0, :8]
        summed = mine + swap(mine.astype(bf16)).astype(f32)
        cut = lambda n: jnp.where(first, summed[:, :n], summed[:, n : 2 * n])
        six, qv_g, up_g = cut(shard)[:6], cut(2 * shard)[6], mine[7, :per_chip]
    else:
        reduce = lambda v: lax.psum_scatter(v, AXES, scatter_dimension=0, tiled=True)

        def spread(v, dim):
            v = v.astype(f32)
            zero = jnp.zeros_like(v)
            return jnp.stack([jnp.where(first, v, zero), jnp.where(first, zero, v)], axis=dim)

        gdown, gup = g_ff
        w_down_g = reduce(
            spread(gdown.reshape(chips, per_chip, width), 1).reshape(2 * units, width)
        )
        w_up_g = reduce(spread(gup.reshape(width, chips, per_chip), 2).reshape(width, 2 * units))
        w_out_g = reduce(spread(g_out.reshape(width, half), 1).reshape(width, width))
        per_pair = jnp.concatenate([g_first, g_last]).reshape(pairs, width, 3, 128)
        per_pair = jnp.transpose(per_pair, (1, 2, 0, 3)).reshape(width, 3, half)
        w_qkv_g = reduce(spread(per_pair, 2).reshape(width, 6 * half))
        nothing = jnp.zeros_like(up_sums)
        sums = jnp.concatenate(
            [
                sums1[0:2],
                sums2[0:4],
                sums1[2:4],
                jnp.where(first, up_sums, nothing),
                jnp.where(first, nothing, up_sums),
            ]
        )
        sums = lax.psum(sums, AXES)
        me = (lax.axis_index("dp") * blk) + lax.axis_index("blk")
        six = lax.dynamic_slice(sums, (0, me * shard), (6, shard))
        qv_g = lax.dynamic_slice(sums[6:8].reshape(2 * width), (me * 2 * shard,), (2 * shard,))
        up_g = at_core(sums[8:12].reshape(2, units))
        up_g = lax.dynamic_slice(up_g, (me // 2 * per_chip,), (per_chip,))

    return (
        output,
        input_grad,
        six[0],
        six[1],
        w_qkv_g,
        qv_g,
        w_out_g,
        six[2],
        six[3],
        six[4],
        w_up_g,
        up_g,
        w_down_g,
        six[5],
    )


def solution(mesh):
    both = P(("dp", "blk"))
    rows = P(("dp", "blk"), None)
    tokens = P("dp", "blk", None)
    return jax.shard_map(
        functools.partial(body, mesh.shape["dp"], mesh.shape["blk"]),
        mesh=mesh,
        in_specs=(
            tokens,
            P("dp", "blk"),
            both,
            both,
            rows,
            both,
            rows,
            both,
            both,
            both,
            rows,
            both,
            rows,
            both,
            tokens,
        ),
        out_specs=(
            tokens,
            tokens,
            both,
            both,
            rows,
            both,
            rows,
            both,
            both,
            both,
            rows,
            both,
            rows,
            both,
        ),
        check_vma=False,
    )
```

profile of v0, /device:TPU:0, one launch (start us, length us, event | category | flops | bytes accessed | tf_op | source)
XLA Modules:
  0.0 322.9 jit_solution(2045417590107518975)
XLA Ops:
  14.3 2.7 collective-permute-start.4
  17.1 1.6 collective-permute-start.1
  18.7 2.6 collective-permute-start.2
  21.3 1.3 collective-permute-start.3
  22.8 2.9 collective-permute-done.1
  25.6 5.9 %collective-permute-done.2 = bf16[64,1152]{1,0:T(8,128)(2,1)S(1)} collective-permute-done((bf16[64,1152]{1,0:T(8,128)(2,1)S(1)}, bf16[64,1152]{1,0:T(8,128)(2,1)S(1)}, u32[]{:S(2)}, u32[]{:S(2)}) %collective-permute-start.2) | collective-permute-done | bytes 147488 | tf_op jit(solution)/shard_map/ppermute | solution.py:49
  32.5 1.6 collective-permute-start.7
  34.1 1.5 collective-permute-start.8
  37.3 5.1 %all-to-all-start = ((bf16[4,128,768]{2,1,0:T(8,128)(2,1)}), bf16[4,128,768]{2,1,0:T(8,128)(2,1)}, u32[]{:S(2)}, u32[]{:S(2)}) async-start(bf16[4,128,768]{2,1,0:T(8,128)(2,1)} %broadcast_in_dim.37), calls=%async_computation | async-start | bytes 1572864 | tf_op jit(solution)/shard_map/all_to_all | solution.py:133
  42.4 6.3 %collective-permute-done.7.refs_1_ = bf16[4,64,1152]{2,1,0:T(8,128)(2,1)S(1)} collective-permute-done((bf16[4,64,1152]{2,1,0:T(8,128)(2,1)S(1)}, bf16[4,64,1152]{2,1,0:T(8,128)(2,1)S(1)}, u32[]{:S(2)}, u32[]{:S(2)}) %collective-permute-start.7) | collective-permute-done | bytes 589856 | tf_op jit(solution)/shard_map/ppermute | solution.py:49
  48.7 1.3 collective-permute-done.8.refs_2_
  50.1 1.4 collective-permute-start.11
  52.8 1.6 select_bitcast_fusion
  57.2 3.6 %fusion.n1_ref.refs_7_.refs_3_ = f32[1536,768]{1,0:T(8,128)} fusion(f32[1536]{0:T(1024)S(1)} %add_rsqrt_fusion, f32[1536]{0:T(1024)S(1)} %broadcast_multiply_fusion, bf16[768,768]{1,0:T(8,128)(2,1)S(1)} %bitcast.268, bf16[768,768]{1,0:T(8,128)(2,1)S(1)} %bitcast.264), kind=kLoop, calls=%fused_computation.2 | loop fusion | flops 7077888 | bytes 7090176 | tf_op jit(solution)/shard_map/mul | solution.py:1104
  64.6 2.3 copy-done
  71.0 8.5 %qkv.1 = (bf16[768,384]{1,0:T(8,128)(2,1)S(1)}, bf16[1536,384]{1,0:T(8,128)(2,1)S(1)}, bf16[1536,384]{1,0:T(8,128)(2,1)S(1)}, bf16[768,1536]{1,0:T(8,128)(2,1)S(1)}, bf16[16,48,1152]{2,1,0:T(8,128)(2,1)S(1)}) custom-call(s32[4]{0:T(128)S(1)} %pad_add_fusion.place, f32[1536,768]{1,0:T(8,128)S(1)} %copy-done, f32[16,768]{1,0:T(8,128)S(1)} %vectors.1.vec_ref.refs_6_, ...), custom_call_target="tpu_custom_call" | custom-call | flops 1000 | bytes 1000 | tf_op jit(solution)/shard_map/qkv/pallas_call | solution.py:163
  79.5 1.5 copy-done.7
  82.8 1.5 collective-permute-start.13
  86.3 13.1 %attn_fwd.2 = (f32[768,256]{1,0:T(8,128)S(1)}, bf16[768,256]{1,0:T(8,128)(2,1)S(1)}, f32[2,2,768]{2,1,0:T(2,128)S(1)}) custom-call(bf16[768,384]{1,0:T(8,128)(2,1)S(1)} %get-tuple-element.141.q_ref, bf16[1536,384]{1,0:T(8,128)(2,1)S(1)} %get-tuple-element.134.k_ref, bf16[1536,384]{1,0:T(8,128)(2,1)S(1)} %get-tuple-element.135.v_ref, ...), custom_call_target="tpu_custom_call" | custom-call | flops 1000 | bytes 1000 | tf_op jit(solution)/shard_map/attn_fwd/pallas_call | solution.py:320
  99.4 9.1 %collective-permute-done.13.refs_1_ = bf16[4,128,768]{2,1,0:T(8,128)(2,1)S(1)} collective-permute-done((bf16[4,128,768]{2,1,0:T(8,128)(2,1)}, bf16[4,128,768]{2,1,0:T(8,128)(2,1)S(1)}, u32[]{:S(2)}, u32[]{:S(2)}) %collective-permute-start.13) | collective-permute-done | bytes 786464 | tf_op jit(solution)/shard_map/ppermute | solution.py:49
  108.5 1.7 collective-permute-done.14.refs_2_
  113.0 5.4 %collective-permute-done.15.refs_3_ = bf16[2,128,768]{2,1,0:T(8,128)(2,1)S(1)} collective-permute-done((bf16[2,128,768]{2,1,0:T(8,128)(2,1)S(1)}, bf16[2,128,768]{2,1,0:T(8,128)(2,1)S(1)}, u32[]{:S(2)}, u32[]{:S(2)}) %collective-permute-start.15) | collective-permute-done | bytes 393248 | tf_op jit(solution)/shard_map/ppermute | solution.py:49
  123.7 6.4 %attn_fwd.3 = (f32[768,128]{1,0:T(8,128)S(1)}, bf16[768,128]{1,0:T(8,128)(2,1)S(1)}, f32[1,2,768]{2,1,0:T(2,128)S(1)}) custom-call(bf16[768,384]{1,0:T(8,128)(2,1)S(1)} %get-tuple-element.141.q_ref, bf16[1536,384]{1,0:T(8,128)(2,1)S(1)} %get-tuple-element.134.k_ref, bf16[1536,384]{1,0:T(8,128)(2,1)S(1)} %get-tuple-element.135.v_ref, ...), custom_call_target="tpu_custom_call" | custom-call | flops 1000 | bytes 1000 | tf_op jit(solution)/shard_map/attn_fwd/pallas_call | solution.py:320
  131.7 3.2 out_proj.1
  134.9 1.4 copy-done.22
  138.8 1.4 copy-done.56
  144.5 1.7 copy-done.21
  150.2 18.7 %feed_forward.1 = (bf16[4,4,192,768]{3,2,1,0:T(8,128)(2,1)}, f32[2,1,768]{2,1,0:T(1,128)S(1)}, f32[768,768]{1,0:T(8,128)S(1)}, f32[768,768]{1,0:T(8,128)S(1)}, bf16[768,768]{1,0:T(8,128)(2,1)S(1)}) custom-call(s32[4]{0:T(128)S(1)} %pad_add_fusion.place, bf16[768,768]{1,0:T(8,128)(2,1)S(1)} %copy-done.45, bf16[768,768]{1,0:T(8,128)(2,1)S(1)} %bitcast.250, ...), custom_call_target="tpu_custom_call" | custom-call | flops 1000 | bytes 1000 | tf_op jit(solution)/shard_map/feed_forward/pallas_call | solution.py:163
  169.2 2.4 slice_bitcast_fusion.1
  171.7 1.7 collective-permute-start.21
  173.8 3.1 out_back.1
  177.0 1.4 w_out_grad.1
  178.5 8.6 %collective-permute-done.21 = bf16[2,192,768]{2,1,0:T(8,128)(2,1)S(1)} collective-permute-done((bf16[2,192,768]{2,1,0:T(8,128)(2,1)S(1)}, bf16[2,192,768]{2,1,0:T(8,128)(2,1)S(1)}, u32[]{:S(2)}, u32[]{:S(2)}) %collective-permute-start.21) | collective-permute-done | bytes 589856 | tf_op jit(solution)/shard_map/ppermute | solution.py:49
  187.1 1.4 collective-permute-done.22
  190.6 14.6 %attn_bwd.2 = (bf16[768,256]{1,0:T(8,128)(2,1)S(1)}, bf16[1536,256]{1,0:T(8,128)(2,1)S(1)}, bf16[1536,256]{1,0:T(8,128)(2,1)S(1)}) custom-call(bf16[768,384]{1,0:T(8,128)(2,1)S(1)} %copy-done.6, bf16[1536,384]{1,0:T(8,128)(2,1)S(1)} %get-tuple-element.134.k_ref, bf16[1536,384]{1,0:T(8,128)(2,1)S(1)} %get-tuple-element.135.v_ref, ...), custom_call_target="tpu_custom_call" | custom-call | flops 1000 | bytes 1000 | tf_op jit(solution)/shard_map/attn_bwd/pallas_call | solution.py:416
  205.2 3.7 %w_qkv_grad.2 = bf16[4,4,2,48,384]{4,3,2,1,0:T(8,128)(2,1)S(1)} custom-call(s32[4]{0:T(128)S(1)} %pad_add_fusion.place, bf16[768,1536]{1,0:T(8,128)(2,1)S(1)} %copy-done.8, bf16[768,256]{1,0:T(8,128)(2,1)S(1)} %get-tuple-element.171.dq_ref.refs_0_, bf16[1536,256]{1,0:T(8,128)(2,1)S(1)} %get-tuple-element.172.dk_ref.refs_1_, ...), custom_call_target="tpu_custom_call" | custom-call | flops 1000 | bytes 1000 | tf_op jit(solution)/shard_map/w_qkv_grad/pallas_call | solution.py:163
  210.4 1.6 collective-permute-start.26
  212.0 6.8 %attn_bwd.3 = (bf16[768,128]{1,0:T(8,128)(2,1)S(1)}, bf16[1536,128]{1,0:T(8,128)(2,1)S(1)}, bf16[1536,128]{1,0:T(8,128)(2,1)S(1)}) custom-call(bf16[768,384]{1,0:T(8,128)(2,1)S(1)} %copy-done.6, bf16[1536,384]{1,0:T(8,128)(2,1)S(1)} %get-tuple-element.134.k_ref, bf16[1536,384]{1,0:T(8,128)(2,1)S(1)} %get-tuple-element.135.v_ref, ...), custom_call_target="tpu_custom_call" | custom-call | flops 1000 | bytes 1000 | tf_op jit(solution)/shard_map/attn_bwd/pallas_call | solution.py:416
  218.8 1.7 collective-permute-done.25
  222.8 1.5 fusion.4
  224.4 7.0 %input_back.1 = (f32[2,384,768]{2,1,0:T(8,128)S(1)}, bf16[2,384,768]{2,1,0:T(8,128)(2,1)}, f32[8,768]{1,0:T(8,128)S(1)}) custom-call(s32[4]{0:T(128)S(1)} %pad_add_fusion.place, bf16[768,256]{1,0:T(8,128)(2,1)S(1)} %get-tuple-element.171.dq_ref.refs_0_, bf16[1536,256]{1,0:T(8,128)(2,1)S(1)} %get-tuple-element.172.dk_ref.refs_1_, ...), custom_call_target="tpu_custom_call" | custom-call | flops 1000 | bytes 1000 | tf_op jit(solution)/shard_map/input_back/pallas_call | solution.py:163
  231.3 1.5 copy-done.10
  235.0 6.7 %all-to-all-start.1 = ((bf16[4,192,768]{2,1,0:T(8,128)(2,1)}), bf16[4,192,768]{2,1,0:T(8,128)(2,1)}, u32[]{:S(2)}, u32[]{:S(2)}) async-start(bf16[4,192,768]{2,1,0:T(8,128)(2,1)} %fusion.4), calls=%async_computation.1 | async-start | bytes 2359296 | tf_op jit(solution)/shard_map/all_to_all | solution.py:133
  243.7 2.6 w_qkv_grad.3
  246.3 1.4 fusion.13
  247.8 2.2 fusion.15
  250.0 5.7 %collective-permute-start.40 = (bf16[3,48,384]{2,1,0:T(8,128)(2,1)S(1)}, bf16[3,48,384]{2,1,0:T(8,128)(2,1)S(1)}, u32[]{:S(2)}, u32[]{:S(2)}) collective-permute-start(bf16[3,48,384]{2,1,0:T(8,128)(2,1)S(1)} %get-tuple-element.227), channel_id=1, source_target_pairs={{0,8},{1,9},{2,10},{3,11},{4,12},{5,13},{6,14},{7,15},{8,16},{9,17... | collective-permute-start | bytes 331784 | tf_op jit(solution)/shard_map/ppermute | solution.py:49
  256.4 1.7 collective-permute-start.34
  258.2 1.4 collective-permute-start.31
  261.4 2.4 collective-permute-start.42
  263.9 4.8 %collective-permute-done.40 = bf16[3,48,384]{2,1,0:T(8,128)(2,1)S(1)} collective-permute-done((bf16[3,48,384]{2,1,0:T(8,128)(2,1)S(1)}, bf16[3,48,384]{2,1,0:T(8,128)(2,1)S(1)}, u32[]{:S(2)}, u32[]{:S(2)}) %collective-permute-start.40) | collective-permute-done | bytes 110624 | tf_op jit(solution)/shard_map/ppermute | solution.py:49
  268.7 1.4 collective-permute-start.35
  270.1 8.4 %collective-permute-done.41 = bf16[3,48,384]{2,1,0:T(8,128)(2,1)S(1)} collective-permute-done((bf16[3,48,384]{2,1,0:T(8,128)(2,1)S(1)}, bf16[3,48,384]{2,1,0:T(8,128)(2,1)S(1)}, u32[]{:S(2)}, u32[]{:S(2)}) %collective-permute-start.41) | collective-permute-done | bytes 110624 | tf_op jit(solution)/shard_map/ppermute | solution.py:49
  278.7 1.8 collective-permute-start.33
  280.5 5.5 %collective-permute-done.33 = bf16[4,1,64,384]{3,2,0,1:T(8,128)(2,1)S(1)} collective-permute-done((bf16[4,1,64,384]{3,2,0,1:T(8,128)(2,1)S(1)}, bf16[4,1,64,384]{3,2,0,1:T(8,128)(2,1)S(1)}, u32[]{:S(2)}, u32[]{:S(2)}) %collective-permute-start.33) | collective-permute-done | bytes 196640 | tf_op jit(solution)/shard_map/ppermute | solution.py:49
  286.2 2.0 collective-permute-start.36
  288.1 3.0 collective-permute-start.37
  291.1 1.4 collective-permute-start.38
  293.1 1.6 collective-permute-done.37
  300.6 1.8 reshape.368
  302.4 1.4 convert_add_fusion.4
  304.9 2.6 fusion.17
  307.5 2.3 copy-done.1
  309.9 3.6 %finish.1 = f32[384,768]{1,0:T(8,128)} custom-call(s32[4]{0:T(128)S(1)} %pad_add_fusion.place, f32[2,384,768]{2,1,0:T(8,128)S(1)} %copy-done.12, bf16[2,384,768]{2,1,0:T(8,128)(2,1)} %collective-permute-done.27.refs_1_, bf16[384,768]{1,0:T(8,128)(2,1)} %collective-permute-done.31.refs_2_, f32[1536,768]{1,0:T(8,128)S(1)} %copy-done.1, ...), custom_call_target="tpu_custom_call" | custom-call | flops 1000 | bytes 1000 | tf_op jit(solution)/shard_map/finish/pallas_call | solution.py:163
  (392 shorter events, 68.9 us)
Async XLA Ops:
  7.3 133.7 %all-gather.2.cloned.1.call-start = ((), (), s32[]{:S(2)}) async-start(), calls=%async_computation.2 | async-start | bytes 2506752 | tf_op jit(solution)/shard_map/all_gather | solution.py:138
  10.9 10.4 %collective-permute-start.6 = (bf16[24,1920]{1,0:T(8,128)(2,1)S(1)}, bf16[24,1920]{1,0:T(8,128)(2,1)S(1)}, u32[]{:S(2)}, u32[]{:S(2)}) collective-permute-start(bf16[24,1920]{1,0:T(8,128)(2,1)S(1)} %pad_maximum_fusion.14), channel_id=1, source_target_pairs={{0,1},{1,0},{2,3},{3,2},{4,5},{5,4},{6,7},{7,6},{8,9},{9,8},{10,11... | collective-permute-start | bytes 276488 | tf_op jit(solution)/shard_map/ppermute | solution.py:49
  12.9 1.4 collective-permute-start
  13.3 19.2 %copy-start.75 = (bf16[400,768]{1,0:T(8,128)(2,1)}, bf16[400,768]{1,0:T(8,128)(2,1)S(1)}, u32[]{:S(2)}) copy-start(bf16[400,768]{1,0:T(8,128)(2,1)S(1)} %fusion.14) | copy-start | bytes 1843204
  14.3 17.3 %collective-permute-start.4 = (bf16[400,768]{1,0:T(8,128)(2,1)S(1)}, bf16[400,768]{1,0:T(8,128)(2,1)S(1)}, u32[]{:S(2)}, u32[]{:S(2)}) collective-permute-start(bf16[400,768]{1,0:T(8,128)(2,1)S(1)} %fusion.14), channel_id=1, source_target_pairs={{0,2},{1,3},{2,0},{3,1},{4,6},{5,7},{6,4},{7,5},{8,10},{9,11},{10,... | collective-permute-start | bytes 1843208 | tf_op jit(solution)/shard_map/ppermute | solution.py:49
  17.0 14.5 %collective-permute-start.5 = (bf16[400,768]{1,0:T(8,128)(2,1)S(1)}, bf16[400,768]{1,0:T(8,128)(2,1)S(1)}, u32[]{:S(2)}, u32[]{:S(2)}) collective-permute-start(bf16[400,768]{1,0:T(8,128)(2,1)S(1)} %fusion.14), channel_id=1, source_target_pairs={{0,1},{1,0},{2,3},{3,2},{4,5},{5,4},{6,7},{7,6},{8,9},{9,8},{10,11... | collective-permute-start | bytes 1843208 | tf_op jit(solution)/shard_map/ppermute | solution.py:49
  17.1 8.5 %collective-permute-start.1 = (bf16[64,1152]{1,0:T(8,128)(2,1)S(1)}, bf16[64,1152]{1,0:T(8,128)(2,1)S(1)}, u32[]{:S(2)}, u32[]{:S(2)}) collective-permute-start(bf16[64,1152]{1,0:T(8,128)(2,1)S(1)} %fusion.34), channel_id=1, source_target_pairs={{0,8},{1,9},{2,10},{3,11},{4,12},{5,13},{6,14},{7,15},{8,16},{9,17... | collective-permute-start | bytes 442376 | tf_op jit(solution)/shard_map/ppermute | solution.py:49
  18.7 12.9 %collective-permute-start.2 = (bf16[64,1152]{1,0:T(8,128)(2,1)S(1)}, bf16[64,1152]{1,0:T(8,128)(2,1)S(1)}, u32[]{:S(2)}, u32[]{:S(2)}) collective-permute-start(bf16[64,1152]{1,0:T(8,128)(2,1)S(1)} %fusion.34), channel_id=1, source_target_pairs={{0,16},{1,17},{2,18},{3,19},{4,20},{5,21},{6,22},{7,23},{8,24},{9,... | collective-permute-start | bytes 442376 | tf_op jit(solution)/shard_map/ppermute | solution.py:49
  21.3 10.3 %collective-permute-start.3 = (bf16[64,1152]{1,0:T(8,128)(2,1)S(1)}, bf16[64,1152]{1,0:T(8,128)(2,1)S(1)}, u32[]{:S(2)}, u32[]{:S(2)}) collective-permute-start(bf16[64,1152]{1,0:T(8,128)(2,1)S(1)} %fusion.34), channel_id=1, source_target_pairs={{0,24},{1,25},{2,26},{3,27},{4,28},{5,29},{6,30},{7,31},{8,0},{9,1... | collective-permute-start | bytes 442376 | tf_op jit(solution)/shard_map/ppermute | solution.py:49
  25.6 16.8 %collective-permute-start.10 = (bf16[384,768]{1,0:T(8,128)(2,1)}, bf16[384,768]{1,0:T(8,128)(2,1)}, u32[]{:S(2)}, u32[]{:S(2)}) collective-permute-start(bf16[384,768]{1,0:T(8,128)(2,1)} %bitcast.26), channel_id=1, source_target_pairs={{0,1},{1,0},{2,3},{3,2},{4,5},{5,4},{6,7},{7,6},{8,9},{9,8},{10,11... | collective-permute-start | bytes 1769480 | tf_op jit(solution)/shard_map/ppermute | solution.py:49
  31.6 18.5 %collective-permute-start.9 = (bf16[400,768]{1,0:T(8,128)(2,1)S(1)}, bf16[400,768]{1,0:T(8,128)(2,1)}, u32[]{:S(2)}, u32[]{:S(2)}) collective-permute-start(bf16[400,768]{1,0:T(8,128)(2,1)S(1)} %collective-permute-done.4), channel_id=1, source_target_pairs={{0,1},{1,0},{2,3},{3,2},{4,5},{5,4},{6,7},{7,6},{8,9},{9,8},{10,11... | collective-permute-start | bytes 1843208 | tf_op jit(solution)/shard_map/ppermute | solution.py:49
  32.5 16.2 %collective-permute-start.7 = (bf16[4,64,1152]{2,1,0:T(8,128)(2,1)S(1)}, bf16[4,64,1152]{2,1,0:T(8,128)(2,1)S(1)}, u32[]{:S(2)}, u32[]{:S(2)}) collective-permute-start(bf16[4,64,1152]{2,1,0:T(8,128)(2,1)S(1)} %pad_maximum_fusion.6.refs_0_), channel_id=1, source_target_pairs={{0,4},{1,5},{2,6},{3,7},{4,0},{5,1},{6,2},{7,3},{8,12},{9,13},{10,... | collective-permute-start | bytes 1769480 | tf_op jit(solution)/shard_map/ppermute | solution.py:49
  34.1 15.9 %collective-permute-start.8 = (bf16[4,64,1152]{2,1,0:T(8,128)(2,1)S(1)}, bf16[4,64,1152]{2,1,0:T(8,128)(2,1)S(1)}, u32[]{:S(2)}, u32[]{:S(2)}) collective-permute-start(bf16[4,64,1152]{2,1,0:T(8,128)(2,1)S(1)} %pad_maximum_fusion.6.refs_0_), channel_id=1, source_target_pairs={{0,2},{1,3},{2,0},{3,1},{4,6},{5,7},{6,4},{7,5},{8,10},{9,11},{10,... | collective-permute-start | bytes 1769480 | tf_op jit(solution)/shard_map/ppermute | solution.py:49
  37.3 45.5 %all-to-all-start = ((bf16[4,128,768]{2,1,0:T(8,128)(2,1)}), bf16[4,128,768]{2,1,0:T(8,128)(2,1)}, u32[]{:S(2)}, u32[]{:S(2)}) async-start(bf16[4,128,768]{2,1,0:T(8,128)(2,1)} %broadcast_in_dim.37), calls=%async_computation | async-start | bytes 1572864 | tf_op jit(solution)/shard_map/all_to_all | solution.py:133
  48.7 12.1 %copy-start.38 = (bf16[4,64,1152]{2,1,0:T(8,128)(2,1)}, bf16[4,64,1152]{2,1,0:T(8,128)(2,1)S(1)}, u32[]{:S(2)}) copy-start(bf16[4,64,1152]{2,1,0:T(8,128)(2,1)S(1)} %collective-permute-done.7.refs_1_) | copy-start | bytes 1769476
  50.1 10.7 %copy-start.40 = (bf16[4,64,1152]{2,1,0:T(8,128)(2,1)}, bf16[4,64,1152]{2,1,0:T(8,128)(2,1)S(1)}, u32[]{:S(2)}) copy-start(bf16[4,64,1152]{2,1,0:T(8,128)(2,1)S(1)} %collective-permute-done.8.refs_2_) | copy-start | bytes 1769476
  50.1 11.5 %collective-permute-start.11 = (bf16[2,64,1152]{2,1,0:T(8,128)(2,1)S(1)}, bf16[2,64,1152]{2,1,0:T(8,128)(2,1)S(1)}, u32[]{:S(2)}, u32[]{:S(2)}) collective-permute-start(bf16[2,64,1152]{2,1,0:T(8,128)(2,1)S(1)} %slice.362), channel_id=1, source_target_pairs={{0,2},{1,3},{2,0},{3,1},{4,6},{5,7},{6,4},{7,5},{8,10},{9,11},{10,... | collective-permute-start | bytes 884744 | tf_op jit(solution)/shard_map/ppermute | solution.py:49
  52.2 10.1 %collective-permute-start.12 = (bf16[2,64,1152]{2,1,0:T(8,128)(2,1)}, bf16[2,64,1152]{2,1,0:T(8,128)(2,1)S(1)}, u32[]{:S(2)}, u32[]{:S(2)}) collective-permute-start(bf16[2,64,1152]{2,1,0:T(8,128)(2,1)} %slice.364), channel_id=1, source_target_pairs={{0,4},{1,5},{2,6},{3,7},{4,0},{5,1},{6,2},{7,3},{8,12},{9,13},{10,... | collective-permute-start | bytes 884744 | tf_op jit(solution)/shard_map/ppermute | solution.py:49
  82.8 40.9 %copy-start.5 = (bf16[768,384]{1,0:T(8,128)(2,1)}, bf16[768,384]{1,0:T(8,128)(2,1)S(1)}, u32[]{:S(2)}) copy-start(bf16[768,384]{1,0:T(8,128)(2,1)S(1)} %get-tuple-element.141.q_ref) | copy-start | bytes 1769476
  82.8 25.8 %collective-permute-start.13 = (bf16[4,128,768]{2,1,0:T(8,128)(2,1)}, bf16[4,128,768]{2,1,0:T(8,128)(2,1)S(1)}, u32[]{:S(2)}, u32[]{:S(2)}) collective-permute-start(bf16[4,128,768]{2,1,0:T(8,128)(2,1)} %all-to-all-done.refs_0_), channel_id=1, source_target_pairs={{0,4},{1,5},{2,6},{3,7},{4,0},{5,1},{6,2},{7,3},{8,12},{9,13},{10,... | collective-permute-start | bytes 2359304 | tf_op jit(solution)/shard_map/ppermute | solution.py:49
  84.3 26.0 %collective-permute-start.14 = (bf16[4,128,768]{2,1,0:T(8,128)(2,1)}, bf16[4,128,768]{2,1,0:T(8,128)(2,1)S(1)}, u32[]{:S(2)}, u32[]{:S(2)}) collective-permute-start(bf16[4,128,768]{2,1,0:T(8,128)(2,1)} %all-to-all-done.refs_0_), channel_id=1, source_target_pairs={{0,2},{1,3},{2,0},{3,1},{4,6},{5,7},{6,4},{7,5},{8,10},{9,11},{10,... | collective-permute-start | bytes 2359304 | tf_op jit(solution)/shard_map/ppermute | solution.py:49
  85.3 38.4 %copy-start.13 = (bf16[768,128]{1,0:T(8,128)(2,1)}, bf16[768,128]{1,0:T(8,128)(2,1)S(1)}, u32[]{:S(2)}) copy-start(bf16[768,128]{1,0:T(8,128)(2,1)S(1)} %slice_convert_fusion.hot_ref) | copy-start | bytes 589828
  86.3 37.4 %copy-start.3 = (bf16[1536,128]{1,0:T(8,128)(2,1)}, bf16[1536,128]{1,0:T(8,128)(2,1)S(1)}, u32[]{:S(2)}) copy-start(bf16[1536,128]{1,0:T(8,128)(2,1)S(1)} %select_convert_fusion.pen_ref) | copy-start | bytes 1179652
  99.4 13.5 %copy-start.50 = (f32[768,256]{1,0:T(8,128)}, f32[768,256]{1,0:T(8,128)S(1)}, u32[]{:S(2)}) copy-start(f32[768,256]{1,0:T(8,128)S(1)} %get-tuple-element.136.o_ref) | copy-start | bytes 2359300
  99.4 32.3 %copy-start.34 = (bf16[768,256]{1,0:T(8,128)(2,1)}, bf16[768,256]{1,0:T(8,128)(2,1)S(1)}, u32[]{:S(2)}) copy-start(bf16[768,256]{1,0:T(8,128)(2,1)S(1)} %get-tuple-element.137.refs_0_) | copy-start | bytes 1179652
  110.3 8.1 %collective-permute-start.15 = (bf16[2,128,768]{2,1,0:T(8,128)(2,1)S(1)}, bf16[2,128,768]{2,1,0:T(8,128)(2,1)S(1)}, u32[]{:S(2)}, u32[]{:S(2)}) collective-permute-start(bf16[2,128,768]{2,1,0:T(8,128)(2,1)S(1)} %slice.372), channel_id=1, source_target_pairs={{0,2},{1,3},{2,0},{3,1},{4,6},{5,7},{6,4},{7,5},{8,10},{9,11},{10,... | collective-permute-start | bytes 1179656 | tf_op jit(solution)/shard_map/ppermute | solution.py:49
  110.7 7.8 %collective-permute-start.16 = (bf16[2,128,768]{2,1,0:T(8,128)(2,1)S(1)}, bf16[2,128,768]{2,1,0:T(8,128)(2,1)S(1)}, u32[]{:S(2)}, u32[]{:S(2)}) collective-permute-start(bf16[2,128,768]{2,1,0:T(8,128)(2,1)S(1)} %slice.374), channel_id=1, source_target_pairs={{0,4},{1,5},{2,6},{3,7},{4,0},{5,1},{6,2},{7,3},{8,12},{9,13},{10,... | collective-permute-start | bytes 1179656 | tf_op jit(solution)/shard_map/ppermute | solution.py:49
  119.5 10.8 %collective-permute-start.17 = (bf16[768,384]{1,0:T(8,128)(2,1)S(1)}, bf16[768,384]{1,0:T(8,128)(2,1)S(1)}, u32[]{:S(2)}, u32[]{:S(2)}) collective-permute-start(bf16[768,384]{1,0:T(8,128)(2,1)S(1)} %bitcast.272), channel_id=1, source_target_pairs={{0,1},{1,0},{2,3},{3,2},{4,5},{5,4},{6,7},{7,6},{8,9},{9,8},{10,11... | collective-permute-start | bytes 1769480 | tf_op jit(solution)/shard_map/ppermute | solution.py:49
  123.1 7.8 %collective-permute-start.18 = (bf16[768,256]{1,0:T(8,128)(2,1)S(1)}, bf16[768,256]{1,0:T(8,128)(2,1)S(1)}, u32[]{:S(2)}, u32[]{:S(2)}) collective-permute-start(bf16[768,256]{1,0:T(8,128)(2,1)S(1)} %get-tuple-element.137.refs_0_), channel_id=1, source_target_pairs={{0,1},{1,0},{2,3},{3,2},{4,5},{5,4},{6,7},{7,6},{8,9},{9,8},{10,11... | collective-permute-start | bytes 1179656 | tf_op jit(solution)/shard_map/ppermute | solution.py:49
  130.2 1.5 collective-permute-start.19
  169.0 4.8 %collective-permute-start.20 = (bf16[768,768]{1,0:T(8,128)(2,1)S(1)}, bf16[768,768]{1,0:T(8,128)(2,1)S(1)}, u32[]{:S(2)}, u32[]{:S(2)}) collective-permute-start(bf16[768,768]{1,0:T(8,128)(2,1)S(1)} %get-tuple-element.147), channel_id=1, source_target_pairs={{0,1},{1,0},{2,3},{3,2},{4,5},{5,4},{6,7},{7,6},{8,9},{9,8},{10,11... | collective-permute-start | bytes 3538952 | tf_op jit(solution)/shard_map/ppermute | solution.py:49
  169.2 19.2 %slice-start.2 = ((s8[4718592]{0:T(1024)(128)(4,1)}), s8[4194304]{0:T(1024)(128)(4,1)S(1)}, s32[]{:S(2)}) async-start(s8[4718592]{0:T(1024)(128)(4,1)} %bitcast.270), calls=%async_computation.5 | async-start | bytes 8388608
  171.7 15.4 %collective-permute-start.21 = (bf16[2,192,768]{2,1,0:T(8,128)(2,1)S(1)}, bf16[2,192,768]{2,1,0:T(8,128)(2,1)S(1)}, u32[]{:S(2)}, u32[]{:S(2)}) collective-permute-start(bf16[2,192,768]{2,1,0:T(8,128)(2,1)S(1)} %get-tuple-element.204), channel_id=1, source_target_pairs={{0,2},{1,3},{2,0},{3,1},{4,6},{5,7},{6,4},{7,5},{8,10},{9,11},{10,... | collective-permute-start | bytes 1769480 | tf_op jit(solution)/shard_map/ppermute | solution.py:49
  173.4 15.1 %collective-permute-start.22 = (bf16[2,192,768]{2,1,0:T(8,128)(2,1)S(1)}, bf16[2,192,768]{2,1,0:T(8,128)(2,1)S(1)}, u32[]{:S(2)}, u32[]{:S(2)}) collective-permute-start(bf16[2,192,768]{2,1,0:T(8,128)(2,1)S(1)} %get-tuple-element.202), channel_id=1, source_target_pairs={{0,4},{1,5},{2,6},{3,7},{4,0},{5,1},{6,2},{7,3},{8,12},{9,13},{10,... | collective-permute-start | bytes 1769480 | tf_op jit(solution)/shard_map/ppermute | solution.py:49
  173.8 14.6 %slice-start.3 = ((s8[4718592]{0:T(1024)(128)(4,1)}), s8[524288]{0:T(1024)(128)(4,1)S(1)}, s32[]{:S(2)}) async-start(s8[4718592]{0:T(1024)(128)(4,1)} %bitcast.270), calls=%async_computation.6 | async-start | bytes 1048576
  188.9 33.9 %collective-permute-start.24 = (bf16[4,192,768]{2,1,0:T(8,128)(2,1)S(1)}, bf16[4,192,768]{2,1,0:T(8,128)(2,1)S(1)}, u32[]{:S(2)}, u32[]{:S(2)}) collective-permute-start(bf16[4,192,768]{2,1,0:T(8,128)(2,1)S(1)} %pad_maximum_fusion.5), channel_id=1, source_target_pairs={{0,2},{1,3},{2,0},{3,1},{4,6},{5,7},{6,4},{7,5},{8,10},{9,11},{10,... | collective-permute-start | bytes 3538952 | tf_op jit(solution)/shard_map/ppermute | solution.py:49
  189.4 33.4 %collective-permute-start.23 = (bf16[4,192,768]{2,1,0:T(8,128)(2,1)S(1)}, bf16[4,192,768]{2,1,0:T(8,128)(2,1)S(1)}, u32[]{:S(2)}, u32[]{:S(2)}) collective-permute-start(bf16[4,192,768]{2,1,0:T(8,128)(2,1)S(1)} %pad_maximum_fusion.4), channel_id=1, source_target_pairs={{0,4},{1,5},{2,6},{3,7},{4,0},{5,1},{6,2},{7,3},{8,12},{9,13},{10,... | collective-permute-start | bytes 3538952 | tf_op jit(solution)/shard_map/ppermute | solution.py:49
  190.6 14.6 %copy-start.8 = (bf16[768,1536]{1,0:T(8,128)(2,1)S(1)}, bf16[768,1536]{1,0:T(8,128)(2,1)}, u32[]{:S(2)}) copy-start(bf16[768,1536]{1,0:T(8,128)(2,1)} %copy-done.7) | copy-start | bytes 7077892
  209.2 11.8 %copy-start.73 = (bf16[4,4,3,48,384]{4,3,2,1,0:T(8,128)(2,1)}, bf16[4,4,3,48,384]{4,3,2,1,0:T(8,128)(2,1)S(1)}, u32[]{:S(2)}) copy-start(bf16[4,4,3,48,384]{4,3,2,1,0:T(8,128)(2,1)S(1)} %pad_maximum_fusion.1) | copy-start | bytes 5308420
  209.2 15.1 %slice-start = ((s8[4718592]{0:T(1024)(128)(4,1)}), s8[4194304]{0:T(1024)(128)(4,1)S(1)}, s32[]{:S(2)}) async-start(s8[4718592]{0:T(1024)(128)(4,1)} %bitcast.246), calls=%async_computation.3 | async-start | bytes 8388608
  209.3 11.2 %collective-permute-start.25 = (bf16[2,3,48,384]{3,2,1,0:T(8,128)(2,1)S(1)}, bf16[2,3,48,384]{3,2,1,0:T(8,128)(2,1)S(1)}, u32[]{:S(2)}, u32[]{:S(2)}) collective-permute-start(bf16[2,3,48,384]{3,2,1,0:T(8,128)(2,1)S(1)} %get-tuple-element.210), channel_id=1, source_target_pairs={{0,2},{1,3},{2,0},{3,1},{4,6},{5,7},{6,4},{7,5},{8,10},{9,11},{10,... | collective-permute-start | bytes 663560 | tf_op jit(solution)/shard_map/ppermute | solution.py:49
  210.4 10.7 %collective-permute-start.26 = (bf16[2,3,48,384]{3,2,1,0:T(8,128)(2,1)S(1)}, bf16[2,3,48,384]{3,2,1,0:T(8,128)(2,1)S(1)}, u32[]{:S(2)}, u32[]{:S(2)}) collective-permute-start(bf16[2,3,48,384]{3,2,1,0:T(8,128)(2,1)S(1)} %get-tuple-element.208), channel_id=1, source_target_pairs={{0,4},{1,5},{2,6},{3,7},{4,0},{5,1},{6,2},{7,3},{8,12},{9,13},{10,... | collective-permute-start | bytes 663560 | tf_op jit(solution)/shard_map/ppermute | solution.py:49
  224.4 10.5 %copy-start.27 = (f32[16,768]{1,0:T(8,128)S(1)}, f32[16,768]{1,0:T(8,128)}, u32[]{:S(2)}) copy-start(f32[16,768]{1,0:T(8,128)} %copy-done.24) | copy-start | bytes 147460
  232.8 14.9 %collective-permute-start.27 = (bf16[2,384,768]{2,1,0:T(8,128)(2,1)}, bf16[2,384,768]{2,1,0:T(8,128)(2,1)}, u32[]{:S(2)}, u32[]{:S(2)}) collective-permute-start(bf16[2,384,768]{2,1,0:T(8,128)(2,1)} %get-tuple-element.179), channel_id=1, source_target_pairs={{0,1},{1,0},{2,3},{3,2},{4,5},{5,4},{6,7},{7,6},{8,9},{9,8},{10,11... | collective-permute-start | bytes 3538952 | tf_op jit(solution)/shard_map/ppermute | solution.py:49
  232.8 13.5 %collective-permute-start.28 = (bf16[4,3,48,384]{3,2,1,0:T(8,128)(2,1)}, bf16[4,3,48,384]{3,2,1,0:T(8,128)(2,1)}, u32[]{:S(2)}, u32[]{:S(2)}) collective-permute-start(bf16[4,3,48,384]{3,2,1,0:T(8,128)(2,1)} %pad_maximum_fusion.8), channel_id=1, source_target_pairs={{0,4},{1,5},{2,6},{3,7},{4,0},{5,1},{6,2},{7,3},{8,12},{9,13},{10,... | collective-permute-start | bytes 1327112 | tf_op jit(solution)/shard_map/ppermute | solution.py:49
  233.7 12.6 %collective-permute-start.29 = (bf16[4,3,48,384]{3,2,1,0:T(8,128)(2,1)}, bf16[4,3,48,384]{3,2,1,0:T(8,128)(2,1)}, u32[]{:S(2)}, u32[]{:S(2)}) collective-permute-start(bf16[4,3,48,384]{3,2,1,0:T(8,128)(2,1)} %pad_maximum_fusion.9), channel_id=1, source_target_pairs={{0,2},{1,3},{2,0},{3,1},{4,6},{5,7},{6,4},{7,5},{8,10},{9,11},{10,... | collective-permute-start | bytes 1327112 | tf_op jit(solution)/shard_map/ppermute | solution.py:49
  235.0 67.4 %all-to-all-start.1 = ((bf16[4,192,768]{2,1,0:T(8,128)(2,1)}), bf16[4,192,768]{2,1,0:T(8,128)(2,1)}, u32[]{:S(2)}, u32[]{:S(2)}) async-start(bf16[4,192,768]{2,1,0:T(8,128)(2,1)} %fusion.4), calls=%async_computation.1 | async-start | bytes 2359296 | tf_op jit(solution)/shard_map/all_to_all | solution.py:133
  247.8 11.8 %copy-start.43 = (f32[768,768]{1,0:T(8,128)S(1)}, f32[768,768]{1,0:T(8,128)}, u32[]{:S(2)}) copy-start(f32[768,768]{1,0:T(8,128)} %copy-done.42) | copy-start | bytes 7077892
  250.0 18.7 %collective-permute-start.40 = (bf16[3,48,384]{2,1,0:T(8,128)(2,1)S(1)}, bf16[3,48,384]{2,1,0:T(8,128)(2,1)S(1)}, u32[]{:S(2)}, u32[]{:S(2)}) collective-permute-start(bf16[3,48,384]{2,1,0:T(8,128)(2,1)S(1)} %get-tuple-element.227), channel_id=1, source_target_pairs={{0,8},{1,9},{2,10},{3,11},{4,12},{5,13},{6,14},{7,15},{8,16},{9,17... | collective-permute-start | bytes 331784 | tf_op jit(solution)/shard_map/ppermute | solution.py:49
  255.7 22.8 %collective-permute-start.41 = (bf16[3,48,384]{2,1,0:T(8,128)(2,1)S(1)}, bf16[3,48,384]{2,1,0:T(8,128)(2,1)S(1)}, u32[]{:S(2)}, u32[]{:S(2)}) collective-permute-start(bf16[3,48,384]{2,1,0:T(8,128)(2,1)S(1)} %get-tuple-element.229), channel_id=1, source_target_pairs={{0,16},{1,17},{2,18},{3,19},{4,20},{5,21},{6,22},{7,23},{8,24},{9,... | collective-permute-start | bytes 331784 | tf_op jit(solution)/shard_map/ppermute | solution.py:49
  255.8 5.6 %collective-permute-start.32 = (bf16[2,1,64,384]{3,2,0,1:T(8,128)(2,1)S(1)}, bf16[2,1,64,384]{3,2,0,1:T(8,128)(2,1)S(1)}, u32[]{:S(2)}, u32[]{:S(2)}) collective-permute-start(bf16[2,1,64,384]{3,2,0,1:T(8,128)(2,1)S(1)} %get-tuple-element.223), channel_id=1, source_target_pairs={{0,2},{1,3},{2,0},{3,1},{4,6},{5,7},{6,4},{7,5},{8,10},{9,11},{10,... | collective-permute-start | bytes 294920 | tf_op jit(solution)/shard_map/ppermute | solution.py:49
  256.4 7.4 %collective-permute-start.34 = (bf16[2,1,64,384]{3,2,0,1:T(8,128)(2,1)S(1)}, bf16[2,1,64,384]{3,2,0,1:T(8,128)(2,1)S(1)}, u32[]{:S(2)}, u32[]{:S(2)}) collective-permute-start(bf16[2,1,64,384]{3,2,0,1:T(8,128)(2,1)S(1)} %get-tuple-element.222), channel_id=1, source_target_pairs={{0,4},{1,5},{2,6},{3,7},{4,0},{5,1},{6,2},{7,3},{8,12},{9,13},{10,... | collective-permute-start | bytes 294920 | tf_op jit(solution)/shard_map/ppermute | solution.py:49
  258.2 49.4 %collective-permute-start.31 = (bf16[384,768]{1,0:T(8,128)(2,1)}, bf16[384,768]{1,0:T(8,128)(2,1)}, u32[]{:S(2)}, u32[]{:S(2)}) collective-permute-start(bf16[384,768]{1,0:T(8,128)(2,1)} %fusion.15), channel_id=1, source_target_pairs={{0,2},{1,3},{2,0},{3,1},{4,6},{5,7},{6,4},{7,5},{8,10},{9,11},{10,... | collective-permute-start | bytes 1769480 | tf_op jit(solution)/shard_map/ppermute | solution.py:49
  261.4 17.1 %collective-permute-start.42 = (bf16[3,48,384]{2,1,0:T(8,128)(2,1)S(1)}, bf16[3,48,384]{2,1,0:T(8,128)(2,1)S(1)}, u32[]{:S(2)}, u32[]{:S(2)}) collective-permute-start(bf16[3,48,384]{2,1,0:T(8,128)(2,1)S(1)} %get-tuple-element.228), channel_id=1, source_target_pairs={{0,24},{1,25},{2,26},{3,27},{4,28},{5,29},{6,30},{7,31},{8,0},{9,1... | collective-permute-start | bytes 331784 | tf_op jit(solution)/shard_map/ppermute | solution.py:49
  263.8 41.1 %collective-permute-start.30 = (bf16[384,768]{1,0:T(8,128)(2,1)}, bf16[384,768]{1,0:T(8,128)(2,1)}, u32[]{:S(2)}, u32[]{:S(2)}) collective-permute-start(bf16[384,768]{1,0:T(8,128)(2,1)} %fusion.16), channel_id=1, source_target_pairs={{0,1},{1,0},{2,3},{3,2},{4,5},{5,4},{6,7},{7,6},{8,9},{9,8},{10,11... | collective-permute-start | bytes 1769480 | tf_op jit(solution)/shard_map/ppermute | solution.py:49
  268.7 11.8 %collective-permute-start.35 = (bf16[4,1,64,384]{3,2,0,1:T(8,128)(2,1)S(1)}, bf16[4,1,64,384]{3,2,0,1:T(8,128)(2,1)S(1)}, u32[]{:S(2)}, u32[]{:S(2)}) collective-permute-start(bf16[4,1,64,384]{3,2,0,1:T(8,128)(2,1)S(1)} %pad_maximum_fusion.11), channel_id=1, source_target_pairs={{0,2},{1,3},{2,0},{3,1},{4,6},{5,7},{6,4},{7,5},{8,10},{9,11},{10,... | collective-permute-start | bytes 589832 | tf_op jit(solution)/shard_map/ppermute | solution.py:49
  278.6 1.9 collective-permute-start.43
  278.7 7.4 %collective-permute-start.33 = (bf16[4,1,64,384]{3,2,0,1:T(8,128)(2,1)S(1)}, bf16[4,1,64,384]{3,2,0,1:T(8,128)(2,1)S(1)}, u32[]{:S(2)}, u32[]{:S(2)}) collective-permute-start(bf16[4,1,64,384]{3,2,0,1:T(8,128)(2,1)S(1)} %pad_maximum_fusion.10), channel_id=1, source_target_pairs={{0,4},{1,5},{2,6},{3,7},{4,0},{5,1},{6,2},{7,3},{8,12},{9,13},{10,... | collective-permute-start | bytes 589832 | tf_op jit(solution)/shard_map/ppermute | solution.py:49
  286.2 6.9 %collective-permute-start.36 = (bf16[1,64,384]{2,1,0:T(8,128)(2,1)S(1)}, bf16[1,64,384]{2,1,0:T(8,128)(2,1)S(1)}, u32[]{:S(2)}, u32[]{:S(2)}) collective-permute-start(bf16[1,64,384]{2,1,0:T(8,128)(2,1)S(1)} %get-tuple-element.234), channel_id=1, source_target_pairs={{0,8},{1,9},{2,10},{3,11},{4,12},{5,13},{6,14},{7,15},{8,16},{9,17... | collective-permute-start | bytes 147464 | tf_op jit(solution)/shard_map/ppermute | solution.py:49
  288.1 6.6 %collective-permute-start.37 = (bf16[1,64,384]{2,1,0:T(8,128)(2,1)S(1)}, bf16[1,64,384]{2,1,0:T(8,128)(2,1)S(1)}, u32[]{:S(2)}, u32[]{:S(2)}) collective-permute-start(bf16[1,64,384]{2,1,0:T(8,128)(2,1)S(1)} %get-tuple-element.235), channel_id=1, source_target_pairs={{0,16},{1,17},{2,18},{3,19},{4,20},{5,21},{6,22},{7,23},{8,24},{9,... | collective-permute-start | bytes 147464 | tf_op jit(solution)/shard_map/ppermute | solution.py:49
  291.1 4.2 %collective-permute-start.38 = (bf16[1,64,384]{2,1,0:T(8,128)(2,1)S(1)}, bf16[1,64,384]{2,1,0:T(8,128)(2,1)S(1)}, u32[]{:S(2)}, u32[]{:S(2)}) collective-permute-start(bf16[1,64,384]{2,1,0:T(8,128)(2,1)S(1)} %slice_bitcast_fusion.19), channel_id=1, source_target_pairs={{0,24},{1,25},{2,26},{3,27},{4,28},{5,29},{6,30},{7,31},{8,0},{9,1... | collective-permute-start | bytes 147464 | tf_op jit(solution)/shard_map/ppermute | solution.py:49
  295.4 2.6 collective-permute-start.44
  295.5 1.3 collective-permute-start.39
  304.5 8.9 %collective-permute-start.45 = (bf16[2,24,768]{2,1,0:T(8,128)(2,1)S(1)}, bf16[2,24,768]{2,1,0:T(8,128)(2,1)S(1)}, u32[]{:S(2)}, u32[]{:S(2)}) collective-permute-start(bf16[2,24,768]{2,1,0:T(8,128)(2,1)S(1)} %fusion.40), channel_id=1, source_target_pairs={{0,1},{1,0},{2,3},{3,2},{4,5},{5,4},{6,7},{7,6},{8,9},{9,8},{10,11... | collective-permute-start | bytes 221192 | tf_op jit(solution)/shard_map/ppermute | solution.py:49
  (81 other events, 216.8 us)
Sparse Core Ops, SparseCore 0:
  35.8 76.7 all-gather.1
where the time goes:
time: 328 us; the launch traced here: 323 us
  Pallas kernels  94.9 us (29%)
  waiting for transfers between devices  68.9 us (21%)
  starting transfers between devices  61.4 us (19%)
  local copies, waits for them, and re-layouts  55.2 us (17%)
  other arithmetic  26.8 us (8%)
  between operations  15.8 us (5%)
    ppermute x46, waiting for transfers between devices, shift(): return lax.ppermute(value, AXES, pairs)  68.9 us
    pallas_call x12, Pallas kernels, call(): pl.pallas_call(kernel, grid_spec=spec, compiler_params=pltpu.CompilerPara...  53.9 us
    ppermute x46, starting transfers between devices, shift(): return lax.ppermute(value, AXES, pairs)  49.5 us
    unnamed x196, local copies, waits for them, and re-layouts  36.1 us
    pallas_call x2, Pallas kernels, attn_bwd(): pl.pallas_call(attn_bwd_kernel, grid=(pairs, rows // block), in_specs=[by...  21.4 us
    pallas_call x2, Pallas kernels, attn_fwd(): pl.pallas_call(attn_fwd_kernel, grid=(pairs, rows // block), in_specs=[pl...  19.5 us
    all_to_all x2, starting transfers between devices, exchange(): lax.all_to_all(blocks, AXES, 0, 0, axis_index_groups=self.groups(('z',)),...  11.8 us
  transfers between devices with their start and end apart: 49, of which 21 were waited for; matrix products, arithmetic and copies ran while one was open for 12% of the time, Pallas kernels for 21%

commit v1 on v0

--- a/solution.py
+++ b/solution.py
@@ -150,6 +150,10 @@
 
 def behind(value, *others):
     return lax.optimization_barrier((value, others))[0]
+
+
+def hbm(value):
+    return pltpu.with_memory_space_constraint(value, pltpu.HBM)
 
 
 def call(kernel, place, operands, **kw):
@@ -451,10 +455,11 @@
         c.wait()
 
 
-def qkv_kernel(weights, moves, place, n1_ref, vec_ref, *refs):
-    pieces, (q_ref, k_ref, v_ref, h1t_ref, w_out, w_s, sem) = refs[:-7], refs[-7:]
+def qkv_kernel(weights, moves, place, x_ref, vec_ref, *refs):
+    pieces, refs = refs[:-9], refs[-9:]
+    q_ref, k_ref, v_ref, h1t_ref, n1_ref, rstd_ref, w_out, w_s, sem = refs
     half = q_ref.shape[1]
-    width = n1_ref.shape[1]
+    width = x_ref.shape[1]
     step = pl.program_id(0)
 
     @pl.when(step == 0)
@@ -465,7 +470,13 @@
             load_all([pltpu.make_async_copy(pieces[0], w_s.at[0], sem.at[0])])
         w_out[...] = w_s[...]
 
-    h1 = (n1_ref[...] * vec_ref[0:1, :] + vec_ref[1:2, :]).astype(bf16)
+    x = x_ref[...].astype(f32)
+    centered = x - mean_of(x)
+    rstd = lax.rsqrt(mean_of(centered * centered) + NORM_EPS)
+    n1 = centered * rstd
+    n1_ref[...] = n1.astype(bf16)
+    rstd_ref[...] = rstd
+    h1 = (n1 * vec_ref[0:1, :] + vec_ref[1:2, :]).astype(bf16)
     low, high = vec_ref[6:8, :half], vec_ref[6:8, half:]
     bias = jnp.where(place[3] == 0, low, high)
     w = w_s[...].reshape(width, 3 * half)
@@ -481,8 +492,8 @@
     h1t_ref[...] = h1.T
 
 
-def project_qkv(grid, n1, vec, weights, local):
-    rows, width = n1.shape
+def project_qkv(grid, x, vec, weights, local):
+    rows, width = x.shape
     half = width // 2
     if isinstance(weights, Pieces):
         r = width // grid.chips
@@ -491,10 +502,10 @@
     else:
         moves = None
         shape = (1, width, 3 * half)
-    q, k, v, h1t, w = call(
+    *found, w = call(
         functools.partial(qkv_kernel, weights, moves),
         grid.place,
-        [n1, vec] + weights.arrays,
+        [x, vec] + [hbm(w) for w in weights.arrays],
         grid=(rows // local,),
         in_specs=[
             pl.BlockSpec((local, width), lambda i, s: (i, 0)),
@@ -506,21 +517,25 @@
             pl.BlockSpec((local, half), lambda i, s: (i, 0)),
             pl.BlockSpec((local, half), lambda i, s: (i, 0)),
             pl.BlockSpec((width, local), lambda i, s: (0, i)),
+            pl.BlockSpec((local, width), lambda i, s: (i, 0)),
+            pl.BlockSpec((local, 1), lambda i, s: (i, 0)),
             pl.BlockSpec(shape, lambda i, s: (0, 0, 0)),
         ],
         out_shape=[
             jax.ShapeDtypeStruct((2 * local, half), bf16),
             jax.ShapeDtypeStruct((rows, half), bf16),
             jax.ShapeDtypeStruct((rows, half), bf16),
-            jax.ShapeDtypeStruct((width, rows), bf16),
-            jax.ShapeDtypeStruct(shape, bf16),
+            pltpu.HBM((width, rows), bf16),
+            pltpu.HBM((rows, width), bf16),
+            pltpu.HBM((rows, 1), f32),
+            pltpu.HBM(shape, bf16),
         ],
         scratch_shapes=[pltpu.VMEM(shape, bf16), pltpu.SemaphoreType.DMA((weights.count,))],
         cost_estimate=SMALL,
         mib=20,
         name="qkv",
     )
-    return q, k, v, h1t, w.reshape(width, 3 * half)
+    return found + [w.reshape(width, 3 * half)]
 
 
 def mean_of(v):
@@ -539,7 +554,7 @@
     centered = after - mean_of(after)
     rstd = lax.rsqrt(mean_of(centered * centered) + NORM_EPS)
     n2 = centered * rstd
-    n2_ref[...] = n2
+    n2_ref[...] = n2.astype(bf16)
     rstd_ref[...] = jnp.broadcast_to(rstd, rstd_ref.shape)
     h2_ref[...] = (n2 * vec_ref[3:4, :] + vec_ref[4:5, :]).astype(bf16)
 
@@ -561,10 +576,10 @@
         + [line(v.shape[1]) for v in mine + other],
         out_specs=[line(width), line(width), line(width), line(128)],
         out_shape=[
-            jax.ShapeDtypeStruct((rows, width), f32),
-            jax.ShapeDtypeStruct((rows, width), bf16),
-            jax.ShapeDtypeStruct((rows, width), f32),
-            jax.ShapeDtypeStruct((rows, 128), f32),
+            pltpu.HBM((rows, width), f32),
+            pltpu.HBM((rows, width), bf16),
+            pltpu.HBM((rows, width), bf16),
+            pltpu.HBM((rows, 128), f32),
         ],
         cost_estimate=SMALL,
         mib=16,
@@ -586,7 +601,7 @@
 ):
     d_h2 = mine_ref[...] + got_ref[...].astype(f32)
     dy = dy_ref[...].astype(f32)
-    n2 = n2_ref[...]
+    n2 = n2_ref[...].astype(f32)
     d_after = dy + norm_back(d_h2, n2, rstd_ref[:, 0:1], vec_ref[3:4, :])
     after_ref[...] = d_after
     branch = d_after.astype(bf16)
@@ -609,7 +624,7 @@
     return call(
         out_back_kernel,
         grid.place,
-        [mine, got, dy, n2, rstd, vec, w],
+        [mine, got, hbm(dy), hbm(n2), hbm(rstd), vec, hbm(w)],
         grid=(rows // block,),
         in_specs=[
             line(width),
@@ -627,7 +642,7 @@
             pl.BlockSpec((8, width), lambda i, s: (0, 0)),
         ],
         out_shape=[
-            jax.ShapeDtypeStruct((rows, width), f32),
+            pltpu.HBM((rows, width), f32),
             jax.ShapeDtypeStruct((rows, width), bf16),
             jax.ShapeDtypeStruct((rows, width // 2), bf16),
             jax.ShapeDtypeStruct((8, width), f32),
@@ -638,41 +653,10 @@
     )
 
 
-def store_rows(grid, place, ref, value, first, shard, to, tail=()):
-    for i in range(value.shape[0] // shard):
-        column, z = grid.relative(place, first + i, True)
-        at = (column, z) + tail + (pl.ds(to, shard),) + (slice(None),)
-        ref[at] = value[i * shard : (i + 1) * shard]
-
-
-def out_grad_kernel(grid, fast, n, place, d_ref, *refs):
-    g_ref = refs[-1]
-    parts = halves(place, join(refs[:n]), join(refs[n : 2 * n]))
-    for i, part in enumerate(parts):
-        g = mm(part, d_ref[...], ((0,), (0,))).astype(bf16)
-        if fast:
-            shard = 2 * g.shape[0] // grid.chips
-            store_rows(grid, place, g_ref, g, i * g.shape[0] // shard, shard, 0)
-        else:
-            g_ref[i] = g
-
-
-def out_gradient(grid, fast, mine, other, branch):
-    rows, half = branch.shape[0], branch.shape[1] // 2
-    shape = (2 * grid.q, grid.z, 2 * half // grid.chips, half) if fast else (2, half, half)
-    return call(
-        functools.partial(out_grad_kernel, grid, fast, len(mine)),
-        grid.place,
-        [branch] + mine + other,
-        grid=(1,),
-        in_specs=[pl.BlockSpec((rows, half), lambda i, s: (0, s[3]))]
-        + [pl.BlockSpec(v.shape, lambda i, s: (0, 0)) for v in mine + other],
-        out_specs=pl.BlockSpec(shape, lambda i, s: (0,) * len(shape)),
-        out_shape=jax.ShapeDtypeStruct(shape, bf16),
-        cost_estimate=SMALL,
-        mib=8,
-        name="w_out_grad",
-    )
+def store_rows(grid, place, ref, value, shard, slot):
+    for i in range(grid.chips):
+        column, z = grid.relative(place, i, True)
+        ref[column, z, slot, 0:shard, :] = value[i * shard : (i + 1) * shard]
 
 
 def vector_rows(chips, sums1, sums2, ups):
@@ -697,48 +681,59 @@
     return jnp.where(row < 6, a, b).astype(bf16)
 
 
-def qkv_grad_kernel(grid, fast, pairs, more, place, h1t_ref, dq_ref, dk_ref, dv_ref, *refs):
+def matrix_grads_kernel(grid, fast, n, place, h1t_ref, d_ref, *refs):
     g_ref = refs[-1]
-    chip_rows = dq_ref.shape[0]
-    if more:
-        rows = vector_rows(grid.chips, *(r[...] for r in refs[:-1]))
-        shard = h1t_ref.shape[0] // grid.chips
+    mine, other, flat, more = refs[:n], refs[n : 2 * n], refs[2 * n : 5 * n], refs[5 * n : -1]
+    shard = h1t_ref.shape[0] // grid.chips
+    slot = 0
+    for part in range(n):
+        dq_ref, dk_ref, dv_ref = flat[3 * part : 3 * part + 3]
+        chip_rows = dq_ref.shape[0]
+        for p in range(dq_ref.shape[1] // 128):
+            cols = slice(p * 128, (p + 1) * 128)
+            gq = mm(h1t_ref[:, :chip_rows], dq_ref[:, cols])
+            gkv = mm(h1t_ref[...], jnp.concatenate([dk_ref[:, cols], dv_ref[:, cols]], axis=1))
+            g = jnp.concatenate([gq, gkv], axis=1).astype(bf16)
+            if fast:
+                store_rows(grid, place, g_ref, g, shard, slot)
+            else:
+                g_ref[slot] = g
+            slot += 1
+    a, b = halves(place, join(mine), join(other))
+    g = mm(jnp.concatenate([a, b], axis=1), d_ref[...], ((0,), (0,))).astype(bf16)
+    if fast:
+        store_rows(grid, place, g_ref, g, shard, slot)
+        rows = vector_rows(grid.chips, *(r[...] for r in more))
         rows = jnp.concatenate([rows, jnp.zeros_like(rows)], axis=1)
         for i in range(grid.chips):
             column, z = grid.relative(place, i, True)
             g_ref[column, z, 0, pl.ds(shard, 16), 0:128] = rows[i]
-            g_ref[column, z, 0, pl.ds(shard, 16), 128:384] = jnp.zeros((16, 256), bf16)
-    for p in range(pairs):
-        cols = slice(p * 128, (p + 1) * 128)
-        gq = mm(h1t_ref[:, :chip_rows], dq_ref[:, cols])
-        gk = mm(h1t_ref[...], dk_ref[:, cols])
-        gv = mm(h1t_ref[...], dv_ref[:, cols])
-        g = jnp.concatenate([gq, gk, gv], axis=1).astype(bf16)
-        if fast:
-            store_rows(grid, place, g_ref, g, 0, g.shape[0] // grid.chips, 0, (p,))
-        else:
-            g_ref[p] = g
-
-
-def qkv_gradient(grid, fast, h1t, dq, dk, dv, *more):
-    width, rows = h1t.shape
-    pairs = dq.shape[1] // 128
+    else:
+        g_ref[slot] = g
+
+
+def matrix_gradients(grid, fast, h1t, branch, mine, other, grads, more):
+    width = h1t.shape[0]
+    rows, half = branch.shape[0], branch.shape[1] // 2
+    slots = half // 128 + 1
     if fast:
-        shape = (2 * grid.q, grid.z, pairs, width // grid.chips + (16 if more else 0), 384)
+        shape = (2 * grid.q, grid.z, slots, width // grid.chips + 16, half)
     else:
-        shape = (pairs, width, 384)
+        shape = (slots, width, half)
+    flat = [v for part in grads for v in part]
     whole = lambda v: pl.BlockSpec(v.shape, lambda i, s: (0, 0))
     return call(
-        functools.partial(qkv_grad_kernel, grid, fast, pairs, len(more)),
+        functools.partial(matrix_grads_kernel, grid, fast, len(mine)),
         grid.place,
-        [h1t, dq, dk, dv] + list(more),
+        [hbm(h1t), branch] + mine + other + flat + more,
         grid=(1,),
-        in_specs=[whole(v) for v in (h1t, dq, dk, dv) + more],
+        in_specs=[whole(h1t), pl.BlockSpec((rows, half), lambda i, s: (0, s[3]))]
+        + [whole(v) for v in mine + other + flat + more],
         out_specs=pl.BlockSpec(shape, lambda i, s: (0,) * len(shape)),
-        out_shape=jax.ShapeDtypeStruct(shape, bf16),
+        out_shape=pltpu.HBM(shape, bf16),
         cost_estimate=SMALL,
-        mib=16,
-        name="w_qkv_grad",
+        mib=30,
+        name="matrix_grads",
     )
 
 
@@ -769,7 +764,7 @@
         first = place[3] == 0
         return jnp.concatenate([jnp.where(first, v, none), jnp.where(first, none, v)], axis=1)
 
-    rows = [sum_rows(d * n1_ref[...]), sum_rows(d), spread(dq), spread(dv)]
+    rows = [sum_rows(d * n1_ref[...].astype(f32)), sum_rows(d), spread(dq), spread(dv)]
     sums = jnp.concatenate(rows + [jnp.zeros((4, width), f32)], axis=0)
 
     @pl.when(step == 0)
@@ -791,7 +786,7 @@
     return call(
         functools.partial(input_back_kernel, len(grads)),
         grid.place,
-        flat + [w, n1],
+        flat + [hbm(w), hbm(n1)],
         grid=(rows // local,),
         in_specs=specs
         + [
@@ -804,7 +799,7 @@
             pl.BlockSpec((8, width), lambda i, s: (0, 0)),
         ],
         out_shape=[
-            jax.ShapeDtypeStruct(shape, f32),
+            pltpu.HBM(shape, f32),
             jax.ShapeDtypeStruct(shape, bf16),
             jax.ShapeDtypeStruct((8, width), f32),
         ],
@@ -821,7 +816,9 @@
     d = mine_ref[0] + got_ref[0].astype(f32)
     for s in sides:
         d = d + s[...].astype(f32)
-    out_ref[...] = after_ref[...] + norm_back(d, n1_ref[...], rstd_ref[...], vec_ref[0:1, :])
+    out_ref[...] = after_ref[...] + norm_back(
+        d, n1_ref[...].astype(f32), rstd_ref[...], vec_ref[0:1, :]
+    )
 
 
 def finish(grid, mine, got, sides, n1, rstd1, d_after, vec):
@@ -831,7 +828,7 @@
     return call(
         functools.partial(finish_kernel, len(sides)),
         grid.place,
-        [mine, got] + sides + [n1, rstd1, d_after, vec],
+        [hbm(mine), got] + sides + [hbm(n1), rstd1, hbm(d_after), vec],
         grid=(1,),
         in_specs=[first, first]
         + [pl.BlockSpec((rows, width), lambda i, s: (0, 0))] * len(sides)
@@ -877,7 +874,7 @@
                 pltpu.make_async_copy(pieces[0].at[:, tile[i]], up_s.at[i, 0], sem.at[i])
                 for i in range(2)
             ]
-        copies.append(pltpu.make_async_copy(pieces[n_up], down_s, down_sem.at[0]))
+        copies.append(pltpu.make_async_copy(pieces[n_up].at[:, place[3], pl.ds(0, down_s.shape[1])], down_s, down_sem.at[0]))
         for c in copies:
             c.start()
         h2t_s[...] = h2_ref[...].T
@@ -886,7 +883,7 @@
 
     w_up = up_s[step].reshape(width, units)
     d = down_s.shape[0] // 2
-    w_down = down_s[pl.ds(step * d, d)]
+    w_down = down_s[pl.ds(step * d, d)].reshape(units, width)
     bias = jnp.where(step == 0, vec_ref[8:9, :], vec_ref[9:10, :])
     for at in range(0, rows, part):
         here = slice(at, at + part)
@@ -943,7 +940,7 @@
     if fast:
         shape = (2 * grid.q, grid.z, (units + width * 2) // chips, width)
         g_specs = [pl.BlockSpec(shape, lambda j, s: (0, 0, 0, 0))]
-        g_shapes = [jax.ShapeDtypeStruct(shape, bf16)]
+        g_shapes = [pltpu.HBM(shape, bf16)]
         up_shape = (2, chips, width // chips, tile)
     else:
         g_specs = [lines, cols]
@@ -955,7 +952,7 @@
     return call(
         functools.partial(ff_kernel, grid, ups, downs),
         grid.place,
-        [h2, dy, vec] + ups.arrays + downs.arrays,
+        [hbm(h2), hbm(dy), vec] + [hbm(w) for w in ups.arrays + downs.arrays],
         grid=(2,),
         in_specs=[whole, whole, pl.BlockSpec(vec.shape, lambda j, s: (0, 0))]
         + [pl.BlockSpec(memory_space=pl.ANY)] * len(ups.arrays + downs.arrays),
@@ -964,7 +961,7 @@
         out_shape=g_shapes
         + [
             jax.ShapeDtypeStruct((2, 1, tile), f32),
-            jax.ShapeDtypeStruct((rows, width), f32),
+            pltpu.HBM((rows, width), f32),
             jax.ShapeDtypeStruct((rows, width), f32),
             jax.ShapeDtypeStruct((rows, width), bf16),
         ],
@@ -973,13 +970,89 @@
             pltpu.VMEM((rows, tile), bf16),
             pltpu.VMEM((width, rows), bf16),
             pltpu.VMEM(up_shape, bf16),
-            pltpu.VMEM((units, width), bf16),
+            pltpu.VMEM((chips, units // chips, width), bf16),
             pltpu.SemaphoreType.DMA((2 * ups.count,)),
             pltpu.SemaphoreType.DMA((downs.count,)),
         ],
         cost_estimate=SMALL,
         mib=40,
         name="feed_forward",
+    )
+
+
+def mine_and_other(place, mine_ref, other_ref, slot, first, shard):
+    at = pl.ds(pl.multiple_of(first + shard * place[3], 8), shard)
+    return halves(place, mine_ref[slot, at, :], other_ref[slot, at, :].astype(f32))
+
+
+def last_ff_kernel(grid, shard, place, ff_ref, other_ref, up_ref, down_ref):
+    width = ff_ref.shape[1]
+    per_chip = down_ref.shape[0]
+    down_ref[...] = ff_ref[:per_chip, :]
+    half = grid.chips // 2
+    for h in range(2):
+        first = 2 * shard * h
+        at = lambda n: pl.ds(pl.multiple_of(n + first + shard * place[3], 8), shard)
+        a, b = halves(place, ff_ref[at(per_chip), :], other_ref[at(0), :].astype(f32))
+        for i in range(half):
+            to = (h * half + i) * 2 * per_chip
+            cols = slice(i * per_chip, (i + 1) * per_chip)
+            up_ref[:, to : to + 2 * per_chip] = jnp.concatenate([a[:, cols], b[:, cols]], axis=1)
+
+
+def last_ff(grid, ff, other, shard):
+    rows, width = ff.shape
+    whole = lambda shape: pl.BlockSpec(shape, lambda i, s: (0, 0))
+    up, down = (shard, 4 * width * 2 // 2), (rows - 4 * shard, width)
+    return call(
+        functools.partial(last_ff_kernel, grid, shard),
+        grid.place,
+        [ff, other],
+        grid=(1,),
+        in_specs=[whole(ff.shape), whole(other.shape)],
+        out_specs=[whole(up), whole(down)],
+        out_shape=[jax.ShapeDtypeStruct(up, f32), jax.ShapeDtypeStruct(down, f32)],
+        cost_estimate=SMALL,
+        mib=8,
+        name="last_ff",
+    )
+
+
+def last_rest_kernel(shard, place, own_ref, other_ref, qkv_ref, out_ref, six_ref, qv_ref, up_ref):
+    pairs, half = own_ref.shape[0] - 1, own_ref.shape[2]
+    for p in range(pairs + 1):
+        both = mine_and_other(place, own_ref, other_ref, p, 0, shard)
+        for core, value in enumerate(both):
+            if p == pairs:
+                out_ref[:, core * half : (core + 1) * half] = value
+                continue
+            for t in range(3):
+                to = 2 * half * t + half * core + 128 * p
+                qkv_ref[:, to : to + 128] = value[:, 128 * t : 128 * (t + 1)]
+    mine = own_ref[0, 2 * shard : 2 * shard + 8, 0:128]
+    total = mine + other_ref[0, 2 * shard : 2 * shard + 8, 0:128].astype(f32)
+    first = place[3] == 0
+    six_ref[...] = jnp.where(first, total[:, :shard], total[:, shard : 2 * shard])
+    n = 2 * shard
+    qv_ref[...] = jnp.where(first, total[6:7, :n], total[6:7, n : 2 * n])
+    up_ref[...] = mine[7:8, : up_ref.shape[1]]
+
+
+def last_rest(grid, own, other, shard, per_chip):
+    half = own.shape[2]
+    whole = lambda shape: pl.BlockSpec(shape, lambda i, s: (0,) * len(shape))
+    shapes = [(shard, 6 * half), (shard, 2 * half), (8, shard), (1, 2 * shard), (1, per_chip)]
+    return call(
+        functools.partial(last_rest_kernel, shard),
+        grid.place,
+        [own, other],
+        grid=(1,),
+        in_specs=[whole(own.shape), whole(other.shape)],
+        out_specs=[whole(s) for s in shapes],
+        out_shape=[jax.ShapeDtypeStruct(s, f32) for s in shapes],
+        cost_estimate=SMALL,
+        mib=8,
+        name="last_rest",
     )
 
 
@@ -1039,28 +1112,22 @@
         my_qkv = at_core(split, 2).reshape(shard, 3 * half)
         to_qkv = not_core(split, 2).reshape(shard, 3 * half)
         up_split = w_up.reshape(shard, chips, 2, per_chip)
-        out_split = w_out.reshape(shard, 2, half)
         my_up = at_core(up_split, 2).reshape(shard, units)
         to_up = not_core(up_split, 2).reshape(shard, units)
-        my_out, to_out = at_core(out_split, 1), not_core(out_split, 1)
         got = swap(jnp.concatenate([to_qkv, widen(their_small)]))
         pair = in_order(first, my_qkv, got[:shard])
         small_chip = mine_small + got[shard:, :128]
         qkv_piece = jnp.concatenate([pair.reshape(2 * shard, 3 * half), widen(small_chip)])
 
-        full_down = grid.gather_chips(w_down)
-        downs = Whole([full_down])
+        lines = lax.all_gather(jnp.concatenate([w_down, w_out]), AXES, axis=0, tiled=False)
+        full_out = lines[:, per_chip:].reshape(width, width)
+        downs = Whole([lines.reshape(chips, 2, per_chip + shard, width)])
         qkv_piece, x_sent = lock(qkv_piece, mine)
         qkv_z = grid.along(qkv_piece, "z")
         x_far = grid.along(x_sent, "q")
         x_near = swap(x_sent)
-        got = swap(jnp.concatenate([to_up, to_out], axis=1))
-        up_pair = in_order(first, my_up, got[:, :units]).reshape(2 * shard, units)
+        up_pair = in_order(first, my_up, swap(to_up)).reshape(2 * shard, units)
         up_piece = jnp.concatenate([up_pair[:, :width], up_pair[:, width:]])
-        out_piece = in_order(first, my_out, got[:, units:]).reshape(2 * shard, half)
-        cut = 2 * shard * 2 // 3 // 16 * 16
-        low = jnp.pad(out_piece[cut:], ((0, 2 * cut - 2 * shard), (0, 0)))
-        up_piece = jnp.concatenate([up_piece, jnp.concatenate([out_piece[:cut], low], axis=1)])
 
         qkv_z, x_far, x_near, up_piece = lock(qkv_z, x_far, x_near, up_piece)
         qkv_line = grid.line(qkv_piece, qkv_z)
@@ -1082,9 +1149,7 @@
         qkv_weights = Whole([full_qkv])
         full_out = whole(w_out)
         full_up = at_core(whole(w_up).reshape(width, chips, 2, per_chip), 2).reshape(width, units)
-        full_down = at_core(whole(w_down).reshape(chips, 2, per_chip, width), 1).reshape(
-            units, width
-        )
+        full_down = whole(w_down).reshape(chips, 2, per_chip, width)
         ups, downs = Whole([full_up]), Whole([full_down])
         up_all = at_core(whole(up_bias).reshape(chips, 2, per_chip), 1).reshape(2, width)
         singles = [ln1_gain, ln1_bias, out_bias, ln2_gain, ln2_bias, down_bias]
@@ -1098,76 +1163,61 @@
     both = [in_order(first, *v) for v in x_both]
     token_rows = jnp.concatenate([b[:, :local].reshape(chip_rows, width) for b in both])
     clips = jnp.concatenate([b[:, local, :local].reshape(chip_rows) for b in both])
-    x_all = token_rows.astype(f32)
-    centered = x_all - mean_of(x_all)
-    rstd1 = lax.rsqrt(mean_of(centered * centered) + NORM_EPS)
-    n1 = centered * rstd1
     lane = lax.broadcasted_iota(jnp.int32, (1, 128), 1) % HEAD_DIM
     same = clips[:, None].astype(jnp.int32) == lane
     hot = same[:chip_rows].astype(bf16)
     pen = jnp.where(same | (lane >= 8), 0.0, -1e30).astype(bf16)
     dy = in_order(first, dy_mine, dy_near).reshape(chip_rows, width)
 
-    queries, keys, values, h1t, full_qkv = project_qkv(grid, n1, vec, qkv_weights, local)
+    queries, keys, values, h1t, n1, rstd1, full_qkv = project_qkv(
+        grid, token_rows, vec, qkv_weights, local
+    )
     pairs = half // 128
     forward = lambda q, a, n: attn_fwd(q, keys, values, hot, pen, a, n)
     if fast:
-        queries, up_line = lock(queries, up_line)
+        up_line = behind(up_line, [f[0] for f in found])
         up_over, up_sides = grid.shift(up_line, "x", 1), grid.along(up_line, "q")
-    parts = [forward(queries, 0, pairs - 1)]
+    parts = [forward(queries, 0, 1)]
     if fast:
         up_over, up_sides = behind((up_over, up_sides), parts[0])
         queries = behind(queries, up_over, up_sides)
         corners = grid.corner_pieces(up_over, up_sides)
         found = grid.found(up_line, up_over, up_sides, corners, True)
         ups = Pieces(grid, found)
-        out_all = pick(grid, found, 4 * shard, width)
-        low = out_all[:, : 2 * shard - cut, half:]
-        out_cols = jnp.concatenate([out_all[:, :, :half], low], axis=1).reshape(width, half)
-        full_out = jnp.concatenate(list(in_order(first, out_cols, swap(out_cols))), axis=1)
-    parts.append(forward(queries, pairs - 1, 1))
+    parts.append(forward(queries, 1, pairs - 1))
     att_mine = [p[1] for p in parts]
+    if fast:
+        att_mine[1] = behind(att_mine[1], corners)
     att_other = [swap(v) for v in att_mine]
     out_rows = full_out.reshape(2, half, width)
     after, h2, n2, rstd2 = project_out(grid, token_rows, att_mine, att_other, out_rows, vec)
 
     *g_ff, gbias, ff_out, dh, dh_b = feed_forward(grid, h2, dy, ups, downs, vec, units)
     d_after, d_branch, d_att, sums2 = out_back(grid, dh, swap(dh_b), dy, n2, rstd2, vec, out_rows)
-    g_out = out_gradient(grid, fast, att_mine, att_other, d_branch)
 
     def back(d, i):
         att, _, lse = parts[i]
-        start = i * (pairs - 1)
+        start = i
         return attn_bwd(queries, keys, values, hot, pen, att, d, lse, start, att.shape[1] // 128)
 
     by_core = lambda v: v.reshape(2, local, width)
     up_sums = gbias.reshape(2, width)
+    grads = [back(d_att, 0)]
     if fast:
-        ff_over, ff_sides = grid.corners(g_ff[0], (d_att, g_out))
+        ff_over, ff_sides = grid.corners(g_ff[0], grads[0])
         d_att = behind(d_att, ff_over, ff_sides)
-    grads = [back(d_att, 0)]
-    g_first = qkv_gradient(grid, fast, h1t, *grads[0])
+    grads.append(back(d_att, 1))
+    d_mine, d_other, sums1 = input_back(grid, grads, full_qkv, n1, local)
+    more = [sums1, sums2, up_sums] if fast else []
+    g_all = matrix_gradients(grid, fast, h1t, d_branch, att_mine, att_other, grads, more)
     if fast:
-        g_first = jnp.concatenate([g_first, g_out[:, :, None]], axis=2)
-    d_att, g_first = lock(d_att, g_first)
-    grads.append(back(d_att, 1))
-    if fast:
-        first_over, first_sides = grid.corners(g_first, grads[1])
-        ff_own = grid.edges(g_ff[0], ff_over, ff_sides, grads[1])
-        grads, ff_own, first_over, first_sides = lock(grads, ff_own, first_over, first_sides)
-    d_mine, d_other, sums1 = input_back(grid, grads, full_qkv, n1, local)
+        ff_own = grid.edges(g_ff[0], ff_over, ff_sides, g_all)
+        g_all, ff_own, d_other = lock(g_all, ff_own, d_other)
+        ff = grid.column(ff_own)
     d_got = swap(d_other)
-    if fast:
-        g_last = qkv_gradient(grid, fast, h1t, *grads[1], sums1, sums2, up_sums)
-        ff = grid.column(ff_own)
-    else:
-        g_last = qkv_gradient(grid, fast, h1t, *grads[1])
     sent = [
         (d_mine[k] + d_got[k].astype(f32)).astype(bf16) for k in range(1, grid.q)
     ]
-    if fast:
-        first_own = grid.edges(g_first, first_over, first_sides, g_last)
-        sent, g_last, first_own = lock(sent, g_last, first_own)
     got = [grid.shift(s, "q", grid.q - k) for k, s in enumerate(sent, 1)]
     ff_out = behind(ff_out, sent)
     out_got = swap(not_core(by_core(ff_out)).astype(bf16)).astype(f32)
@@ -1176,33 +1226,14 @@
     input_grad = finish(grid, d_mine, d_got, got, n1, rstd1, d_after, vec)[None]
 
     if fast:
-        last_over, last_sides = grid.corners(g_last)
-        last_own = grid.edges(g_last, last_over, last_sides, ff)
-        g_first, g_last = grid.column_near(first_own), grid.column_near(last_own)
-        mine, g_last = g_last[:, 2 * shard :, :128], g_last[:, : 2 * shard]
-        w_down_g = ff[:per_chip]
-        up_chip = ff[per_chip:].reshape(2, 2, shard, width)
-        up_other = swap(not_core(up_chip, 1).astype(bf16)).astype(f32)
-        up_both = in_order(first, at_core(up_chip, 1), up_other)
-        w_up_g = jnp.transpose(
-            up_both.reshape(2, 2, shard, chips // 2, per_chip), (2, 1, 3, 0, 4)
-        ).reshape(shard, 2 * units)
-
-        def across(v):
-            v = v.reshape(v.shape[0], 2, shard, half)
-            other = swap(not_core(v, 1).astype(bf16)).astype(f32)
-            return in_order(first, at_core(v, 1), other)
-
-        g_first, g_last = across(g_first), across(g_last)
-        early = pairs - 1
-        w_out_g = jnp.concatenate([g_first[0, early], g_first[1, early]], axis=1)
-        per_pair = jnp.concatenate([g_first[:, :early], g_last], axis=1)
-        per_pair = per_pair.reshape(2, pairs, shard, 3, 128)
-        w_qkv_g = jnp.transpose(per_pair, (2, 3, 0, 1, 4)).reshape(shard, 6 * half)
-        mine = mine[0, :8]
-        summed = mine + swap(mine.astype(bf16)).astype(f32)
-        cut = lambda n: jnp.where(first, summed[:, :n], summed[:, n : 2 * n])
-        six, qv_g, up_g = cut(shard)[:6], cut(2 * shard)[6], mine[7, :per_chip]
+        over, sides = grid.corners(g_all, got)
+        own = grid.column_near(grid.edges(g_all, over, sides))
+        ff = behind(ff, sides)
+        w_up_g, w_down_g = last_ff(grid, ff, swap(ff[per_chip:].astype(bf16)), shard)
+        w_qkv_g, w_out_g, six, qv_g, up_g = last_rest(
+            grid, own, swap(own.astype(bf16)), shard, per_chip
+        )
+        qv_g, up_g = qv_g[0], up_g[0]
     else:
         reduce = lambda v: lax.psum_scatter(v, AXES, scatter_dimension=0, tiled=True)
 
@@ -1216,8 +1247,8 @@
             spread(gdown.reshape(chips, per_chip, width), 1).reshape(2 * units, width)
         )
         w_up_g = reduce(spread(gup.reshape(width, chips, per_chip), 2).reshape(width, 2 * units))
-        w_out_g = reduce(spread(g_out.reshape(width, half), 1).reshape(width, width))
-        per_pair = jnp.concatenate([g_first, g_last]).reshape(pairs, width, 3, 128)
+        w_out_g = reduce(spread(g_all[pairs], 1).reshape(width, width))
+        per_pair = g_all[:pairs].reshape(pairs, width, 3, 128)
         per_pair = jnp.transpose(per_pair, (1, 2, 0, 3)).reshape(width, 3, half)
         w_qkv_g = reduce(spread(per_pair, 2).reshape(width, 6 * half))
         nothing = jnp.zeros_like(up_sums)

time: 328 us -> 281 us (0.86)
  local copies, waits for them, and re-layouts: 55.2 us -> 17.7 us
  starting transfers between devices: 61.4 us -> 42.9 us
  Pallas kernels: 94.9 us -> 110 us
  other arithmetic: 26.8 us -> 20.2 us
  waiting for transfers between devices: 68.9 us -> 72.4 us
    unnamed x196 -> x99, local copies, waits for them, and re-layouts: 36.1 us -> 1.62 us
    ppermute x46 -> x36, starting transfers between devices: 49.5 us -> 31.4 us  [shift(): return lax.ppermute(value, AXES, pairs)]
    pallas_call x12 -> x11, Pallas kernels: 53.9 us -> 67.7 us  [call(): pl.pallas_call(kernel, grid_spec=spec, compiler_params=pltpu.CompilerPara...]
    all_to_all x2, waiting for transfers between devices: 0.01 us -> 5.54 us  [exchange(): lax.all_to_all(blocks, AXES, 0, 0, axis_index_groups=self.groups(('z',)),...]
    reshape x4 -> x0, local copies, waits for them, and re-layouts: 4.8 us -> none  [the longest x1 1.76 us: body(): w_qkv_g = jnp.transpose(per_pair, (2, 3, 0, 1, 4)).reshape(shard, 6 * half)]
    mul x1 -> x0, other arithmetic: 3.63 us -> none  [body(): n1 = centered * rstd1]
    ppermute x46 -> x36, waiting for transfers between devices: 68.9 us -> 66.8 us  [shift(): return lax.ppermute(value, AXES, pairs)]
  transfers between devices with their start and end apart: 49 -> 39, of which waited for: 21 -> 17; matrix products, arithmetic and copies ran while one was open for 12% -> 12% of each run, Pallas kernels for 21% -> 30%
where the time goes in v1:
time: 281 us; the launch traced here: 278 us
  Pallas kernels  110 us (39%)
  waiting for transfers between devices  72.4 us (26%)
  starting transfers between devices  42.9 us (15%)
  other arithmetic  20.2 us (7%)
  local copies, waits for them, and re-layouts  17.7 us (6%)
  between operations  14.9 us (5%)
    pallas_call x11, Pallas kernels, call(): pl.pallas_call(kernel, grid_spec=spec, compiler_params=pltpu.CompilerPara...  67.7 us
    ppermute x36, waiting for transfers between devices, shift(): return lax.ppermute(value, AXES, pairs)  66.8 us
    ppermute x36, starting transfers between devices, shift(): return lax.ppermute(value, AXES, pairs)  31.4 us
    pallas_call x2, Pallas kernels, attn_bwd(): pl.pallas_call(attn_bwd_kernel, grid=(pairs, rows // block), in_specs=[by...  21.2 us
    pallas_call x2, Pallas kernels, attn_fwd(): pl.pallas_call(attn_fwd_kernel, grid=(pairs, rows // block), in_specs=[pl...  20.9 us
    all_to_all x2, starting transfers between devices, exchange(): lax.all_to_all(blocks, AXES, 0, 0, axis_index_groups=self.groups(('z',)),...  11.4 us
  transfers between devices with their start and end apart: 39, of which 17 were waited for; matrix products, arithmetic and copies ran while one was open for 12% of the time, Pallas kernels for 30%

profile of v1, /device:TPU:0, one launch (start us, length us, event | category | flops | bytes accessed | tf_op | source)
XLA Modules:
  0.0 277.9 jit_solution(10920409483626004777)
XLA Ops:
  7.3 1.7 pad_maximum_fusion.7
  9.1 1.2 reshape.212
  10.3 1.3 dynamic-slice_reduce_fusion.1
  14.1 0.9 collective-permute-done
  15.1 2.7 collective-permute-start.4
  18.0 1.6 collective-permute-start.1
  19.6 2.6 collective-permute-start.2
  22.2 1.3 collective-permute-start.3
  23.6 3.0 %collective-permute-done.1 = bf16[64,1152]{1,0:T(8,128)(2,1)S(1)} collective-permute-done((bf16[64,1152]{1,0:T(8,128)(2,1)S(1)}, bf16[64,1152]{1,0:T(8,128)(2,1)S(1)}, u32[]{:S(2)}, u32[]{:S(2)}) %collective-permute-start.1) | collective-permute-done | bytes 147488 | tf_op jit(solution)/shard_map/ppermute | solution.py:49
  26.6 8.5 %collective-permute-done.2 = bf16[64,1152]{1,0:T(8,128)(2,1)S(1)} collective-permute-done((bf16[64,1152]{1,0:T(8,128)(2,1)S(1)}, bf16[64,1152]{1,0:T(8,128)(2,1)S(1)}, u32[]{:S(2)}, u32[]{:S(2)}) %collective-permute-start.2) | collective-permute-done | bytes 147488 | tf_op jit(solution)/shard_map/ppermute | solution.py:49
  35.4 1.6 collective-permute-start.7
  37.2 0.8 broadcast_in_dim.34
  38.1 7.1 %all-to-all-start = ((bf16[4,96,768]{2,1,0:T(8,128)(2,1)}), bf16[4,96,768]{2,1,0:T(8,128)(2,1)}, u32[]{:S(2)}, u32[]{:S(2)}) async-start(bf16[4,96,768]{2,1,0:T(8,128)(2,1)} %broadcast_in_dim.34), calls=%async_computation | async-start | bytes 1179648 | tf_op jit(solution)/shard_map/all_to_all | solution.py:133
  45.2 9.8 %collective-permute-done.7.refs_1_ = bf16[4,64,1152]{2,1,0:T(8,128)(2,1)S(1)} collective-permute-done((bf16[4,64,1152]{2,1,0:T(8,128)(2,1)S(1)}, bf16[4,64,1152]{2,1,0:T(8,128)(2,1)S(1)}, u32[]{:S(2)}, u32[]{:S(2)}) %collective-permute-start.7) | collective-permute-done | bytes 589856 | tf_op jit(solution)/shard_map/ppermute | solution.py:49
  55.0 0.8 slice.225
  56.9 2.2 collective-permute-start.12
  59.0 1.5 select_bitcast_fusion
  60.6 1.0 select_convert_fusion.pen_ref
  61.7 0.9 broadcast_compare_fusion
  62.6 1.1 fusion.6
  63.8 5.5 %all-to-all-done.refs_0_ = bf16[4,96,768]{2,1,0:T(8,128)(2,1)} async-done(((bf16[4,96,768]{2,1,0:T(8,128)(2,1)}), bf16[4,96,768]{2,1,0:T(8,128)(2,1)}, u32[]{:S(2)}, u32[]{:S(2)}) %all-to-all-start) | async-done | bytes 589856 | tf_op jit(solution)/shard_map/all_to_all | solution.py:133
  69.8 1.7 collective-permute-start.14
  74.6 0.9 vectors.1.vec_ref.refs_6_
  75.6 9.1 %qkv.1 = (bf16[768,384]{1,0:T(8,128)(2,1)S(1)}, bf16[1536,384]{1,0:T(8,128)(2,1)S(1)}, bf16[1536,384]{1,0:T(8,128)(2,1)S(1)}, bf16[768,1536]{1,0:T(8,128)(2,1)},...) custom-call(s32[4]{0:T(128)S(1)} %pad_add_fusion.place, ...), custom_call_target="tpu_custom_call" | custom-call | flops 1000 | bytes 1000 | tf_op jit(solution)/shard_map/qkv/pallas_call | solution.py:167
  84.7 7.1 %attn_fwd.2 = (f32[768,128]{1,0:T(8,128)S(1)}, bf16[768,128]{1,0:T(8,128)(2,1)}, f32[1,2,768]{2,1,0:T(2,128)S(1)}) custom-call(bf16[768,384]{1,0:T(8,128)(2,1)S(1)} %get-tuple-element.137.q_ref, bf16[1536,384]{1,0:T(8,128)(2,1)S(1)} %get-tuple-element.128.k_ref, bf16[1536,384]{1,0:T(8,128)(2,1)S(1)} %get-tuple-element.129.v_ref, ...), custom_call_target="tpu_custom_call" | custom-call | flops 1000 | bytes 1000 | tf_op jit(solution)/shard_map/attn_fwd/pallas_call | solution.py:324
  91.9 3.3 %collective-permute-done.13.refs_1_ = bf16[4,96,768]{2,1,0:T(8,128)(2,1)S(1)} collective-permute-done((bf16[4,96,768]{2,1,0:T(8,128)(2,1)}, bf16[4,96,768]{2,1,0:T(8,128)(2,1)S(1)}, u32[]{:S(2)}, u32[]{:S(2)}) %collective-permute-start.13) | collective-permute-done | bytes 589856 | tf_op jit(solution)/shard_map/ppermute | solution.py:49
  95.3 1.7 collective-permute-start.15
  97.0 1.7 collective-permute-start.16
  98.8 13.8 %attn_fwd.3 = (f32[768,256]{1,0:T(8,128)S(1)}, bf16[768,256]{1,0:T(8,128)(2,1)}, f32[2,2,768]{2,1,0:T(2,128)S(1)}) custom-call(bf16[768,384]{1,0:T(8,128)(2,1)S(1)} %get-tuple-element.137.q_ref, bf16[1536,384]{1,0:T(8,128)(2,1)S(1)} %get-tuple-element.128.k_ref, bf16[1536,384]{1,0:T(8,128)(2,1)S(1)} %get-tuple-element.129.v_ref, ...), custom_call_target="tpu_custom_call" | custom-call | flops 1000 | bytes 1000 | tf_op jit(solution)/shard_map/attn_fwd/pallas_call | solution.py:324
  113.9 1.3 select_bitcast_fusion.5
  115.2 1.2 pad_maximum_fusion.1
  116.5 1.4 slice.278
  117.9 5.8 %out_proj.1 = (f32[768,768]{1,0:T(8,128)}, bf16[768,768]{1,0:T(8,128)(2,1)}, bf16[768,768]{1,0:T(8,128)(2,1)}, f32[768,128]{1,0:T(8,128)}) custom-call(s32[4]{0:T(128)S(1)} %pad_add_fusion.place, bf16[1536,768]{1,0:T(8,128)(2,1)S(1)} %pad_maximum_fusion.x_ref, bf16[2,384,768]{2,1,0:T(8,128)(2,1)S(1)} %bitcast.149, f32[16,768]{1,0:T(8,128)S(1)} %copy-done.10, ...), custom_call_target="tpu_custom_call" | custom-call | flops 1000 | bytes 1000 | tf_op jit(solution)/shard_map/out_proj/pallas_call | solution.py:167
  123.7 20.7 %feed_forward.1 = (bf16[4,4,192,768]{3,2,1,0:T(8,128)(2,1)}, f32[2,1,768]{2,1,0:T(1,128)S(1)}, f32[768,768]{1,0:T(8,128)}, f32[768,768]{1,0:T(8,128)S(1)}, bf16[768,768]{1,0:T(8,128)(2,1)S(1)}) custom-call(s32[4]{0:T(128)S(1)} %pad_add_fusion.place, bf16[768,768]{1,0:T(8,128)(2,1)} %get-tuple-element.140.h2_ref, bf16[768,768]{1,0:T(8,128)(2,1)} %bitcast.153, ...), custom_call_target="tpu_custom_call" | custom-call | flops 1000 | bytes 1000 | tf_op jit(solution)/shard_map/feed_forward/pallas_call | solution.py:167
  144.5 1.8 slice_bitcast_fusion.1
  147.3 6.3 %out_back.1 = (f32[768,768]{1,0:T(8,128)}, bf16[768,768]{1,0:T(8,128)(2,1)S(1)}, bf16[768,384]{1,0:T(8,128)(2,1)S(1)}, f32[8,768]{1,0:T(8,128)S(1)}) custom-call(s32[4]{0:T(128)S(1)} %pad_add_fusion.place, f32[768,768]{1,0:T(8,128)S(1)} %get-tuple-element.143.mine_ref, bf16[768,768]{1,0:T(8,128)(2,1)S(1)} %collective-permute-done.19.got_ref, ...), custom_call_target="tpu_custom_call" | custom-call | flops 1000 | bytes 1000 | tf_op jit(solution)/shard_map/out_back/pallas_call | solution.py:167
  153.7 6.9 %attn_bwd.2 = (bf16[768,128]{1,0:T(8,128)(2,1)S(1)}, bf16[1536,128]{1,0:T(8,128)(2,1)S(1)}, bf16[1536,128]{1,0:T(8,128)(2,1)S(1)}) custom-call(bf16[768,384]{1,0:T(8,128)(2,1)S(1)} %copy-done.6, bf16[1536,384]{1,0:T(8,128)(2,1)S(1)} %get-tuple-element.128.k_ref, bf16[1536,384]{1,0:T(8,128)(2,1)S(1)} %copy-done.1, bf16[768,128]{1,0:T(8,128)(2,1)S(1)} %copy-done.8, ...), custom_call_target="tpu_custom_call" | custom-call | flops 1000 | bytes 1000 | tf_op jit(solution)/shard_map/attn_bwd/pallas_call | solution.py:420
  160.5 1.5 collective-permute-done.20
  162.6 1.7 collective-permute-start.23
  165.4 14.4 %attn_bwd.3 = (bf16[768,256]{1,0:T(8,128)(2,1)S(1)}, bf16[1536,256]{1,0:T(8,128)(2,1)S(1)}, bf16[1536,256]{1,0:T(8,128)(2,1)S(1)}) custom-call(bf16[768,384]{1,0:T(8,128)(2,1)S(1)} %copy-done.6, bf16[1536,384]{1,0:T(8,128)(2,1)S(1)} %get-tuple-element.128.k_ref, bf16[1536,384]{1,0:T(8,128)(2,1)S(1)} %copy-done.1, bf16[768,128]{1,0:T(8,128)(2,1)S(1)} %copy-done.8, ...), custom_call_target="tpu_custom_call" | custom-call | flops 1000 | bytes 1000 | tf_op jit(solution)/shard_map/attn_bwd/pallas_call | solution.py:420
  179.8 9.0 %input_back.1 = (f32[2,384,768]{2,1,0:T(8,128)}, bf16[2,384,768]{2,1,0:T(8,128)(2,1)S(1)}, f32[8,768]{1,0:T(8,128)S(1)}) custom-call(s32[4]{0:T(128)S(1)} %pad_add_fusion.place, bf16[768,128]{1,0:T(8,128)(2,1)S(1)} %get-tuple-element.148.refs_0_.refs_4_, bf16[1536,128]{1,0:T(8,128)(2,1)S(1)} %get-tuple-element.149.refs_1_.refs_5_, ...), custom_call_target="tpu_custom_call" | custom-call | flops 1000 | bytes 1000 | tf_op jit(solution)/shard_map/input_back/pallas_call | solution.py:167
  188.8 8.0 %matrix_grads.1 = bf16[4,4,4,64,384]{4,3,2,1,0:T(8,128)(2,1)} custom-call(s32[4]{0:T(128)S(1)} %pad_add_fusion.place, bf16[768,1536]{1,0:T(8,128)(2,1)} %get-tuple-element.163.h1t_ref, bf16[768,768]{1,0:T(8,128)(2,1)S(1)} %get-tuple-element.164.d_ref, bf16[768,128]{1,0:T(8,128)(2,1)} %get-tuple-element.130.refs_0_, ...), custom_call_target="tpu_custom_call" | custom-call | flops 1000 | bytes 1000 | tf_op jit(solution)/shard_map/matrix_grads/pallas_call | solution.py:167
  196.8 1.5 fusion.1
  198.3 2.8 %collective-permute-done.24.refs_1_ = bf16[2,384,768]{2,1,0:T(8,128)(2,1)S(1)} collective-permute-done((bf16[2,384,768]{2,1,0:T(8,128)(2,1)S(1)}, bf16[2,384,768]{2,1,0:T(8,128)(2,1)S(1)}, u32[]{:S(2)}, u32[]{:S(2)}) %collective-permute-start.24) | collective-permute-done | bytes 1179680 | tf_op jit(solution)/shard_map/ppermute | solution.py:49
  201.8 1.1 slice_bitcast_fusion.5
  202.9 1.6 collective-permute-start.27
  204.5 1.1 collective-permute-start.29
  205.6 4.3 %all-to-all-start.1 = ((bf16[4,192,768]{2,1,0:T(8,128)(2,1)}), bf16[4,192,768]{2,1,0:T(8,128)(2,1)}, u32[]{:S(2)}, u32[]{:S(2)}) async-start(bf16[4,192,768]{2,1,0:T(8,128)(2,1)} %fusion.1), calls=%async_computation.1 | async-start | bytes 2359296 | tf_op jit(solution)/shard_map/all_to_all | solution.py:133
  209.9 15.4 %collective-permute-done.27 = bf16[2,4,64,384]{3,2,1,0:T(8,128)(2,1)} collective-permute-done((bf16[2,4,64,384]{3,2,1,0:T(8,128)(2,1)}, bf16[2,4,64,384]{3,2,1,0:T(8,128)(2,1)}, u32[]{:S(2)}, u32[]{:S(2)}) %collective-permute-start.27) | collective-permute-done | bytes 393248 | tf_op jit(solution)/shard_map/ppermute | solution.py:49
  225.3 1.6 fusion.11
  227.6 1.1 collective-permute-start.28
  228.7 2.2 fusion.15
  230.9 14.9 %collective-permute-done.30 = bf16[4,4,64,384]{3,2,1,0:T(8,128)(2,1)S(1)} collective-permute-done((bf16[4,4,64,384]{3,2,1,0:T(8,128)(2,1)S(1)}, bf16[4,4,64,384]{3,2,1,0:T(8,128)(2,1)S(1)}, u32[]{:S(2)}, u32[]{:S(2)}) %collective-permute-start.30) | collective-permute-done | bytes 786464 | tf_op jit(solution)/shard_map/ppermute | solution.py:49
  246.1 1.5 fusion.3
  247.6 0.8 slice_bitcast_fusion.10
  248.5 1.3 collective-permute-start.31
  249.8 2.7 collective-permute-start.32
  252.5 1.4 add_bitcast_fusion.ff_ref
  254.0 4.4 %finish.1 = f32[384,768]{1,0:T(8,128)} custom-call(s32[4]{0:T(128)S(1)} %pad_add_fusion.place, f32[2,384,768]{2,1,0:T(8,128)} %get-tuple-element.162.refs_0_, bf16[2,384,768]{2,1,0:T(8,128)(2,1)S(1)} %collective-permute-done.24.refs_1_, bf16[384,768]{1,0:T(8,128)(2,1)S(1)} %collective-permute-done.26.refs_2_, ...), custom_call_target="tpu_custom_call" | custom-call | flops 1000 | bytes 1000 | tf_op jit(solution)/shard_map/finish/pallas_call | solution.py:167
  258.5 5.6 %collective-permute-done.32 = bf16[4,64,384]{2,1,0:T(8,128)(2,1)} collective-permute-done((bf16[4,64,384]{2,1,0:T(8,128)(2,1)}, bf16[4,64,384]{2,1,0:T(8,128)(2,1)}, u32[]{:S(2)}, u32[]{:S(2)}) %collective-permute-start.32) | collective-permute-done | bytes 196640 | tf_op jit(solution)/shard_map/ppermute | solution.py:49
  264.1 1.2 fusion.25
  265.4 2.1 fusion.16
  267.5 1.7 last_ff.1
  269.2 1.3 last_rest.1
  (215 shorter events, 14.7 us)
Async XLA Ops:
  7.2 6.0 %copy-start.41 = (bf16[24]{0:T(256)(128)(2,1)S(1)}, bf16[24]{0:T(256)(128)(2,1)}, u32[]{:S(2)}) copy-start(bf16[24]{0:T(256)(128)(2,1)} %param.27) | copy-start | bytes 148
  7.2 6.1 %copy-start.42 = (bf16[24]{0:T(256)(128)(2,1)S(1)}, bf16[24]{0:T(256)(128)(2,1)}, u32[]{:S(2)}) copy-start(bf16[24]{0:T(256)(128)(2,1)} %param.26) | copy-start | bytes 148
  7.2 6.2 %copy-start.43 = (bf16[24]{0:T(256)(128)(2,1)S(1)}, bf16[24]{0:T(256)(128)(2,1)}, u32[]{:S(2)}) copy-start(bf16[24]{0:T(256)(128)(2,1)} %param.22) | copy-start | bytes 148
  7.3 6.3 %copy-start.44 = (bf16[24]{0:T(256)(128)(2,1)S(1)}, bf16[24]{0:T(256)(128)(2,1)}, u32[]{:S(2)}) copy-start(bf16[24]{0:T(256)(128)(2,1)} %param.21) | copy-start | bytes 148
  7.3 109.2 %all-gather.3.cloned.1.call-start = ((), (), s32[]{:S(2)}) async-start(), calls=%async_computation.2 | async-start | bytes 6082560 | tf_op jit(solution)/shard_map/all_gather | solution.py:1122
  11.7 6.2 %collective-permute-start.6 = (bf16[24,1536]{1,0:T(8,128)(2,1)S(1)}, bf16[24,1536]{1,0:T(8,128)(2,1)S(1)}, u32[]{:S(2)}, u32[]{:S(2)}) collective-permute-start(bf16[24,1536]{1,0:T(8,128)(2,1)S(1)} %reshape.214), channel_id=1, source_target_pairs={{0,1},{1,0},{2,3},{3,2},{4,5},{5,4},{6,7},{7,6},{8,9},{9,8},{10,11... | collective-permute-start | bytes 221192 | tf_op jit(solution)/shard_map/ppermute | solution.py:49
  13.7 1.4 collective-permute-start
  15.1 20.1 %collective-permute-start.4 = (bf16[400,768]{1,0:T(8,128)(2,1)S(1)}, bf16[400,768]{1,0:T(8,128)(2,1)S(1)}, u32[]{:S(2)}, u32[]{:S(2)}) collective-permute-start(bf16[400,768]{1,0:T(8,128)(2,1)S(1)} %fusion.13), channel_id=1, source_target_pairs={{0,2},{1,3},{2,0},{3,1},{4,6},{5,7},{6,4},{7,5},{8,10},{9,11},{10,... | collective-permute-start | bytes 1843208 | tf_op jit(solution)/shard_map/ppermute | solution.py:49
  17.8 17.4 %collective-permute-start.5 = (bf16[400,768]{1,0:T(8,128)(2,1)S(1)}, bf16[400,768]{1,0:T(8,128)(2,1)}, u32[]{:S(2)}, u32[]{:S(2)}) collective-permute-start(bf16[400,768]{1,0:T(8,128)(2,1)S(1)} %fusion.13), channel_id=1, source_target_pairs={{0,1},{1,0},{2,3},{3,2},{4,5},{5,4},{6,7},{7,6},{8,9},{9,8},{10,11... | collective-permute-start | bytes 1843208 | tf_op jit(solution)/shard_map/ppermute | solution.py:49
  18.0 8.6 %collective-permute-start.1 = (bf16[64,1152]{1,0:T(8,128)(2,1)S(1)}, bf16[64,1152]{1,0:T(8,128)(2,1)S(1)}, u32[]{:S(2)}, u32[]{:S(2)}) collective-permute-start(bf16[64,1152]{1,0:T(8,128)(2,1)S(1)} %fusion.21), channel_id=1, source_target_pairs={{0,8},{1,9},{2,10},{3,11},{4,12},{5,13},{6,14},{7,15},{8,16},{9,17... | collective-permute-start | bytes 442376 | tf_op jit(solution)/shard_map/ppermute | solution.py:49
  19.6 15.5 %collective-permute-start.2 = (bf16[64,1152]{1,0:T(8,128)(2,1)S(1)}, bf16[64,1152]{1,0:T(8,128)(2,1)S(1)}, u32[]{:S(2)}, u32[]{:S(2)}) collective-permute-start(bf16[64,1152]{1,0:T(8,128)(2,1)S(1)} %fusion.21), channel_id=1, source_target_pairs={{0,16},{1,17},{2,18},{3,19},{4,20},{5,21},{6,22},{7,23},{8,24},{9,... | collective-permute-start | bytes 442376 | tf_op jit(solution)/shard_map/ppermute | solution.py:49
  22.2 13.0 %collective-permute-start.3 = (bf16[64,1152]{1,0:T(8,128)(2,1)S(1)}, bf16[64,1152]{1,0:T(8,128)(2,1)S(1)}, u32[]{:S(2)}, u32[]{:S(2)}) collective-permute-start(bf16[64,1152]{1,0:T(8,128)(2,1)S(1)} %fusion.21), channel_id=1, source_target_pairs={{0,24},{1,25},{2,26},{3,27},{4,28},{5,29},{6,30},{7,31},{8,0},{9,1... | collective-permute-start | bytes 442376 | tf_op jit(solution)/shard_map/ppermute | solution.py:49
  26.6 18.6 %collective-permute-start.10 = (bf16[384,768]{1,0:T(8,128)(2,1)}, bf16[384,768]{1,0:T(8,128)(2,1)}, u32[]{:S(2)}, u32[]{:S(2)}) collective-permute-start(bf16[384,768]{1,0:T(8,128)(2,1)} %bitcast.23), channel_id=1, source_target_pairs={{0,1},{1,0},{2,3},{3,2},{4,5},{5,4},{6,7},{7,6},{8,9},{9,8},{10,11... | collective-permute-start | bytes 1769480 | tf_op jit(solution)/shard_map/ppermute | solution.py:49
  35.2 19.8 %collective-permute-start.9 = (bf16[400,768]{1,0:T(8,128)(2,1)S(1)}, bf16[400,768]{1,0:T(8,128)(2,1)}, u32[]{:S(2)}, u32[]{:S(2)}) collective-permute-start(bf16[400,768]{1,0:T(8,128)(2,1)S(1)} %collective-permute-done.4), channel_id=1, source_target_pairs={{0,1},{1,0},{2,3},{3,2},{4,5},{5,4},{6,7},{7,6},{8,9},{9,8},{10,11... | collective-permute-start | bytes 1843208 | tf_op jit(solution)/shard_map/ppermute | solution.py:49
  35.4 20.5 %copy-start.22 = (bf16[4,64,1152]{2,1,0:T(8,128)(2,1)}, bf16[4,64,1152]{2,1,0:T(8,128)(2,1)S(1)}, u32[]{:S(2)}) copy-start(bf16[4,64,1152]{2,1,0:T(8,128)(2,1)S(1)} %pad_maximum_fusion.6.refs_0_) | copy-start | bytes 1769476
  35.4 19.6 %collective-permute-start.7 = (bf16[4,64,1152]{2,1,0:T(8,128)(2,1)S(1)}, bf16[4,64,1152]{2,1,0:T(8,128)(2,1)S(1)}, u32[]{:S(2)}, u32[]{:S(2)}) collective-permute-start(bf16[4,64,1152]{2,1,0:T(8,128)(2,1)S(1)} %pad_maximum_fusion.6.refs_0_), channel_id=1, source_target_pairs={{0,4},{1,5},{2,6},{3,7},{4,0},{5,1},{6,2},{7,3},{8,12},{9,13},{10,... | collective-permute-start | bytes 1769480 | tf_op jit(solution)/shard_map/ppermute | solution.py:49
  37.0 18.1 %collective-permute-start.8 = (bf16[4,64,1152]{2,1,0:T(8,128)(2,1)S(1)}, bf16[4,64,1152]{2,1,0:T(8,128)(2,1)S(1)}, u32[]{:S(2)}, u32[]{:S(2)}) collective-permute-start(bf16[4,64,1152]{2,1,0:T(8,128)(2,1)S(1)} %pad_maximum_fusion.6.refs_0_), channel_id=1, source_target_pairs={{0,2},{1,3},{2,0},{3,1},{4,6},{5,7},{6,4},{7,5},{8,10},{9,11},{10,... | collective-permute-start | bytes 1769480 | tf_op jit(solution)/shard_map/ppermute | solution.py:49
  38.1 31.2 %all-to-all-start = ((bf16[4,96,768]{2,1,0:T(8,128)(2,1)}), bf16[4,96,768]{2,1,0:T(8,128)(2,1)}, u32[]{:S(2)}, u32[]{:S(2)}) async-start(bf16[4,96,768]{2,1,0:T(8,128)(2,1)} %broadcast_in_dim.34), calls=%async_computation | async-start | bytes 1179648 | tf_op jit(solution)/shard_map/all_to_all | solution.py:133
  45.2 13.9 %copy-start.29 = (bf16[400,768]{1,0:T(8,128)(2,1)S(1)}, bf16[400,768]{1,0:T(8,128)(2,1)}, u32[]{:S(2)}) copy-start(bf16[400,768]{1,0:T(8,128)(2,1)} %copy-done.28) | copy-start | bytes 1843204
  55.8 13.5 %collective-permute-start.11 = (bf16[2,64,1152]{2,1,0:T(8,128)(2,1)}, bf16[2,64,1152]{2,1,0:T(8,128)(2,1)S(1)}, u32[]{:S(2)}, u32[]{:S(2)}) collective-permute-start(bf16[2,64,1152]{2,1,0:T(8,128)(2,1)} %slice.225), channel_id=1, source_target_pairs={{0,2},{1,3},{2,0},{3,1},{4,6},{5,7},{6,4},{7,5},{8,10},{9,11},{10,... | collective-permute-start | bytes 884744 | tf_op jit(solution)/shard_map/ppermute | solution.py:49
  56.9 12.4 %collective-permute-start.12 = (bf16[2,64,1152]{2,1,0:T(8,128)(2,1)}, bf16[2,64,1152]{2,1,0:T(8,128)(2,1)}, u32[]{:S(2)}, u32[]{:S(2)}) collective-permute-start(bf16[2,64,1152]{2,1,0:T(8,128)(2,1)} %slice.227), channel_id=1, source_target_pairs={{0,4},{1,5},{2,6},{3,7},{4,0},{5,1},{6,2},{7,3},{8,12},{9,13},{10,... | collective-permute-start | bytes 884744 | tf_op jit(solution)/shard_map/ppermute | solution.py:49
  69.3 25.9 %collective-permute-start.13 = (bf16[4,96,768]{2,1,0:T(8,128)(2,1)}, bf16[4,96,768]{2,1,0:T(8,128)(2,1)S(1)}, u32[]{:S(2)}, u32[]{:S(2)}) collective-permute-start(bf16[4,96,768]{2,1,0:T(8,128)(2,1)} %all-to-all-done.refs_0_), channel_id=1, source_target_pairs={{0,4},{1,5},{2,6},{3,7},{4,0},{5,1},{6,2},{7,3},{8,12},{9,13},{10,... | collective-permute-start | bytes 1769480 | tf_op jit(solution)/shard_map/ppermute | solution.py:49
  69.8 25.4 %collective-permute-start.14 = (bf16[4,96,768]{2,1,0:T(8,128)(2,1)}, bf16[4,96,768]{2,1,0:T(8,128)(2,1)S(1)}, u32[]{:S(2)}, u32[]{:S(2)}) collective-permute-start(bf16[4,96,768]{2,1,0:T(8,128)(2,1)} %all-to-all-done.refs_0_), channel_id=1, source_target_pairs={{0,2},{1,3},{2,0},{3,1},{4,6},{5,7},{6,4},{7,5},{8,10},{9,11},{10,... | collective-permute-start | bytes 1769480 | tf_op jit(solution)/shard_map/ppermute | solution.py:49
  75.5 9.2 %copy-start.9 = (f32[16,768]{1,0:T(8,128)}, f32[16,768]{1,0:T(8,128)S(1)}, u32[]{:S(2)}) copy-start(f32[16,768]{1,0:T(8,128)S(1)} %vectors.1.vec_ref.refs_6_) | copy-start | bytes 147460
  75.6 23.2 %copy-start.7 = (bf16[768,128]{1,0:T(8,128)(2,1)}, bf16[768,128]{1,0:T(8,128)(2,1)S(1)}, u32[]{:S(2)}) copy-start(bf16[768,128]{1,0:T(8,128)(2,1)S(1)} %slice_convert_fusion.hot_ref) | copy-start | bytes 589828
  75.6 9.2 %copy-start.3 = (bf16[1536,128]{1,0:T(8,128)(2,1)S(1)}, bf16[1536,128]{1,0:T(8,128)(2,1)}, u32[]{:S(2)}) copy-start(bf16[1536,128]{1,0:T(8,128)(2,1)} %select_convert_fusion.pen_ref) | copy-start | bytes 1179652
  84.7 14.0 %copy-start = (bf16[1536,384]{1,0:T(8,128)(2,1)}, bf16[1536,384]{1,0:T(8,128)(2,1)S(1)}, u32[]{:S(2)}) copy-start(bf16[1536,384]{1,0:T(8,128)(2,1)S(1)} %get-tuple-element.129.v_ref) | copy-start | bytes 3538948
  84.7 14.0 %copy-start.5 = (bf16[768,384]{1,0:T(8,128)(2,1)}, bf16[768,384]{1,0:T(8,128)(2,1)S(1)}, u32[]{:S(2)}) copy-start(bf16[768,384]{1,0:T(8,128)(2,1)S(1)} %get-tuple-element.137.q_ref) | copy-start | bytes 1769476
  91.9 6.9 %copy-start.15 = (f32[768,128]{1,0:T(8,128)}, f32[768,128]{1,0:T(8,128)S(1)}, u32[]{:S(2)}) copy-start(f32[768,128]{1,0:T(8,128)S(1)} %get-tuple-element.133.o_ref) | copy-start | bytes 1179652
  91.9 20.7 %copy-start.17 = (f32[1,2,768]{2,1,0:T(2,128)}, f32[1,2,768]{2,1,0:T(2,128)S(1)}, u32[]{:S(2)}) copy-start(f32[1,2,768]{2,1,0:T(2,128)S(1)} %get-tuple-element.134.lse_ref) | copy-start | bytes 18436
  95.2 17.4 %copy-start.26 = (bf16[4,96,768]{2,1,0:T(8,128)(2,1)}, bf16[4,96,768]{2,1,0:T(8,128)(2,1)S(1)}, u32[]{:S(2)}) copy-start(bf16[4,96,768]{2,1,0:T(8,128)(2,1)S(1)} %collective-permute-done.13.refs_1_) | copy-start | bytes 1769476
  95.3 17.3 %copy-start.27 = (bf16[4,96,768]{2,1,0:T(8,128)(2,1)}, bf16[4,96,768]{2,1,0:T(8,128)(2,1)S(1)}, u32[]{:S(2)}) copy-start(bf16[4,96,768]{2,1,0:T(8,128)(2,1)S(1)} %collective-permute-done.14.refs_2_) | copy-start | bytes 1769476
  95.3 17.3 %collective-permute-start.15 = (bf16[2,96,768]{2,1,0:T(8,128)(2,1)S(1)}, bf16[2,96,768]{2,1,0:T(8,128)(2,1)S(1)}, u32[]{:S(2)}, u32[]{:S(2)}) collective-permute-start(bf16[2,96,768]{2,1,0:T(8,128)(2,1)S(1)} %slice.232), channel_id=1, source_target_pairs={{0,2},{1,3},{2,0},{3,1},{4,6},{5,7},{6,4},{7,5},{8,10},{9,11},{10,... | collective-permute-start | bytes 884744 | tf_op jit(solution)/shard_map/ppermute | solution.py:49
  97.0 15.6 %collective-permute-start.16 = (bf16[2,96,768]{2,1,0:T(8,128)(2,1)S(1)}, bf16[2,96,768]{2,1,0:T(8,128)(2,1)S(1)}, u32[]{:S(2)}, u32[]{:S(2)}) collective-permute-start(bf16[2,96,768]{2,1,0:T(8,128)(2,1)S(1)} %slice.233), channel_id=1, source_target_pairs={{0,4},{1,5},{2,6},{3,7},{4,0},{5,1},{6,2},{7,3},{8,12},{9,13},{10,... | collective-permute-start | bytes 884744 | tf_op jit(solution)/shard_map/ppermute | solution.py:49
  98.7 19.1 %collective-permute-start.17 = (bf16[768,128]{1,0:T(8,128)(2,1)}, bf16[768,128]{1,0:T(8,128)(2,1)}, u32[]{:S(2)}, u32[]{:S(2)}) collective-permute-start(bf16[768,128]{1,0:T(8,128)(2,1)} %get-tuple-element.130.refs_0_), channel_id=1, source_target_pairs={{0,1},{1,0},{2,3},{3,2},{4,5},{5,4},{6,7},{7,6},{8,9},{9,8},{10,11... | collective-permute-start | bytes 589832 | tf_op jit(solution)/shard_map/ppermute | solution.py:49
  113.4 4.4 %collective-permute-start.18 = (bf16[768,256]{1,0:T(8,128)(2,1)}, bf16[768,256]{1,0:T(8,128)(2,1)}, u32[]{:S(2)}, u32[]{:S(2)}) collective-permute-start(bf16[768,256]{1,0:T(8,128)(2,1)} %get-tuple-element.139.refs_1_), channel_id=1, source_target_pairs={{0,1},{1,0},{2,3},{3,2},{4,5},{5,4},{6,7},{7,6},{8,9},{9,8},{10,11... | collective-permute-start | bytes 1179656 | tf_op jit(solution)/shard_map/ppermute | solution.py:49
  144.4 2.9 %collective-permute-start.19 = (bf16[768,768]{1,0:T(8,128)(2,1)S(1)}, bf16[768,768]{1,0:T(8,128)(2,1)S(1)}, u32[]{:S(2)}, u32[]{:S(2)}) collective-permute-start(bf16[768,768]{1,0:T(8,128)(2,1)S(1)} %get-tuple-element.144), channel_id=1, source_target_pairs={{0,1},{1,0},{2,3},{3,2},{4,5},{5,4},{6,7},{7,6},{8,9},{9,8},{10,11... | collective-permute-start | bytes 3538952 | tf_op jit(solution)/shard_map/ppermute | solution.py:49
  144.5 17.7 %slice-start = ((s8[4718592]{0:T(1024)(128)(4,1)}), s8[524288]{0:T(1024)(128)(4,1)S(1)}, s32[]{:S(2)}) async-start(s8[4718592]{0:T(1024)(128)(4,1)} %bitcast.157), calls=%async_computation.3 | async-start | bytes 1048576
  146.3 15.8 %collective-permute-start.20 = (bf16[2,192,768]{2,1,0:T(8,128)(2,1)S(1)}, bf16[2,192,768]{2,1,0:T(8,128)(2,1)S(1)}, u32[]{:S(2)}, u32[]{:S(2)}) collective-permute-start(bf16[2,192,768]{2,1,0:T(8,128)(2,1)S(1)} %get-tuple-element.200), channel_id=1, source_target_pairs={{0,2},{1,3},{2,0},{3,1},{4,6},{5,7},{6,4},{7,5},{8,10},{9,11},{10,... | collective-permute-start | bytes 1769480 | tf_op jit(solution)/shard_map/ppermute | solution.py:49
  146.8 15.4 %collective-permute-start.21 = (bf16[2,192,768]{2,1,0:T(8,128)(2,1)S(1)}, bf16[2,192,768]{2,1,0:T(8,128)(2,1)S(1)}, u32[]{:S(2)}, u32[]{:S(2)}) collective-permute-start(bf16[2,192,768]{2,1,0:T(8,128)(2,1)S(1)} %get-tuple-element.198), channel_id=1, source_target_pairs={{0,4},{1,5},{2,6},{3,7},{4,0},{5,1},{6,2},{7,3},{8,12},{9,13},{10,... | collective-permute-start | bytes 1769480 | tf_op jit(solution)/shard_map/ppermute | solution.py:49
  147.3 6.3 %copy-start.1 = (bf16[1536,384]{1,0:T(8,128)(2,1)S(1)}, bf16[1536,384]{1,0:T(8,128)(2,1)}, u32[]{:S(2)}) copy-start(bf16[1536,384]{1,0:T(8,128)(2,1)} %copy-done) | copy-start | bytes 3538948
  147.3 6.3 %copy-start.4 = (bf16[1536,128]{1,0:T(8,128)(2,1)S(1)}, bf16[1536,128]{1,0:T(8,128)(2,1)}, u32[]{:S(2)}) copy-start(bf16[1536,128]{1,0:T(8,128)(2,1)} %select_convert_fusion.pen_ref) | copy-start | bytes 1179652
  147.3 6.3 %copy-start.6 = (bf16[768,384]{1,0:T(8,128)(2,1)S(1)}, bf16[768,384]{1,0:T(8,128)(2,1)}, u32[]{:S(2)}) copy-start(bf16[768,384]{1,0:T(8,128)(2,1)} %copy-done.5) | copy-start | bytes 1769476
  147.3 6.3 %copy-start.8 = (bf16[768,128]{1,0:T(8,128)(2,1)S(1)}, bf16[768,128]{1,0:T(8,128)(2,1)}, u32[]{:S(2)}) copy-start(bf16[768,128]{1,0:T(8,128)(2,1)} %copy-done.7) | copy-start | bytes 589828
  147.3 6.3 %copy-start.16 = (f32[768,128]{1,0:T(8,128)S(1)}, f32[768,128]{1,0:T(8,128)}, u32[]{:S(2)}) copy-start(f32[768,128]{1,0:T(8,128)} %copy-done.15) | copy-start | bytes 1179652
  147.3 6.3 %copy-start.18 = (f32[1,2,768]{2,1,0:T(2,128)S(1)}, f32[1,2,768]{2,1,0:T(2,128)}, u32[]{:S(2)}) copy-start(f32[1,2,768]{2,1,0:T(2,128)} %copy-done.17) | copy-start | bytes 18436
  147.3 14.9 %slice-start.1 = ((s8[4718592]{0:T(1024)(128)(4,1)}), s8[4194304]{0:T(1024)(128)(4,1)S(1)}, s32[]{:S(2)}) async-start(s8[4718592]{0:T(1024)(128)(4,1)} %bitcast.157), calls=%async_computation.4 | async-start | bytes 8388608
  162.6 34.2 %collective-permute-start.23 = (bf16[4,192,768]{2,1,0:T(8,128)(2,1)S(1)}, bf16[4,192,768]{2,1,0:T(8,128)(2,1)S(1)}, u32[]{:S(2)}, u32[]{:S(2)}) collective-permute-start(bf16[4,192,768]{2,1,0:T(8,128)(2,1)S(1)} %pad_maximum_fusion.3), channel_id=1, source_target_pairs={{0,2},{1,3},{2,0},{3,1},{4,6},{5,7},{6,4},{7,5},{8,10},{9,11},{10,... | collective-permute-start | bytes 3538952 | tf_op jit(solution)/shard_map/ppermute | solution.py:49
  164.4 32.4 %collective-permute-start.22 = (bf16[4,192,768]{2,1,0:T(8,128)(2,1)S(1)}, bf16[4,192,768]{2,1,0:T(8,128)(2,1)S(1)}, u32[]{:S(2)}, u32[]{:S(2)}) collective-permute-start(bf16[4,192,768]{2,1,0:T(8,128)(2,1)S(1)} %pad_maximum_fusion.2), channel_id=1, source_target_pairs={{0,4},{1,5},{2,6},{3,7},{4,0},{5,1},{6,2},{7,3},{8,12},{9,13},{10,... | collective-permute-start | bytes 3538952 | tf_op jit(solution)/shard_map/ppermute | solution.py:49
  198.3 2.8 %collective-permute-start.24 = (bf16[2,384,768]{2,1,0:T(8,128)(2,1)S(1)}, bf16[2,384,768]{2,1,0:T(8,128)(2,1)S(1)}, u32[]{:S(2)}, u32[]{:S(2)}) collective-permute-start(bf16[2,384,768]{2,1,0:T(8,128)(2,1)S(1)} %get-tuple-element.171), channel_id=1, source_target_pairs={{0,1},{1,0},{2,3},{3,2},{4,5},{5,4},{6,7},{7,6},{8,9},{9,8},{10,11... | collective-permute-start | bytes 3538952 | tf_op jit(solution)/shard_map/ppermute | solution.py:49
  201.3 24.0 %collective-permute-start.26 = (bf16[384,768]{1,0:T(8,128)(2,1)S(1)}, bf16[384,768]{1,0:T(8,128)(2,1)S(1)}, u32[]{:S(2)}, u32[]{:S(2)}) collective-permute-start(bf16[384,768]{1,0:T(8,128)(2,1)S(1)} %fusion.14), channel_id=1, source_target_pairs={{0,2},{1,3},{2,0},{3,1},{4,6},{5,7},{6,4},{7,5},{8,10},{9,11},{10,... | collective-permute-start | bytes 1769480 | tf_op jit(solution)/shard_map/ppermute | solution.py:49
  202.9 22.4 %collective-permute-start.27 = (bf16[2,4,64,384]{3,2,1,0:T(8,128)(2,1)}, bf16[2,4,64,384]{3,2,1,0:T(8,128)(2,1)}, u32[]{:S(2)}, u32[]{:S(2)}) collective-permute-start(bf16[2,4,64,384]{3,2,1,0:T(8,128)(2,1)} %get-tuple-element.206), channel_id=1, source_target_pairs={{0,2},{1,3},{2,0},{3,1},{4,6},{5,7},{6,4},{7,5},{8,10},{9,11},{10,... | collective-permute-start | bytes 1179656 | tf_op jit(solution)/shard_map/ppermute | solution.py:49
  204.5 20.8 %collective-permute-start.29 = (bf16[2,4,64,384]{3,2,1,0:T(8,128)(2,1)}, bf16[2,4,64,384]{3,2,1,0:T(8,128)(2,1)}, u32[]{:S(2)}, u32[]{:S(2)}) collective-permute-start(bf16[2,4,64,384]{3,2,1,0:T(8,128)(2,1)} %get-tuple-element.204), channel_id=1, source_target_pairs={{0,4},{1,5},{2,6},{3,7},{4,0},{5,1},{6,2},{7,3},{8,12},{9,13},{10,... | collective-permute-start | bytes 1179656 | tf_op jit(solution)/shard_map/ppermute | solution.py:49
  205.6 46.9 %all-to-all-start.1 = ((bf16[4,192,768]{2,1,0:T(8,128)(2,1)}), bf16[4,192,768]{2,1,0:T(8,128)(2,1)}, u32[]{:S(2)}, u32[]{:S(2)}) async-start(bf16[4,192,768]{2,1,0:T(8,128)(2,1)} %fusion.1), calls=%async_computation.1 | async-start | bytes 2359296 | tf_op jit(solution)/shard_map/all_to_all | solution.py:133
  227.0 18.8 %collective-permute-start.30 = (bf16[4,4,64,384]{3,2,1,0:T(8,128)(2,1)S(1)}, bf16[4,4,64,384]{3,2,1,0:T(8,128)(2,1)S(1)}, u32[]{:S(2)}, u32[]{:S(2)}) collective-permute-start(bf16[4,4,64,384]{3,2,1,0:T(8,128)(2,1)S(1)} %pad_maximum_fusion.5), channel_id=1, source_target_pairs={{0,2},{1,3},{2,0},{3,1},{4,6},{5,7},{6,4},{7,5},{8,10},{9,11},{10,... | collective-permute-start | bytes 2359304 | tf_op jit(solution)/shard_map/ppermute | solution.py:49
  227.6 18.5 %collective-permute-start.28 = (bf16[4,4,64,384]{3,2,1,0:T(8,128)(2,1)S(1)}, bf16[4,4,64,384]{3,2,1,0:T(8,128)(2,1)S(1)}, u32[]{:S(2)}, u32[]{:S(2)}) collective-permute-start(bf16[4,4,64,384]{3,2,1,0:T(8,128)(2,1)S(1)} %pad_maximum_fusion.4), channel_id=1, source_target_pairs={{0,4},{1,5},{2,6},{3,7},{4,0},{5,1},{6,2},{7,3},{8,12},{9,13},{10,... | collective-permute-start | bytes 2359304 | tf_op jit(solution)/shard_map/ppermute | solution.py:49
  230.9 34.5 %collective-permute-start.25 = (bf16[384,768]{1,0:T(8,128)(2,1)}, bf16[384,768]{1,0:T(8,128)(2,1)}, u32[]{:S(2)}, u32[]{:S(2)}) collective-permute-start(bf16[384,768]{1,0:T(8,128)(2,1)} %fusion.15), channel_id=1, source_target_pairs={{0,1},{1,0},{2,3},{3,2},{4,5},{5,4},{6,7},{7,6},{8,9},{9,8},{10,11... | collective-permute-start | bytes 1769480 | tf_op jit(solution)/shard_map/ppermute | solution.py:49
  248.5 10.0 %collective-permute-start.31 = (bf16[4,64,384]{2,1,0:T(8,128)(2,1)}, bf16[4,64,384]{2,1,0:T(8,128)(2,1)}, u32[]{:S(2)}, u32[]{:S(2)}) collective-permute-start(bf16[4,64,384]{2,1,0:T(8,128)(2,1)} %get-tuple-element.214), channel_id=1, source_target_pairs={{0,8},{1,9},{2,10},{3,11},{4,12},{5,13},{6,14},{7,15},{8,16},{9,17... | collective-permute-start | bytes 589832 | tf_op jit(solution)/shard_map/ppermute | solution.py:49
  249.8 14.2 %collective-permute-start.32 = (bf16[4,64,384]{2,1,0:T(8,128)(2,1)}, bf16[4,64,384]{2,1,0:T(8,128)(2,1)}, u32[]{:S(2)}, u32[]{:S(2)}) collective-permute-start(bf16[4,64,384]{2,1,0:T(8,128)(2,1)} %get-tuple-element.216), channel_id=1, source_target_pairs={{0,16},{1,17},{2,18},{3,19},{4,20},{5,21},{6,22},{7,23},{8,24},{9,... | collective-permute-start | bytes 589832 | tf_op jit(solution)/shard_map/ppermute | solution.py:49
  252.5 11.6 %collective-permute-start.33 = (bf16[4,64,384]{2,1,0:T(8,128)(2,1)}, bf16[4,64,384]{2,1,0:T(8,128)(2,1)}, u32[]{:S(2)}, u32[]{:S(2)}) collective-permute-start(bf16[4,64,384]{2,1,0:T(8,128)(2,1)} %get-tuple-element.215), channel_id=1, source_target_pairs={{0,24},{1,25},{2,26},{3,27},{4,28},{5,29},{6,30},{7,31},{8,0},{9,1... | collective-permute-start | bytes 589832 | tf_op jit(solution)/shard_map/ppermute | solution.py:49
  253.9 13.6 %collective-permute-start.35 = (bf16[96,768]{1,0:T(8,128)(2,1)S(1)}, bf16[96,768]{1,0:T(8,128)(2,1)S(1)}, u32[]{:S(2)}, u32[]{:S(2)}) collective-permute-start(bf16[96,768]{1,0:T(8,128)(2,1)S(1)} %slice.338), channel_id=1, source_target_pairs={{0,1},{1,0},{2,3},{3,2},{4,5},{5,4},{6,7},{7,6},{8,9},{9,8},{10,11... | collective-permute-start | bytes 442376 | tf_op jit(solution)/shard_map/ppermute | solution.py:49
  254.0 11.4 %copy-start.25 = (f32[768,768]{1,0:T(8,128)S(1)}, f32[768,768]{1,0:T(8,128)}, u32[]{:S(2)}) copy-start(f32[768,768]{1,0:T(8,128)} %get-tuple-element.172) | copy-start | bytes 7077892
  254.0 11.4 %copy-start.30 = (f32[768,768]{1,0:T(8,128)S(1)}, f32[768,768]{1,0:T(8,128)}, u32[]{:S(2)}) copy-start(f32[768,768]{1,0:T(8,128)} %get-tuple-element.173) | copy-start | bytes 7077892
  265.3 3.9 %collective-permute-start.34 = (bf16[4,64,384]{2,1,0:T(8,128)(2,1)S(1)}, bf16[4,64,384]{2,1,0:T(8,128)(2,1)S(1)}, u32[]{:S(2)}, u32[]{:S(2)}) collective-permute-start(bf16[4,64,384]{2,1,0:T(8,128)(2,1)S(1)} %get-tuple-element.194), channel_id=1, source_target_pairs={{0,1},{1,0},{2,3},{3,2},{4,5},{5,4},{6,7},{7,6},{8,9},{9,8},{10,11... | collective-permute-start | bytes 589832 | tf_op jit(solution)/shard_map/ppermute | solution.py:49
  (23 other events, 83.5 us)
Sparse Core Ops, SparseCore 0:
  11.0 93.1 all-gather.2

commit v2 on v1

--- a/solution.py
+++ b/solution.py
@@ -112,8 +112,12 @@
     def column(self, own):
         return total_of(*self.exchange(own))
 
-    def column_near(self, own):
-        return total_of(own[0], *(self.shift(own[k], "z", k) for k in range(1, self.z)))
+    def column_near(self, own, vectors, first=()):
+        size = own.shape[1] * own.shape[2]
+        rows = jnp.concatenate([own.reshape(self.z, size, own.shape[3])] + [vectors], axis=1)
+        got = behind([self.shift(rows[k], "z", k) for k in range(1, self.z)], first)
+        total = total_of(own[0], *(v[:size].reshape(own.shape[1:]) for v in got))
+        return total, total_of(vectors[0], *(v[size:] for v in got))
 
     def groups(self, axes):
         names = ("z", "x", "q", "c")
@@ -319,7 +323,7 @@
     rows, width = queries.shape[0], pairs * 128
     total_keys = keys.shape[0]
     pairs = width // 128
-    block = 256 if rows % 256 == 0 else rows
+    block = rows
     cost = SMALL
     return pl.pallas_call(
         attn_fwd_kernel,
@@ -341,39 +345,29 @@
             jax.ShapeDtypeStruct((rows, width), bf16),
             jax.ShapeDtypeStruct((pairs, 2, rows), f32),
         ],
-        compiler_params=pltpu.CompilerParams(vmem_limit_bytes=16 * 2**20),
+        compiler_params=pltpu.CompilerParams(vmem_limit_bytes=32 * 2**20),
         cost_estimate=cost,
         name="attn_fwd",
     )(queries, keys, values, hot, pen)
 
 
 def attn_bwd_kernel(
-    q_ref, k_ref, v_ref, hot_ref, pen_ref, o_ref, do_ref, lse_ref, dq_ref, dk_ref, dv_ref, dk_acc, dv_acc
+    q_ref, k_ref, v_ref, hot_ref, pen_ref, o_ref, do_ref, lse_ref, dq_ref, dk_ref, dv_ref
 ):
     total_keys = k_ref.shape[0]
     chunk = chunk_of(total_keys)
     steps = total_keys // chunk
-    at, last = pl.program_id(1), pl.num_programs(1) - 1
     query, hot, grad = q_ref[...], hot_ref[...], do_ref[...]
-
-    @pl.when(at == 0)
-    def _():
-        dk_acc[...] = jnp.zeros_like(dk_acc)
-        dv_acc[...] = jnp.zeros_like(dv_acc)
-
     flipped = (grad.astype(f32) * o_ref[...]).T
     zero = jnp.zeros_like(query)
 
     def step(rows):
         keys, values, pen = k_ref[rows, :], v_ref[rows, :], pen_ref[rows, :]
-        dq = None
-        dk = dk_acc[rows, :]
-        dv = dv_acc[rows, :]
+        dq, dk, dv = [], 0.0, 0.0
         for head in range(2):
             sel = first_lanes(head)
-            delta = jnp.sum(
-                flipped[head * HEAD_DIM : (head + 1) * HEAD_DIM], axis=0, keepdims=True
-            )
+            lanes = slice(head * HEAD_DIM, (head + 1) * HEAD_DIM)
+            delta = jnp.sum(flipped[lanes], axis=0, keepdims=True)
             k_aug = jnp.where(sel, keys, pen)
             s = mm(k_aug, jnp.where(sel, query, hot), ((1,), (1,)))
             p = jnp.exp2(s - lse_ref[0, head : head + 1, :])
@@ -382,12 +376,10 @@
             ds = (p * (dp - delta)).astype(bf16)
             dv = dv + mm(p.astype(bf16), grad_h)
             dk = dk + mm(ds, jnp.where(sel, query, zero))
-            part = mm(keys, ds, ((0,), (0,)))
-            part = part[head * HEAD_DIM : (head + 1) * HEAD_DIM]
-            dq = part if dq is None else jnp.concatenate([dq, part], axis=0)
-        dk_acc[rows, :] = dk
-        dv_acc[rows, :] = dv
-        return dq
+            dq.append(mm(keys, ds, ((0,), (0,)))[lanes])
+        dk_ref[rows, :] = (dk * (1.0 / LOG2E)).astype(bf16)
+        dv_ref[rows, :] = dv.astype(bf16)
+        return jnp.concatenate(dq, axis=0)
 
     if steps == 1:
         dq = step(slice(0, chunk))
@@ -400,18 +392,12 @@
         )
     dq_ref[...] = (dq.T * HEAD_DIM**-0.5).astype(bf16)
 
-    @pl.when(at == last)
-    def _():
-        dk_ref[...] = (dk_acc[...] * (1.0 / LOG2E)).astype(bf16)
-        dv_ref[...] = dv_acc[...].astype(bf16)
-
 
 def attn_bwd(queries, keys, values, hot, pen, attended, d_attended, lse, start, pairs):
     rows = queries.shape[0]
     total_keys = keys.shape[0]
-    block = 256 if rows % 256 == 0 else rows
+    block = rows
     by_query = pl.BlockSpec((block, 128), lambda p, i: (i, p + start))
-    own = pl.BlockSpec((block, 128), lambda p, i: (i, p))
     by_key = pl.BlockSpec((total_keys, 128), lambda p, i: (0, p + start))
     to_query = pl.BlockSpec((block, 128), lambda p, i: (i, p))
     to_key = pl.BlockSpec((total_keys, 128), lambda p, i: (0, p))
@@ -426,9 +412,9 @@
             by_key,
             pl.BlockSpec((block, 128), lambda p, i: (i, 0)),
             pl.BlockSpec((total_keys, 128), lambda p, i: (0, 0)),
-            own,
             by_query,
-            pl.BlockSpec((1, 2, block), lambda p, i: (p, 0, i)),
+            by_query,
+            pl.BlockSpec((1, 2, block), lambda p, i: (p + start, 0, i)),
         ],
         out_specs=[to_query, to_key, to_key],
         out_shape=[
@@ -436,8 +422,7 @@
             jax.ShapeDtypeStruct((total_keys, width), bf16),
             jax.ShapeDtypeStruct((total_keys, width), bf16),
         ],
-        scratch_shapes=[pltpu.VMEM((total_keys, 128), f32), pltpu.VMEM((total_keys, 128), f32)],
-        compiler_params=pltpu.CompilerParams(vmem_limit_bytes=24 * 2**20),
+        compiler_params=pltpu.CompilerParams(vmem_limit_bytes=40 * 2**20),
         cost_estimate=cost,
         name="attn_bwd",
     )(queries, keys, values, hot, pen, attended, d_attended, lse)
@@ -659,34 +644,13 @@
         ref[column, z, slot, 0:shard, :] = value[i * shard : (i + 1) * shard]
 
 
-def vector_rows(chips, sums1, sums2, ups):
-    width = sums1.shape[1]
-    narrow, wide = width // chips, 2 * width // chips
-    plain = jnp.concatenate([sums1[0:2], sums2[0:4], sums1[0:2]], axis=0)
-
-    def fold(value, n, chip):
-        lane = lax.broadcasted_iota(jnp.int32, (chips, 8, width), 2)
-        value = jnp.where(lane // n == chip, value, 0.0).reshape(chips * 8, width)
-        m = lax.broadcasted_iota(jnp.int32, (width, 128), 1)
-        j = lax.broadcasted_iota(jnp.int32, (width, 128), 0)
-        return mm(value.astype(bf16), (j % n == m).astype(bf16)).reshape(chips, 8, 128)
-
-    chip = lax.broadcasted_iota(jnp.int32, (chips, 8, width), 0)
-    a = fold(jnp.broadcast_to(plain[None], (chips, 8, width)), narrow, chip)
-    low = jnp.concatenate([sums1[2:3], ups[0:1]] * 4, axis=0)
-    high = jnp.concatenate([sums1[3:4], ups[1:2]] * 4, axis=0)
-    both = jnp.where(chip < chips // 2, low[None], high[None])
-    b = fold(both, wide, chip % (chips // 2))
-    row = lax.broadcasted_iota(jnp.int32, (chips, 8, 128), 1)
-    return jnp.where(row < 6, a, b).astype(bf16)
-
-
-def matrix_grads_kernel(grid, fast, n, place, h1t_ref, d_ref, *refs):
+def matrix_grads_kernel(grid, fast, n, parts, place, h1t_ref, d_ref, *refs):
     g_ref = refs[-1]
-    mine, other, flat, more = refs[:n], refs[n : 2 * n], refs[2 * n : 5 * n], refs[5 * n : -1]
+    mine, other, refs = refs[:n], refs[n : 2 * n], refs[2 * n : -1]
+    flat = refs
     shard = h1t_ref.shape[0] // grid.chips
     slot = 0
-    for part in range(n):
+    for part in range(parts):
         dq_ref, dk_ref, dv_ref = flat[3 * part : 3 * part + 3]
         chip_rows = dq_ref.shape[0]
         for p in range(dq_ref.shape[1] // 128):
@@ -703,32 +667,27 @@
     g = mm(jnp.concatenate([a, b], axis=1), d_ref[...], ((0,), (0,))).astype(bf16)
     if fast:
         store_rows(grid, place, g_ref, g, shard, slot)
-        rows = vector_rows(grid.chips, *(r[...] for r in more))
-        rows = jnp.concatenate([rows, jnp.zeros_like(rows)], axis=1)
-        for i in range(grid.chips):
-            column, z = grid.relative(place, i, True)
-            g_ref[column, z, 0, pl.ds(shard, 16), 0:128] = rows[i]
     else:
         g_ref[slot] = g
 
 
-def matrix_gradients(grid, fast, h1t, branch, mine, other, grads, more):
+def matrix_gradients(grid, fast, h1t, branch, mine, other, grads):
     width = h1t.shape[0]
     rows, half = branch.shape[0], branch.shape[1] // 2
     slots = half // 128 + 1
     if fast:
-        shape = (2 * grid.q, grid.z, slots, width // grid.chips + 16, half)
+        shape = (2 * grid.q, grid.z, slots, width // grid.chips, half)
     else:
         shape = (slots, width, half)
     flat = [v for part in grads for v in part]
     whole = lambda v: pl.BlockSpec(v.shape, lambda i, s: (0, 0))
     return call(
-        functools.partial(matrix_grads_kernel, grid, fast, len(mine)),
+        functools.partial(matrix_grads_kernel, grid, fast, len(mine), len(grads)),
         grid.place,
-        [hbm(h1t), branch] + mine + other + flat + more,
+        [hbm(h1t), branch] + mine + other + flat,
         grid=(1,),
         in_specs=[whole(h1t), pl.BlockSpec((rows, half), lambda i, s: (0, s[3]))]
-        + [whole(v) for v in mine + other + flat + more],
+        + [whole(v) for v in mine + other + flat],
         out_specs=pl.BlockSpec(shape, lambda i, s: (0,) * len(shape)),
         out_shape=pltpu.HBM(shape, bf16),
         cost_estimate=SMALL,
@@ -738,73 +697,74 @@
 
 
 def input_back_kernel(parts, place, *refs):
-    grads, (w_ref, n1_ref, mine_ref, other_ref, sums_ref) = refs[: 3 * parts], refs[3 * parts :]
-    step = pl.program_id(0)
+    grads, (w_ref, n1_ref, sums_ref, up_ref) = refs[: 3 * parts], refs[3 * parts : 3 * parts + 4]
+    mine_ref, other_ref, vec_ref = refs[3 * parts + 4 :]
+    step, last = pl.program_id(0), pl.num_programs(0) - 1
     dq, dk, dv = (
         jnp.concatenate([grads[3 * p + i][...] for p in range(parts)], axis=1) for i in range(3)
     )
     half = dq.shape[1]
-    width = n1_ref.shape[1]
-    dq = jnp.where(step < 2, dq, jnp.zeros_like(dq))
+    local, width = n1_ref.shape
+    local = local // 2
+    dq = jnp.where(step < 1, dq, jnp.zeros_like(dq))
     d = mm(jnp.concatenate([dq, dk, dv], axis=1), w_ref[...], ((1,), (1,)))
-    block, core = step // 2, step % 2
-
-    @pl.when(core == place[3])
-    def _():
-        mine_ref[block] = d
-
-    @pl.when(core != place[3])
-    def _():
-        other_ref[block] = d.astype(bf16)
-
+    to = pl.ds(pl.multiple_of(step * local, local), local)
+    a, b = halves(place, d[:local], d[local:])
+    mine_ref[to, :] = a
+    other_ref[to, :] = b.astype(bf16)
     none = jnp.zeros((1, half), f32)
+    first = place[3] == 0
 
     def spread(v):
         v = sum_rows(v.astype(f32))
-        first = place[3] == 0
         return jnp.concatenate([jnp.where(first, v, none), jnp.where(first, none, v)], axis=1)
 
-    rows = [sum_rows(d * n1_ref[...].astype(f32)), sum_rows(d), spread(dq), spread(dv)]
-    sums = jnp.concatenate(rows + [jnp.zeros((4, width), f32)], axis=0)
+    top = jnp.concatenate([sum_rows(d * n1_ref[...].astype(f32)), sum_rows(d)], axis=0)
+    low = jnp.concatenate([spread(dq), spread(dv)], axis=0)
 
     @pl.when(step == 0)
     def _():
-        sums_ref[...] = jnp.zeros_like(sums_ref)
-
-    sums_ref[...] += sums
-
-
-def input_back(grid, grads, w, n1, local):
+        up, no = up_ref[...], jnp.zeros_like(up_ref[...])
+        ups = [jnp.where(first, up, no), jnp.where(first, no, up), jnp.zeros((4, width), f32)]
+        vec_ref[...] = jnp.concatenate([top, sums_ref[0:4, :], low] + ups, axis=0)
+
+    @pl.when(step > 0)
+    def _():
+        vec_ref[0:2, :] += top
+        vec_ref[6:8, :] += low
+
+    @pl.when(step == last)
+    def _():
+        at = other_ref.shape[0] - 16
+        other_ref[at:, :] = vec_ref[...].astype(bf16)
+
+
+def input_back(grid, grads, w, n1, sums, ups, local):
     rows, width = n1.shape
     flat = [g for part in grads for g in part]
     specs = []
     for dq, dk, dv in grads:
         n = dq.shape[1]
-        specs.append(pl.BlockSpec((local, n), lambda i, s: (jnp.minimum(i, 1), 0)))
-        specs += [pl.BlockSpec((local, n), lambda i, s: (i, 0))] * 2
-    shape = (grid.q, local, width)
+        specs.append(pl.BlockSpec((2 * local, n), lambda i, s: (0, 0)))
+        specs += [pl.BlockSpec((2 * local, n), lambda i, s: (i, 0))] * 2
+    whole = lambda shape: pl.BlockSpec(shape, lambda i, s: (0, 0))
+    mine, other, vec = (grid.q * local, width), (grid.q * local + 16, width), (16, width)
     return call(
         functools.partial(input_back_kernel, len(grads)),
         grid.place,
-        flat + [hbm(w), hbm(n1)],
-        grid=(rows // local,),
+        flat + [hbm(w), hbm(n1), sums, ups],
+        grid=(grid.q,),
         in_specs=specs
-        + [
-            pl.BlockSpec(w.shape, lambda i, s: (0, 0)),
-            pl.BlockSpec((local, width), lambda i, s: (i, 0)),
-        ],
-        out_specs=[
-            pl.BlockSpec(shape, lambda i, s: (0, 0, 0)),
-            pl.BlockSpec(shape, lambda i, s: (0, 0, 0)),
-            pl.BlockSpec((8, width), lambda i, s: (0, 0)),
-        ],
+        + [whole(w.shape), pl.BlockSpec((2 * local, width), lambda i, s: (i, 0))]
+        + [whole(sums.shape), whole(ups.shape)],
+        out_specs=[whole(mine), whole(other), whole(vec)],
         out_shape=[
-            pltpu.HBM(shape, f32),
-            jax.ShapeDtypeStruct(shape, bf16),
-            jax.ShapeDtypeStruct((8, width), f32),
+            pltpu.HBM(mine, f32),
+            jax.ShapeDtypeStruct(other, bf16),
+            jax.ShapeDtypeStruct(vec, f32),
         ],
         cost_estimate=SMALL,
-        mib=24,
+        mib=30,
         name="input_back",
     )
 
@@ -813,7 +773,7 @@
     mine_ref, got_ref = refs[:2]
     sides = refs[2 : 2 + n_got]
     n1_ref, rstd_ref, after_ref, vec_ref, out_ref = refs[2 + n_got :]
-    d = mine_ref[0] + got_ref[0].astype(f32)
+    d = mine_ref[...] + got_ref[...].astype(f32)
     for s in sides:
         d = d + s[...].astype(f32)
     out_ref[...] = after_ref[...] + norm_back(
@@ -822,8 +782,8 @@
 
 
 def finish(grid, mine, got, sides, n1, rstd1, d_after, vec):
-    _, rows, width = mine.shape
-    first = pl.BlockSpec((1, rows, width), lambda i, s: (0, 0, 0))
+    rows, width = n1.shape[0] // 2 // grid.q, n1.shape[1]
+    first = pl.BlockSpec((rows, width), lambda i, s: (0, 0))
     own = lambda n: pl.BlockSpec((rows, n), lambda i, s: (s[3], 0))
     return call(
         functools.partial(finish_kernel, len(sides)),
@@ -906,10 +866,10 @@
         up_shard = width // grid.chips
         half = grid.chips // 2
         for i in range(half):
-            column, z = grid.relative(place, step * half + i)
+            column, z = grid.relative(place, step * half + i, True)
             g_ref[column, z, 0:down_shard, :] = gdown[i * down_shard : (i + 1) * down_shard]
         for i in range(grid.chips):
-            column, z = grid.relative(place, i)
+            column, z = grid.relative(place, i, True)
             to = pl.multiple_of(down_shard + step * up_shard, 16)
             g_ref[column, z, pl.ds(to, up_shard), :] = gup[i * up_shard : (i + 1) * up_shard]
     else:
@@ -1018,7 +978,9 @@
     )
 
 
-def last_rest_kernel(shard, place, own_ref, other_ref, qkv_ref, out_ref, six_ref, qv_ref, up_ref):
+def last_rest_kernel(
+    grid, shard, place, own_ref, other_ref, vec_ref, qkv_ref, out_ref, six_ref, qv_ref, up_ref
+):
     pairs, half = own_ref.shape[0] - 1, own_ref.shape[2]
     for p in range(pairs + 1):
         both = mine_and_other(place, own_ref, other_ref, p, 0, shard)
@@ -1029,25 +991,47 @@
             for t in range(3):
                 to = 2 * half * t + half * core + 128 * p
                 qkv_ref[:, to : to + 128] = value[:, 128 * t : 128 * (t + 1)]
-    mine = own_ref[0, 2 * shard : 2 * shard + 8, 0:128]
-    total = mine + other_ref[0, 2 * shard : 2 * shard + 8, 0:128].astype(f32)
+    width = 2 * half
+    vec = jnp.concatenate([vec_ref[0:16, :], vec_ref[16:32, :]], axis=1)
+    chip = (place[0] * grid.x + place[1]) * grid.q + place[2]
+
+    def cut(rows, start):
+        lane = lax.broadcasted_iota(jnp.int32, (width, 128), 0)
+        to = lax.broadcasted_iota(jnp.int32, (width, 128), 1)
+        take = (lane == to + start).astype(f32)
+        return lax.dot_general(
+            rows,
+            take,
+            (((1,), (0,)), ((), ())),
+            precision=lax.Precision.HIGHEST,
+            preferred_element_type=f32,
+        )
+
+    me = chip * 2 + place[3]
+    six_ref[...] = cut(vec[0:8], me * shard)[:, :shard]
+
+    def long(low, high, start, ref):
+        n = ref.shape[1]
+        rows = jnp.where(start >= width, high, low)
+        start = jnp.where(start >= width, start - width, start)
+        ref[...] = cut(jnp.broadcast_to(rows, (8, width)), start)[0:1, :n]
+
+    long(vec[6:7], vec[7:8], me * 2 * shard, qv_ref)
     first = place[3] == 0
-    six_ref[...] = jnp.where(first, total[:, :shard], total[:, shard : 2 * shard])
-    n = 2 * shard
-    qv_ref[...] = jnp.where(first, total[6:7, :n], total[6:7, n : 2 * n])
-    up_ref[...] = mine[7:8, : up_ref.shape[1]]
-
-
-def last_rest(grid, own, other, shard, per_chip):
+    low, high = jnp.where(first, vec[8:9], vec[10:11]), jnp.where(first, vec[9:10], vec[11:12])
+    long(low, high, chip * up_ref.shape[1], up_ref)
+
+
+def last_rest(grid, own, other, vec, shard, per_chip):
     half = own.shape[2]
     whole = lambda shape: pl.BlockSpec(shape, lambda i, s: (0,) * len(shape))
     shapes = [(shard, 6 * half), (shard, 2 * half), (8, shard), (1, 2 * shard), (1, per_chip)]
     return call(
-        functools.partial(last_rest_kernel, shard),
+        functools.partial(last_rest_kernel, grid, shard),
         grid.place,
-        [own, other],
+        [own, other, vec],
         grid=(1,),
-        in_specs=[whole(own.shape), whole(other.shape)],
+        in_specs=[whole(own.shape), whole(other.shape), whole(vec.shape)],
         out_specs=[whole(s) for s in shapes],
         out_shape=[jax.ShapeDtypeStruct(s, f32) for s in shapes],
         cost_estimate=SMALL,
@@ -1173,52 +1157,52 @@
         grid, token_rows, vec, qkv_weights, local
     )
     pairs = half // 128
-    forward = lambda q, a, n: attn_fwd(q, keys, values, hot, pen, a, n)
     if fast:
-        up_line = behind(up_line, [f[0] for f in found])
+        queries, up_line = lock(queries, up_line)
         up_over, up_sides = grid.shift(up_line, "x", 1), grid.along(up_line, "q")
-    parts = [forward(queries, 0, 1)]
+    attended, att, lse = attn_fwd(queries, keys, values, hot, pen, 0, pairs)
     if fast:
-        up_over, up_sides = behind((up_over, up_sides), parts[0])
-        queries = behind(queries, up_over, up_sides)
+        up_over, up_sides = behind((up_over, up_sides), att)
         corners = grid.corner_pieces(up_over, up_sides)
-        found = grid.found(up_line, up_over, up_sides, corners, True)
-        ups = Pieces(grid, found)
-    parts.append(forward(queries, 1, pairs - 1))
-    att_mine = [p[1] for p in parts]
-    if fast:
-        att_mine[1] = behind(att_mine[1], corners)
-    att_other = [swap(v) for v in att_mine]
+        ups = Pieces(grid, grid.found(up_line, up_over, up_sides, corners, True))
+    att_mine, att_other = [att], [swap(att)]
     out_rows = full_out.reshape(2, half, width)
     after, h2, n2, rstd2 = project_out(grid, token_rows, att_mine, att_other, out_rows, vec)
 
     *g_ff, gbias, ff_out, dh, dh_b = feed_forward(grid, h2, dy, ups, downs, vec, units)
     d_after, d_branch, d_att, sums2 = out_back(grid, dh, swap(dh_b), dy, n2, rstd2, vec, out_rows)
 
-    def back(d, i):
-        att, _, lse = parts[i]
-        start = i
-        return attn_bwd(queries, keys, values, hot, pen, att, d, lse, start, att.shape[1] // 128)
+    def back(d, a, n):
+        return attn_bwd(queries, keys, values, hot, pen, attended, d, lse, a, n)
 
     by_core = lambda v: v.reshape(2, local, width)
     up_sums = gbias.reshape(2, width)
-    grads = [back(d_att, 0)]
+    grads = [back(d_att, 0, 1)]
     if fast:
         ff_over, ff_sides = grid.corners(g_ff[0], grads[0])
         d_att = behind(d_att, ff_over, ff_sides)
-    grads.append(back(d_att, 1))
-    d_mine, d_other, sums1 = input_back(grid, grads, full_qkv, n1, local)
-    more = [sums1, sums2, up_sums] if fast else []
-    g_all = matrix_gradients(grid, fast, h1t, d_branch, att_mine, att_other, grads, more)
+    grads.append(back(d_att, 1, pairs - 1))
+    g_all = matrix_gradients(grid, fast, h1t, d_branch, att_mine, att_other, grads)
     if fast:
         ff_own = grid.edges(g_ff[0], ff_over, ff_sides, g_all)
-        g_all, ff_own, d_other = lock(g_all, ff_own, d_other)
-        ff = grid.column(ff_own)
+        grads, g_all, ff_own = lock(grads, g_all, ff_own)
+        ff_z = [grid.shift(ff_own[k], "z", k) for k in range(1, grid.z)]
+    else:
+        grads, g_all = lock(grads, g_all)
+    d_mine, d_other, sums = input_back(grid, grads, full_qkv, n1, sums2, up_sums, local)
+    if fast:
+        over, sides = grid.corners(g_all, d_other)
+        middle = grid.z // 2 - 1
+        ends = ff_z[:middle] + ff_z[middle + 1 :]
+        d_other, over, sides, ends = lock(d_other, over, sides, ends)
     d_got = swap(d_other)
     sent = [
-        (d_mine[k] + d_got[k].astype(f32)).astype(bf16) for k in range(1, grid.q)
+        total_of(*(v[k * local : (k + 1) * local] for v in (d_mine, d_got))).astype(bf16)
+        for k in range(1, grid.q)
     ]
     got = [grid.shift(s, "q", grid.q - k) for k, s in enumerate(sent, 1)]
+    if fast:
+        vectors = sums + d_got[grid.q * local :].astype(f32)
     ff_out = behind(ff_out, sent)
     out_got = swap(not_core(by_core(ff_out)).astype(bf16)).astype(f32)
     result = at_core(by_core(ff_out)) + out_got + at_core(by_core(after)) + vec[5:6]
@@ -1226,12 +1210,17 @@
     input_grad = finish(grid, d_mine, d_got, got, n1, rstd1, d_after, vec)[None]
 
     if fast:
-        over, sides = grid.corners(g_all, got)
-        own = grid.column_near(grid.edges(g_all, over, sides))
-        ff = behind(ff, sides)
+        own = grid.edges(g_all, over, sides, (vectors, sent))
+        ff = total_of(ff_own[0], behind(ff_z[middle], own), *ends)
+        vectors = jnp.concatenate([vectors[:, :half], vectors[:, half:]]).astype(bf16)
+        own, vectors = lock(own, vectors)
+        vectors = jnp.broadcast_to(vectors, (grid.z,) + vectors.shape)
         w_up_g, w_down_g = last_ff(grid, ff, swap(ff[per_chip:].astype(bf16)), shard)
+        own, vectors = grid.column_near(own, vectors, (output, w_up_g))
+        vectors = vectors + behind(grid.shift(vectors, "x", 1), input_grad)
+        vectors = vectors + sum(grid.along(vectors, "q"))
         w_qkv_g, w_out_g, six, qv_g, up_g = last_rest(
-            grid, own, swap(own.astype(bf16)), shard, per_chip
+            grid, own, swap(own.astype(bf16)), vectors, shard, per_chip
         )
         qv_g, up_g = qv_g[0], up_g[0]
     else:
@@ -1251,16 +1240,6 @@
         per_pair = g_all[:pairs].reshape(pairs, width, 3, 128)
         per_pair = jnp.transpose(per_pair, (1, 2, 0, 3)).reshape(width, 3, half)
         w_qkv_g = reduce(spread(per_pair, 2).reshape(width, 6 * half))
-        nothing = jnp.zeros_like(up_sums)
-        sums = jnp.concatenate(
-            [
-                sums1[0:2],
-                sums2[0:4],
-                sums1[2:4],
-                jnp.where(first, up_sums, nothing),
-                jnp.where(first, nothing, up_sums),
-            ]
-        )
         sums = lax.psum(sums, AXES)
         me = (lax.axis_index("dp") * blk) + lax.axis_index("blk")
         six = lax.dynamic_slice(sums, (0, me * shard), (6, shard))

time: 281 us -> 263 us (0.936)
  Pallas kernels: 110 us -> 98 us
  waiting for transfers between devices: 72.4 us -> 61.7 us
  starting transfers between devices: 42.9 us -> 50.7 us
  other arithmetic: 20.2 us -> 12.5 us
    ppermute x36 -> x40, starting transfers between devices: 31.4 us -> 43.4 us  [shift(): return lax.ppermute(value, AXES, pairs)]
    pallas_call x2 -> x1, Pallas kernels: 20.9 us -> 11.6 us  [attn_fwd(): pl.pallas_call(attn_fwd_kernel, grid=(pairs, rows // block), in_specs=[pl...]
    unnamed x99 -> x91, local copies, waits for them, and re-layouts: 1.62 us -> 7.68 us
    all_to_all x2 -> x1, waiting for transfers between devices: 5.54 us -> 0.01 us  [exchange(): lax.all_to_all(blocks, AXES, 0, 0, axis_index_groups=self.groups(('z',)),...]
    ppermute x36 -> x40, waiting for transfers between devices: 66.8 us -> 61.6 us  [shift(): return lax.ppermute(value, AXES, pairs)]
    all_to_all x2 -> x1, starting transfers between devices: 11.4 us -> 7.28 us  [exchange(): lax.all_to_all(blocks, AXES, 0, 0, axis_index_groups=self.groups(('z',)),...]
  transfers between devices with their start and end apart: 39 -> 42, of which waited for: 17 -> 19; matrix products, arithmetic and copies ran while one was open for 12% -> 8% of each run, Pallas kernels for 30% -> 29%
where the time goes in v2:
time: 263 us; the launch traced here: 258 us
  Pallas kernels  98 us (37%)
  waiting for transfers between devices  61.7 us (23%)
  starting transfers between devices  50.7 us (19%)
  local copies, waits for them, and re-layouts  19.7 us (7%)
  between operations  15.2 us (6%)
  other arithmetic  12.5 us (5%)
    pallas_call x11, Pallas kernels, call(): pl.pallas_call(kernel, grid_spec=spec, compiler_params=pltpu.CompilerPara...  67.1 us
    ppermute x40, waiting for transfers between devices, shift(): return lax.ppermute(value, AXES, pairs)  61.6 us
    ppermute x40, starting transfers between devices, shift(): return lax.ppermute(value, AXES, pairs)  43.4 us
    pallas_call x2, Pallas kernels, attn_bwd(): pl.pallas_call(attn_bwd_kernel, grid=(pairs, rows // block), in_specs=[by...  19.3 us
    pallas_call x1, Pallas kernels, attn_fwd(): pl.pallas_call(attn_fwd_kernel, grid=(pairs, rows // block), in_specs=[pl...  11.6 us
    unnamed x91, local copies, waits for them, and re-layouts  7.68 us
    all_to_all x1, starting transfers between devices, exchange(): lax.all_to_all(blocks, AXES, 0, 0, axis_index_groups=self.groups(('z',)),...  7.28 us
  transfers between devices with their start and end apart: 42, of which 19 were waited for; matrix products, arithmetic and copies ran while one was open for 8% of the time, Pallas kernels for 29%

profile of v2, /device:TPU:0, one launch (start us, length us, event | category | flops | bytes accessed | tf_op | source)
XLA Modules:
  0.0 257.8 jit_solution(3167009203195626406)
XLA Ops:
  7.3 1.7 pad_maximum_fusion.7
  9.0 1.2 reshape.216
  10.3 1.3 dynamic-slice_reduce_fusion.1
  14.1 0.9 collective-permute-done
  15.1 2.7 %collective-permute-start.4 = (bf16[400,768]{1,0:T(8,128)(2,1)S(1)}, bf16[400,768]{1,0:T(8,128)(2,1)S(1)}, u32[]{:S(2)}, u32[]{:S(2)}) collective-permute-start(bf16[400,768]{1,0:T(8,128)(2,1)S(1)} %fusion.11), channel_id=1, source_target_pairs={{0,2},{1,3},{2,0},{3,1},{4,6},{5,7},{6,4},{7,5},{8,10},{9,11},{10,... | collective-permute-start | bytes 1843208 | tf_op jit(solution)/shard_map/ppermute | solution.py:49
  17.9 1.6 collective-permute-start.1
  19.6 2.6 %collective-permute-start.2 = (bf16[64,1152]{1,0:T(8,128)(2,1)S(1)}, bf16[64,1152]{1,0:T(8,128)(2,1)S(1)}, u32[]{:S(2)}, u32[]{:S(2)}) collective-permute-start(bf16[64,1152]{1,0:T(8,128)(2,1)S(1)} %fusion.21), channel_id=1, source_target_pairs={{0,16},{1,17},{2,18},{3,19},{4,20},{5,21},{6,22},{7,23},{8,24},{9,... | collective-permute-start | bytes 442376 | tf_op jit(solution)/shard_map/ppermute | solution.py:49
  22.2 1.3 collective-permute-start.3
  23.5 3.0 %collective-permute-done.1 = bf16[64,1152]{1,0:T(8,128)(2,1)S(1)} collective-permute-done((bf16[64,1152]{1,0:T(8,128)(2,1)S(1)}, bf16[64,1152]{1,0:T(8,128)(2,1)S(1)}, u32[]{:S(2)}, u32[]{:S(2)}) %collective-permute-start.1) | collective-permute-done | bytes 147488 | tf_op jit(solution)/shard_map/ppermute | solution.py:49
  26.5 8.5 %collective-permute-done.2 = bf16[64,1152]{1,0:T(8,128)(2,1)S(1)} collective-permute-done((bf16[64,1152]{1,0:T(8,128)(2,1)S(1)}, bf16[64,1152]{1,0:T(8,128)(2,1)S(1)}, u32[]{:S(2)}, u32[]{:S(2)}) %collective-permute-start.2) | collective-permute-done | bytes 147488 | tf_op jit(solution)/shard_map/ppermute | solution.py:49
  35.4 1.6 collective-permute-start.7
  38.6 7.3 %all-to-all-start = ((bf16[4,96,768]{2,1,0:T(8,128)(2,1)}), bf16[4,96,768]{2,1,0:T(8,128)(2,1)}, u32[]{:S(2)}, u32[]{:S(2)}) async-start(bf16[4,96,768]{2,1,0:T(8,128)(2,1)} %broadcast_in_dim.35), calls=%async_computation | async-start | bytes 1179648 | tf_op jit(solution)/shard_map/all_to_all | solution.py:137
  45.9 9.1 %collective-permute-done.7.refs_1_ = bf16[4,64,1152]{2,1,0:T(8,128)(2,1)S(1)} collective-permute-done((bf16[4,64,1152]{2,1,0:T(8,128)(2,1)S(1)}, bf16[4,64,1152]{2,1,0:T(8,128)(2,1)S(1)}, u32[]{:S(2)}, u32[]{:S(2)}) %collective-permute-start.7) | collective-permute-done | bytes 589856 | tf_op jit(solution)/shard_map/ppermute | solution.py:49
  55.8 1.6 select_bitcast_fusion
  57.6 1.0 copy-done.22
  58.6 1.0 slice.269
  59.6 2.5 collective-permute-start.12
  63.4 3.0 %collective-permute-done.11.refs_3_ = bf16[2,64,1152]{2,1,0:T(8,128)(2,1)S(1)} collective-permute-done((bf16[2,64,1152]{2,1,0:T(8,128)(2,1)S(1)}, bf16[2,64,1152]{2,1,0:T(8,128)(2,1)S(1)}, u32[]{:S(2)}, u32[]{:S(2)}) %collective-permute-start.11) | collective-permute-done | bytes 294944 | tf_op jit(solution)/shard_map/ppermute | solution.py:49
  66.4 1.9 collective-permute-done.12.refs_4_
  69.7 0.9 vectors.1.vec_ref.refs_6_
  71.3 9.7 %qkv.1 = (bf16[768,384]{1,0:T(8,128)(2,1)S(1)}, bf16[1536,384]{1,0:T(8,128)(2,1)S(1)}, bf16[1536,384]{1,0:T(8,128)(2,1)S(1)}, bf16[768,1536]{1,0:T(8,128)(2,1)},...) custom-call(s32[4]{0:T(128)S(1)} %pad_add_fusion.place, ...), custom_call_target="tpu_custom_call" | custom-call | flops 1000 | bytes 1000 | tf_op jit(solution)/shard_map/qkv/pallas_call | solution.py:171
  81.0 1.0 copy-done
  82.8 1.6 collective-permute-start.14
  84.4 1.8 collective-permute-start.15
  86.3 0.9 select_convert_fusion.pen_ref
  87.2 1.5 copy-done.1
  88.7 1.1 copy-done.7
  89.8 0.9 copy-done.11
  90.7 11.6 %attn_fwd.1 = (f32[768,384]{1,0:T(8,128)S(1)}, bf16[768,384]{1,0:T(8,128)(2,1)}, f32[3,2,768]{2,1,0:T(2,128)S(1)}) custom-call(bf16[768,384]{1,0:T(8,128)(2,1)S(1)} %copy-done.7, bf16[1536,384]{1,0:T(8,128)(2,1)S(1)} %get-tuple-element.142.k_ref, bf16[1536,384]{1,0:T(8,128)(2,1)S(1)} %copy-done.1, bf16[768,128]{1,0:T(8,128)(2,1)S(1)} %copy-done.11, ...), custom_call_target="tpu_custom_call" | custom-call | flops 1000 | bytes 1000 | tf_op jit(solution)/shard_map/attn_fwd/pallas_call | solution.py:328
  104.5 1.3 select_bitcast_fusion.5
  105.8 1.2 pad_maximum_fusion.1
  107.1 1.4 slice.333
  108.5 5.8 %out_proj.1 = (f32[768,768]{1,0:T(8,128)}, bf16[768,768]{1,0:T(8,128)(2,1)}, bf16[768,768]{1,0:T(8,128)(2,1)}, f32[768,128]{1,0:T(8,128)}) custom-call(s32[4]{0:T(128)S(1)} %pad_add_fusion.place, bf16[1536,768]{1,0:T(8,128)(2,1)S(1)} %pad_maximum_fusion.x_ref, bf16[2,384,768]{2,1,0:T(8,128)(2,1)S(1)} %bitcast.159, f32[16,768]{1,0:T(8,128)S(1)} %copy-done.14, ...), custom_call_target="tpu_custom_call" | custom-call | flops 1000 | bytes 1000 | tf_op jit(solution)/shard_map/out_proj/pallas_call | solution.py:171
  114.2 20.8 %feed_forward.1 = (bf16[4,4,192,768]{3,2,1,0:T(8,128)(2,1)}, f32[2,1,768]{2,1,0:T(1,128)S(1)}, f32[768,768]{1,0:T(8,128)}, f32[768,768]{1,0:T(8,128)S(1)}, bf16[768,768]{1,0:T(8,128)(2,1)S(1)}) custom-call(s32[4]{0:T(128)S(1)} %pad_add_fusion.place, bf16[768,768]{1,0:T(8,128)(2,1)} %get-tuple-element.145.h2_ref, bf16[768,768]{1,0:T(8,128)(2,1)} %bitcast.163, ...), custom_call_target="tpu_custom_call" | custom-call | flops 1000 | bytes 1000 | tf_op jit(solution)/shard_map/feed_forward/pallas_call | solution.py:171
  135.2 1.9 slice_bitcast_fusion.1
  137.1 1.7 collective-permute-start.19
  138.8 1.9 collective-permute-start.20
  140.8 6.6 %out_back.1 = (f32[768,768]{1,0:T(8,128)}, bf16[768,768]{1,0:T(8,128)(2,1)S(1)}, bf16[768,384]{1,0:T(8,128)(2,1)S(1)}, f32[8,768]{1,0:T(8,128)S(1)}) custom-call(s32[4]{0:T(128)S(1)} %pad_add_fusion.place, f32[768,768]{1,0:T(8,128)S(1)} %get-tuple-element.152.mine_ref, bf16[768,768]{1,0:T(8,128)(2,1)S(1)} %collective-permute-done.18.got_ref, ...), custom_call_target="tpu_custom_call" | custom-call | flops 1000 | bytes 1000 | tf_op jit(solution)/shard_map/out_back/pallas_call | solution.py:171
  147.4 6.1 %attn_bwd.2 = (bf16[768,128]{1,0:T(8,128)(2,1)S(1)}, bf16[1536,128]{1,0:T(8,128)(2,1)S(1)}, bf16[1536,128]{1,0:T(8,128)(2,1)S(1)}) custom-call(bf16[768,384]{1,0:T(8,128)(2,1)S(1)} %copy-done.8, bf16[1536,384]{1,0:T(8,128)(2,1)S(1)} %get-tuple-element.142.k_ref, bf16[1536,384]{1,0:T(8,128)(2,1)S(1)} %copy-done.2, bf16[768,128]{1,0:T(8,128)(2,1)S(1)} %copy-done.12, ...), custom_call_target="tpu_custom_call" | custom-call | flops 1000 | bytes 1000 | tf_op jit(solution)/shard_map/attn_bwd/pallas_call | solution.py:406
  153.5 0.9 collective-permute-done.20
  155.4 1.8 collective-permute-start.21
  157.2 13.2 %attn_bwd.3 = (bf16[768,256]{1,0:T(8,128)(2,1)S(1)}, bf16[1536,256]{1,0:T(8,128)(2,1)S(1)}, bf16[1536,256]{1,0:T(8,128)(2,1)S(1)}) custom-call(bf16[768,384]{1,0:T(8,128)(2,1)S(1)} %copy-done.8, bf16[1536,384]{1,0:T(8,128)(2,1)S(1)} %get-tuple-element.142.k_ref, bf16[1536,384]{1,0:T(8,128)(2,1)S(1)} %copy-done.2, bf16[768,128]{1,0:T(8,128)(2,1)S(1)} %copy-done.12, ...), custom_call_target="tpu_custom_call" | custom-call | flops 1000 | bytes 1000 | tf_op jit(solution)/shard_map/attn_bwd/pallas_call | solution.py:406
  170.4 7.5 %matrix_grads.1 = bf16[4,4,4,48,384]{4,3,2,1,0:T(8,128)(2,1)} custom-call(s32[4]{0:T(128)S(1)} %pad_add_fusion.place, bf16[768,1536]{1,0:T(8,128)(2,1)} %get-tuple-element.168.h1t_ref, bf16[768,768]{1,0:T(8,128)(2,1)S(1)} %get-tuple-element.169.d_ref, bf16[768,384]{1,0:T(8,128)(2,1)} %get-tuple-element.144.refs_0_, ...), custom_call_target="tpu_custom_call" | custom-call | flops 1000 | bytes 1000 | tf_op jit(solution)/shard_map/matrix_grads/pallas_call | solution.py:171
  177.9 4.4 %collective-permute-done.22 = bf16[4,192,768]{2,1,0:T(8,128)(2,1)S(1)} collective-permute-done((bf16[4,192,768]{2,1,0:T(8,128)(2,1)S(1)}, bf16[4,192,768]{2,1,0:T(8,128)(2,1)S(1)}, u32[]{:S(2)}, u32[]{:S(2)}) %collective-permute-start.22) | collective-permute-done | bytes 1179680 | tf_op jit(solution)/shard_map/ppermute | solution.py:49
  183.3 1.6 collective-permute-start.23
  184.9 1.6 collective-permute-start.24
  186.6 5.1 %collective-permute-start.25 = (bf16[192,768]{1,0:T(8,128)(2,1)S(1)}, bf16[192,768]{1,0:T(8,128)(2,1)S(1)}, u32[]{:S(2)}, u32[]{:S(2)}) collective-permute-start(bf16[192,768]{1,0:T(8,128)(2,1)S(1)} %get-tuple-element.238), channel_id=1, source_target_pairs={{0,8},{1,9},{2,10},{3,11},{4,12},{5,13},{6,14},{7,15},{8,16},{9,17... | collective-permute-start | bytes 884744 | tf_op jit(solution)/shard_map/ppermute | solution.py:49
  191.7 1.4 collective-permute-start.26
  193.0 7.7 %input_back.1 = (f32[768,768]{1,0:T(8,128)}, bf16[784,768]{1,0:T(8,128)(2,1)S(1)}, f32[16,768]{1,0:T(8,128)S(1)}) custom-call(s32[4]{0:T(128)S(1)} %pad_add_fusion.place, bf16[768,128]{1,0:T(8,128)(2,1)S(1)} %get-tuple-element.172.refs_2_.refs_0_, bf16[1536,128]{1,0:T(8,128)(2,1)S(1)} %get-tuple-element.173.refs_3_.refs_1_, ...), custom_call_target="tpu_custom_call" | custom-call | flops 1000 | bytes 1000 | tf_op jit(solution)/shard_map/input_back/pallas_call | solution.py:171
  201.1 3.0 %collective-permute-done.26 = bf16[192,768]{1,0:T(8,128)(2,1)S(1)} collective-permute-done((bf16[192,768]{1,0:T(8,128)(2,1)S(1)}, bf16[192,768]{1,0:T(8,128)(2,1)S(1)}, u32[]{:S(2)}, u32[]{:S(2)}) %collective-permute-start.26) | collective-permute-done | bytes 294944 | tf_op jit(solution)/shard_map/ppermute | solution.py:49
  207.1 0.9 collective-permute-start.29
  208.1 11.7 %collective-permute-done.30 = bf16[4,4,48,384]{3,2,1,0:T(8,128)(2,1)S(1)} collective-permute-done((bf16[4,4,48,384]{3,2,1,0:T(8,128)(2,1)S(1)}, bf16[4,4,48,384]{3,2,1,0:T(8,128)(2,1)S(1)}, u32[]{:S(2)}, u32[]{:S(2)}) %collective-permute-start.30) | collective-permute-done | bytes 589856 | tf_op jit(solution)/shard_map/ppermute | solution.py:49
  219.8 1.0 collective-permute-done.31
  222.8 2.1 collective-permute-start.33
  224.8 1.8 collective-permute-start.34
  226.6 1.7 last_ff.1
  228.3 1.0 fusion.13
  229.3 2.7 %collective-permute-done.32 = bf16[224,384]{1,0:T(8,128)(2,1)S(1)} collective-permute-done((bf16[224,384]{1,0:T(8,128)(2,1)S(1)}, bf16[224,384]{1,0:T(8,128)(2,1)S(1)}, u32[]{:S(2)}, u32[]{:S(2)}) %collective-permute-start.32) | collective-permute-done | bytes 172064 | tf_op jit(solution)/shard_map/ppermute | solution.py:49
  231.9 6.4 %collective-permute-done.33 = bf16[224,384]{1,0:T(8,128)(2,1)S(1)} collective-permute-done((bf16[224,384]{1,0:T(8,128)(2,1)S(1)}, bf16[224,384]{1,0:T(8,128)(2,1)S(1)}, u32[]{:S(2)}, u32[]{:S(2)}) %collective-permute-start.33) | collective-permute-done | bytes 172064 | tf_op jit(solution)/shard_map/ppermute | solution.py:49
  238.6 1.5 collective-permute-start.38
  240.1 4.1 %finish.1 = f32[384,768]{1,0:T(8,128)} custom-call(s32[4]{0:T(128)S(1)} %pad_add_fusion.place, f32[768,768]{1,0:T(8,128)} %get-tuple-element.182.refs_0_, bf16[784,768]{1,0:T(8,128)(2,1)S(1)} %collective-permute-done.27.refs_1_, bf16[384,768]{1,0:T(8,128)(2,1)S(1)} %collective-permute-done.29.refs_2_, bf16[1536,768]{1,0:T(8,128)(2,1)} %get-tuple-element.179.refs_7_.refs_3_, ...), custom_call_target="tpu_custom_call" | custom-call | flops 1000 | bytes 1000 | tf_op jit(solution)/shard_map/finish/pallas_call | solution.py:171
  244.2 1.2 collective-permute-start.39
  245.5 2.9 %collective-permute-done.39 = f32[32,384]{1,0:T(8,128)S(1)} collective-permute-done((f32[32,384]{1,0:T(8,128)S(1)}, f32[32,384]{1,0:T(8,128)S(1)}, u32[]{:S(2)}, u32[]{:S(2)}) %collective-permute-start.39) | collective-permute-done | bytes 49184 | tf_op jit(solution)/shard_map/ppermute | solution.py:49
  248.4 1.8 last_rest.1
  (223 shorter events, 19.9 us)
Async XLA Ops:
  7.2 5.9 %copy-start.35 = (bf16[24]{0:T(256)(128)(2,1)S(1)}, bf16[24]{0:T(256)(128)(2,1)}, u32[]{:S(2)}) copy-start(bf16[24]{0:T(256)(128)(2,1)} %param.32) | copy-start | bytes 148
  7.2 6.0 %copy-start.36 = (bf16[24]{0:T(256)(128)(2,1)S(1)}, bf16[24]{0:T(256)(128)(2,1)}, u32[]{:S(2)}) copy-start(bf16[24]{0:T(256)(128)(2,1)} %param.28) | copy-start | bytes 148
  7.2 6.0 %copy-start.37 = (bf16[24]{0:T(256)(128)(2,1)S(1)}, bf16[24]{0:T(256)(128)(2,1)}, u32[]{:S(2)}) copy-start(bf16[24]{0:T(256)(128)(2,1)} %param.27) | copy-start | bytes 148
  7.2 6.1 %copy-start.38 = (bf16[24]{0:T(256)(128)(2,1)S(1)}, bf16[24]{0:T(256)(128)(2,1)}, u32[]{:S(2)}) copy-start(bf16[24]{0:T(256)(128)(2,1)} %param.26) | copy-start | bytes 148
  7.2 6.2 %copy-start.39 = (bf16[24]{0:T(256)(128)(2,1)S(1)}, bf16[24]{0:T(256)(128)(2,1)}, u32[]{:S(2)}) copy-start(bf16[24]{0:T(256)(128)(2,1)} %param.22) | copy-start | bytes 148
  7.3 6.3 %copy-start.40 = (bf16[24]{0:T(256)(128)(2,1)S(1)}, bf16[24]{0:T(256)(128)(2,1)}, u32[]{:S(2)}) copy-start(bf16[24]{0:T(256)(128)(2,1)} %param.21) | copy-start | bytes 148
  7.3 99.8 %all-gather.3.cloned.1.call-start = ((), (), s32[]{:S(2)}) async-start(), calls=%async_computation.1 | async-start | bytes 6082560 | tf_op jit(solution)/shard_map/all_gather | solution.py:1106
  11.7 6.2 %collective-permute-start.6 = (bf16[24,1536]{1,0:T(8,128)(2,1)S(1)}, bf16[24,1536]{1,0:T(8,128)(2,1)S(1)}, u32[]{:S(2)}, u32[]{:S(2)}) collective-permute-start(bf16[24,1536]{1,0:T(8,128)(2,1)S(1)} %reshape.218), channel_id=1, source_target_pairs={{0,1},{1,0},{2,3},{3,2},{4,5},{5,4},{6,7},{7,6},{8,9},{9,8},{10,11... | collective-permute-start | bytes 221192 | tf_op jit(solution)/shard_map/ppermute | solution.py:49
  13.7 1.4 collective-permute-start
  15.1 20.1 %collective-permute-start.4 = (bf16[400,768]{1,0:T(8,128)(2,1)S(1)}, bf16[400,768]{1,0:T(8,128)(2,1)S(1)}, u32[]{:S(2)}, u32[]{:S(2)}) collective-permute-start(bf16[400,768]{1,0:T(8,128)(2,1)S(1)} %fusion.11), channel_id=1, source_target_pairs={{0,2},{1,3},{2,0},{3,1},{4,6},{5,7},{6,4},{7,5},{8,10},{9,11},{10,... | collective-permute-start | bytes 1843208 | tf_op jit(solution)/shard_map/ppermute | solution.py:49
  17.8 17.3 %collective-permute-start.5 = (bf16[400,768]{1,0:T(8,128)(2,1)S(1)}, bf16[400,768]{1,0:T(8,128)(2,1)S(1)}, u32[]{:S(2)}, u32[]{:S(2)}) collective-permute-start(bf16[400,768]{1,0:T(8,128)(2,1)S(1)} %fusion.11), channel_id=1, source_target_pairs={{0,1},{1,0},{2,3},{3,2},{4,5},{5,4},{6,7},{7,6},{8,9},{9,8},{10,11... | collective-permute-start | bytes 1843208 | tf_op jit(solution)/shard_map/ppermute | solution.py:49
  17.9 8.6 %collective-permute-start.1 = (bf16[64,1152]{1,0:T(8,128)(2,1)S(1)}, bf16[64,1152]{1,0:T(8,128)(2,1)S(1)}, u32[]{:S(2)}, u32[]{:S(2)}) collective-permute-start(bf16[64,1152]{1,0:T(8,128)(2,1)S(1)} %fusion.21), channel_id=1, source_target_pairs={{0,8},{1,9},{2,10},{3,11},{4,12},{5,13},{6,14},{7,15},{8,16},{9,17... | collective-permute-start | bytes 442376 | tf_op jit(solution)/shard_map/ppermute | solution.py:49
  19.6 15.5 %collective-permute-start.2 = (bf16[64,1152]{1,0:T(8,128)(2,1)S(1)}, bf16[64,1152]{1,0:T(8,128)(2,1)S(1)}, u32[]{:S(2)}, u32[]{:S(2)}) collective-permute-start(bf16[64,1152]{1,0:T(8,128)(2,1)S(1)} %fusion.21), channel_id=1, source_target_pairs={{0,16},{1,17},{2,18},{3,19},{4,20},{5,21},{6,22},{7,23},{8,24},{9,... | collective-permute-start | bytes 442376 | tf_op jit(solution)/shard_map/ppermute | solution.py:49
  22.2 13.0 %collective-permute-start.3 = (bf16[64,1152]{1,0:T(8,128)(2,1)S(1)}, bf16[64,1152]{1,0:T(8,128)(2,1)S(1)}, u32[]{:S(2)}, u32[]{:S(2)}) collective-permute-start(bf16[64,1152]{1,0:T(8,128)(2,1)S(1)} %fusion.21), channel_id=1, source_target_pairs={{0,24},{1,25},{2,26},{3,27},{4,28},{5,29},{6,30},{7,31},{8,0},{9,1... | collective-permute-start | bytes 442376 | tf_op jit(solution)/shard_map/ppermute | solution.py:49
  26.5 19.3 %collective-permute-start.10 = (bf16[384,768]{1,0:T(8,128)(2,1)}, bf16[384,768]{1,0:T(8,128)(2,1)}, u32[]{:S(2)}, u32[]{:S(2)}) collective-permute-start(bf16[384,768]{1,0:T(8,128)(2,1)} %bitcast.23), channel_id=1, source_target_pairs={{0,1},{1,0},{2,3},{3,2},{4,5},{5,4},{6,7},{7,6},{8,9},{9,8},{10,11... | collective-permute-start | bytes 1769480 | tf_op jit(solution)/shard_map/ppermute | solution.py:49
  35.2 20.0 %copy-start.26 = (bf16[400,768]{1,0:T(8,128)(2,1)}, bf16[400,768]{1,0:T(8,128)(2,1)S(1)}, u32[]{:S(2)}) copy-start(bf16[400,768]{1,0:T(8,128)(2,1)S(1)} %collective-permute-done.4) | copy-start | bytes 1843204
  35.2 20.0 %copy-start.27 = (bf16[400,768]{1,0:T(8,128)(2,1)}, bf16[400,768]{1,0:T(8,128)(2,1)S(1)}, u32[]{:S(2)}) copy-start(bf16[400,768]{1,0:T(8,128)(2,1)S(1)} %collective-permute-done.5) | copy-start | bytes 1843204
  35.2 20.6 %collective-permute-start.9 = (bf16[400,768]{1,0:T(8,128)(2,1)S(1)}, bf16[400,768]{1,0:T(8,128)(2,1)}, u32[]{:S(2)}, u32[]{:S(2)}) collective-permute-start(bf16[400,768]{1,0:T(8,128)(2,1)S(1)} %collective-permute-done.4), channel_id=1, source_target_pairs={{0,1},{1,0},{2,3},{3,2},{4,5},{5,4},{6,7},{7,6},{8,9},{9,8},{10,11... | collective-permute-start | bytes 1843208 | tf_op jit(solution)/shard_map/ppermute | solution.py:49
  35.4 19.8 %copy-start.20 = (bf16[4,64,1152]{2,1,0:T(8,128)(2,1)}, bf16[4,64,1152]{2,1,0:T(8,128)(2,1)S(1)}, u32[]{:S(2)}) copy-start(bf16[4,64,1152]{2,1,0:T(8,128)(2,1)S(1)} %pad_maximum_fusion.4.refs_0_) | copy-start | bytes 1769476
  35.4 19.6 %collective-permute-start.7 = (bf16[4,64,1152]{2,1,0:T(8,128)(2,1)S(1)}, bf16[4,64,1152]{2,1,0:T(8,128)(2,1)S(1)}, u32[]{:S(2)}, u32[]{:S(2)}) collective-permute-start(bf16[4,64,1152]{2,1,0:T(8,128)(2,1)S(1)} %pad_maximum_fusion.4.refs_0_), channel_id=1, source_target_pairs={{0,4},{1,5},{2,6},{3,7},{4,0},{5,1},{6,2},{7,3},{8,12},{9,13},{10,... | collective-permute-start | bytes 1769480 | tf_op jit(solution)/shard_map/ppermute | solution.py:49
  37.0 18.2 %collective-permute-start.8 = (bf16[4,64,1152]{2,1,0:T(8,128)(2,1)S(1)}, bf16[4,64,1152]{2,1,0:T(8,128)(2,1)}, u32[]{:S(2)}, u32[]{:S(2)}) collective-permute-start(bf16[4,64,1152]{2,1,0:T(8,128)(2,1)S(1)} %pad_maximum_fusion.4.refs_0_), channel_id=1, source_target_pairs={{0,2},{1,3},{2,0},{3,1},{4,6},{5,7},{6,4},{7,5},{8,10},{9,11},{10,... | collective-permute-start | bytes 1769480 | tf_op jit(solution)/shard_map/ppermute | solution.py:49
  38.6 44.2 %all-to-all-start = ((bf16[4,96,768]{2,1,0:T(8,128)(2,1)}), bf16[4,96,768]{2,1,0:T(8,128)(2,1)}, u32[]{:S(2)}, u32[]{:S(2)}) async-start(bf16[4,96,768]{2,1,0:T(8,128)(2,1)} %broadcast_in_dim.35), calls=%async_computation | async-start | bytes 1179648 | tf_op jit(solution)/shard_map/all_to_all | solution.py:137
  58.6 7.9 %collective-permute-start.11 = (bf16[2,64,1152]{2,1,0:T(8,128)(2,1)S(1)}, bf16[2,64,1152]{2,1,0:T(8,128)(2,1)S(1)}, u32[]{:S(2)}, u32[]{:S(2)}) collective-permute-start(bf16[2,64,1152]{2,1,0:T(8,128)(2,1)S(1)} %slice.267), channel_id=1, source_target_pairs={{0,2},{1,3},{2,0},{3,1},{4,6},{5,7},{6,4},{7,5},{8,10},{9,11},{10,... | collective-permute-start | bytes 884744 | tf_op jit(solution)/shard_map/ppermute | solution.py:49
  59.6 8.7 %collective-permute-start.12 = (bf16[2,64,1152]{2,1,0:T(8,128)(2,1)S(1)}, bf16[2,64,1152]{2,1,0:T(8,128)(2,1)S(1)}, u32[]{:S(2)}, u32[]{:S(2)}) collective-permute-start(bf16[2,64,1152]{2,1,0:T(8,128)(2,1)S(1)} %slice.269), channel_id=1, source_target_pairs={{0,4},{1,5},{2,6},{3,7},{4,0},{5,1},{6,2},{7,3},{8,12},{9,13},{10,... | collective-permute-start | bytes 884744 | tf_op jit(solution)/shard_map/ppermute | solution.py:49
  82.8 19.6 %collective-permute-start.14 = (bf16[4,96,768]{2,1,0:T(8,128)(2,1)}, bf16[4,96,768]{2,1,0:T(8,128)(2,1)S(1)}, u32[]{:S(2)}, u32[]{:S(2)}) collective-permute-start(bf16[4,96,768]{2,1,0:T(8,128)(2,1)} %all-to-all-done.refs_0_), channel_id=1, source_target_pairs={{0,4},{1,5},{2,6},{3,7},{4,0},{5,1},{6,2},{7,3},{8,12},{9,13},{10,... | collective-permute-start | bytes 1769480 | tf_op jit(solution)/shard_map/ppermute | solution.py:49
  84.4 17.9 %collective-permute-start.15 = (bf16[4,96,768]{2,1,0:T(8,128)(2,1)}, bf16[4,96,768]{2,1,0:T(8,128)(2,1)S(1)}, u32[]{:S(2)}, u32[]{:S(2)}) collective-permute-start(bf16[4,96,768]{2,1,0:T(8,128)(2,1)} %all-to-all-done.refs_0_), channel_id=1, source_target_pairs={{0,2},{1,3},{2,0},{3,1},{4,6},{5,7},{6,4},{7,5},{8,10},{9,11},{10,... | collective-permute-start | bytes 1769480 | tf_op jit(solution)/shard_map/ppermute | solution.py:49
  87.2 15.1 %copy-start.4 = (bf16[1536,128]{1,0:T(8,128)(2,1)}, bf16[1536,128]{1,0:T(8,128)(2,1)S(1)}, u32[]{:S(2)}) copy-start(bf16[1536,128]{1,0:T(8,128)(2,1)S(1)} %select_convert_fusion.pen_ref) | copy-start | bytes 1179652
  102.3 6.1 %collective-permute-start.13 = (bf16[768,384]{1,0:T(8,128)(2,1)}, bf16[768,384]{1,0:T(8,128)(2,1)}, u32[]{:S(2)}, u32[]{:S(2)}) collective-permute-start(bf16[768,384]{1,0:T(8,128)(2,1)} %get-tuple-element.144.refs_0_), channel_id=1, source_target_pairs={{0,1},{1,0},{2,3},{3,2},{4,5},{5,4},{6,7},{7,6},{8,9},{9,8},{10,11... | collective-permute-start | bytes 1769480 | tf_op jit(solution)/shard_map/ppermute | solution.py:49
  103.2 11.0 %collective-permute-start.16 = (bf16[2,96,768]{2,1,0:T(8,128)(2,1)}, bf16[2,96,768]{2,1,0:T(8,128)(2,1)}, u32[]{:S(2)}, u32[]{:S(2)}) collective-permute-start(bf16[2,96,768]{2,1,0:T(8,128)(2,1)} %slice.274), channel_id=1, source_target_pairs={{0,2},{1,3},{2,0},{3,1},{4,6},{5,7},{6,4},{7,5},{8,10},{9,11},{10,... | collective-permute-start | bytes 884744 | tf_op jit(solution)/shard_map/ppermute | solution.py:49
  104.1 10.1 %collective-permute-start.17 = (bf16[2,96,768]{2,1,0:T(8,128)(2,1)}, bf16[2,96,768]{2,1,0:T(8,128)(2,1)}, u32[]{:S(2)}, u32[]{:S(2)}) collective-permute-start(bf16[2,96,768]{2,1,0:T(8,128)(2,1)} %slice.275), channel_id=1, source_target_pairs={{0,4},{1,5},{2,6},{3,7},{4,0},{5,1},{6,2},{7,3},{8,12},{9,13},{10,... | collective-permute-start | bytes 884744 | tf_op jit(solution)/shard_map/ppermute | solution.py:49
  135.1 5.6 %collective-permute-start.18 = (bf16[768,768]{1,0:T(8,128)(2,1)S(1)}, bf16[768,768]{1,0:T(8,128)(2,1)S(1)}, u32[]{:S(2)}, u32[]{:S(2)}) collective-permute-start(bf16[768,768]{1,0:T(8,128)(2,1)S(1)} %get-tuple-element.153), channel_id=1, source_target_pairs={{0,1},{1,0},{2,3},{3,2},{4,5},{5,4},{6,7},{7,6},{8,9},{9,8},{10,11... | collective-permute-start | bytes 3538952 | tf_op jit(solution)/shard_map/ppermute | solution.py:49
  135.2 19.2 %slice-start = ((s8[4718592]{0:T(1024)(128)(4,1)}), s8[4194304]{0:T(1024)(128)(4,1)S(1)}, s32[]{:S(2)}) async-start(s8[4718592]{0:T(1024)(128)(4,1)} %bitcast.167), calls=%async_computation.2 | async-start | bytes 8388608
  137.1 16.4 %collective-permute-start.19 = (bf16[2,192,768]{2,1,0:T(8,128)(2,1)S(1)}, bf16[2,192,768]{2,1,0:T(8,128)(2,1)S(1)}, u32[]{:S(2)}, u32[]{:S(2)}) collective-permute-start(bf16[2,192,768]{2,1,0:T(8,128)(2,1)S(1)} %get-tuple-element.224), channel_id=1, source_target_pairs={{0,2},{1,3},{2,0},{3,1},{4,6},{5,7},{6,4},{7,5},{8,10},{9,11},{10,... | collective-permute-start | bytes 1769480 | tf_op jit(solution)/shard_map/ppermute | solution.py:49
  138.8 15.6 %collective-permute-start.20 = (bf16[2,192,768]{2,1,0:T(8,128)(2,1)S(1)}, bf16[2,192,768]{2,1,0:T(8,128)(2,1)S(1)}, u32[]{:S(2)}, u32[]{:S(2)}) collective-permute-start(bf16[2,192,768]{2,1,0:T(8,128)(2,1)S(1)} %get-tuple-element.222), channel_id=1, source_target_pairs={{0,4},{1,5},{2,6},{3,7},{4,0},{5,1},{6,2},{7,3},{8,12},{9,13},{10,... | collective-permute-start | bytes 1769480 | tf_op jit(solution)/shard_map/ppermute | solution.py:49
  140.7 6.6 %copy-start.2 = (bf16[1536,384]{1,0:T(8,128)(2,1)S(1)}, bf16[1536,384]{1,0:T(8,128)(2,1)}, u32[]{:S(2)}) copy-start(bf16[1536,384]{1,0:T(8,128)(2,1)} %copy-done) | copy-start | bytes 3538948
  140.7 6.6 %copy-start.5 = (bf16[1536,128]{1,0:T(8,128)(2,1)S(1)}, bf16[1536,128]{1,0:T(8,128)(2,1)}, u32[]{:S(2)}) copy-start(bf16[1536,128]{1,0:T(8,128)(2,1)} %copy-done.4) | copy-start | bytes 1179652
  140.7 6.6 %copy-start.8 = (bf16[768,384]{1,0:T(8,128)(2,1)S(1)}, bf16[768,384]{1,0:T(8,128)(2,1)}, u32[]{:S(2)}) copy-start(bf16[768,384]{1,0:T(8,128)(2,1)} %copy-done.6) | copy-start | bytes 1769476
  140.7 6.6 %copy-start.10 = (f32[768,384]{1,0:T(8,128)S(1)}, f32[768,384]{1,0:T(8,128)}, u32[]{:S(2)}) copy-start(f32[768,384]{1,0:T(8,128)} %copy-done.9) | copy-start | bytes 3538948
  140.7 6.6 %copy-start.12 = (bf16[768,128]{1,0:T(8,128)(2,1)S(1)}, bf16[768,128]{1,0:T(8,128)(2,1)}, u32[]{:S(2)}) copy-start(bf16[768,128]{1,0:T(8,128)(2,1)} %slice_convert_fusion.hot_ref) | copy-start | bytes 589828
  140.7 6.6 %copy-start.17 = (f32[3,2,768]{2,1,0:T(2,128)S(1)}, f32[3,2,768]{2,1,0:T(2,128)}, u32[]{:S(2)}) copy-start(f32[3,2,768]{2,1,0:T(2,128)} %copy-done.16) | copy-start | bytes 55300
  140.8 13.7 %slice-start.1 = ((s8[4718592]{0:T(1024)(128)(4,1)}), s8[524288]{0:T(1024)(128)(4,1)S(1)}, s32[]{:S(2)}) async-start(s8[4718592]{0:T(1024)(128)(4,1)} %bitcast.167), calls=%async_computation.3 | async-start | bytes 1048576
  154.8 27.5 %collective-permute-start.22 = (bf16[4,192,768]{2,1,0:T(8,128)(2,1)S(1)}, bf16[4,192,768]{2,1,0:T(8,128)(2,1)S(1)}, u32[]{:S(2)}, u32[]{:S(2)}) collective-permute-start(bf16[4,192,768]{2,1,0:T(8,128)(2,1)S(1)} %pad_maximum_fusion.3), channel_id=1, source_target_pairs={{0,2},{1,3},{2,0},{3,1},{4,6},{5,7},{6,4},{7,5},{8,10},{9,11},{10,... | collective-permute-start | bytes 3538952 | tf_op jit(solution)/shard_map/ppermute | solution.py:49
  155.4 27.3 %collective-permute-start.21 = (bf16[4,192,768]{2,1,0:T(8,128)(2,1)S(1)}, bf16[4,192,768]{2,1,0:T(8,128)(2,1)S(1)}, u32[]{:S(2)}, u32[]{:S(2)}) collective-permute-start(bf16[4,192,768]{2,1,0:T(8,128)(2,1)S(1)} %pad_maximum_fusion.2), channel_id=1, source_target_pairs={{0,4},{1,5},{2,6},{3,7},{4,0},{5,1},{6,2},{7,3},{8,12},{9,13},{10,... | collective-permute-start | bytes 3538952 | tf_op jit(solution)/shard_map/ppermute | solution.py:49
  183.3 17.4 %collective-permute-start.23 = (bf16[2,4,48,384]{3,2,1,0:T(8,128)(2,1)S(1)}, bf16[2,4,48,384]{3,2,1,0:T(8,128)(2,1)S(1)}, u32[]{:S(2)}, u32[]{:S(2)}) collective-permute-start(bf16[2,4,48,384]{3,2,1,0:T(8,128)(2,1)S(1)} %get-tuple-element.230), channel_id=1, source_target_pairs={{0,2},{1,3},{2,0},{3,1},{4,6},{5,7},{6,4},{7,5},{8,10},{9,11},{10,... | collective-permute-start | bytes 884744 | tf_op jit(solution)/shard_map/ppermute | solution.py:49
  184.9 15.8 %collective-permute-start.24 = (bf16[2,4,48,384]{3,2,1,0:T(8,128)(2,1)S(1)}, bf16[2,4,48,384]{3,2,1,0:T(8,128)(2,1)S(1)}, u32[]{:S(2)}, u32[]{:S(2)}) collective-permute-start(bf16[2,4,48,384]{3,2,1,0:T(8,128)(2,1)S(1)} %get-tuple-element.228), channel_id=1, source_target_pairs={{0,4},{1,5},{2,6},{3,7},{4,0},{5,1},{6,2},{7,3},{8,12},{9,13},{10,... | collective-permute-start | bytes 884744 | tf_op jit(solution)/shard_map/ppermute | solution.py:49
  186.6 14.5 %collective-permute-start.25 = (bf16[192,768]{1,0:T(8,128)(2,1)S(1)}, bf16[192,768]{1,0:T(8,128)(2,1)S(1)}, u32[]{:S(2)}, u32[]{:S(2)}) collective-permute-start(bf16[192,768]{1,0:T(8,128)(2,1)S(1)} %get-tuple-element.238), channel_id=1, source_target_pairs={{0,8},{1,9},{2,10},{3,11},{4,12},{5,13},{6,14},{7,15},{8,16},{9,17... | collective-permute-start | bytes 884744 | tf_op jit(solution)/shard_map/ppermute | solution.py:49
  191.7 12.4 %collective-permute-start.26 = (bf16[192,768]{1,0:T(8,128)(2,1)S(1)}, bf16[192,768]{1,0:T(8,128)(2,1)S(1)}, u32[]{:S(2)}, u32[]{:S(2)}) collective-permute-start(bf16[192,768]{1,0:T(8,128)(2,1)S(1)} %get-tuple-element.237), channel_id=1, source_target_pairs={{0,24},{1,25},{2,26},{3,27},{4,28},{5,29},{6,30},{7,31},{8,0},{9,1... | collective-permute-start | bytes 884744 | tf_op jit(solution)/shard_map/ppermute | solution.py:49
  200.9 6.1 %copy-start.19 = (f32[768,768]{1,0:T(8,128)S(1)}, f32[768,768]{1,0:T(8,128)}, u32[]{:S(2)}) copy-start(f32[768,768]{1,0:T(8,128)} %get-tuple-element.182.refs_0_) | copy-start | bytes 7077892
  204.1 2.9 %collective-permute-start.27 = (bf16[784,768]{1,0:T(8,128)(2,1)S(1)}, bf16[784,768]{1,0:T(8,128)(2,1)S(1)}, u32[]{:S(2)}, u32[]{:S(2)}) collective-permute-start(bf16[784,768]{1,0:T(8,128)(2,1)S(1)} %get-tuple-element.188), channel_id=1, source_target_pairs={{0,1},{1,0},{2,3},{3,2},{4,5},{5,4},{6,7},{7,6},{8,9},{9,8},{10,11... | collective-permute-start | bytes 3612680 | tf_op jit(solution)/shard_map/ppermute | solution.py:49
  204.1 15.7 %collective-permute-start.30 = (bf16[4,4,48,384]{3,2,1,0:T(8,128)(2,1)S(1)}, bf16[4,4,48,384]{3,2,1,0:T(8,128)(2,1)S(1)}, u32[]{:S(2)}, u32[]{:S(2)}) collective-permute-start(bf16[4,4,48,384]{3,2,1,0:T(8,128)(2,1)S(1)} %pad_maximum_fusion.5), channel_id=1, source_target_pairs={{0,4},{1,5},{2,6},{3,7},{4,0},{5,1},{6,2},{7,3},{8,12},{9,13},{10,... | collective-permute-start | bytes 1769480 | tf_op jit(solution)/shard_map/ppermute | solution.py:49
  204.7 16.2 %collective-permute-start.31 = (bf16[4,4,48,384]{3,2,1,0:T(8,128)(2,1)S(1)}, bf16[4,4,48,384]{3,2,1,0:T(8,128)(2,1)S(1)}, u32[]{:S(2)}, u32[]{:S(2)}) collective-permute-start(bf16[4,4,48,384]{3,2,1,0:T(8,128)(2,1)S(1)} %pad_maximum_fusion.6), channel_id=1, source_target_pairs={{0,2},{1,3},{2,0},{3,1},{4,6},{5,7},{6,4},{7,5},{8,10},{9,11},{10,... | collective-permute-start | bytes 1769480 | tf_op jit(solution)/shard_map/ppermute | solution.py:49
  205.6 16.1 %collective-permute-start.35 = (bf16[192,768]{1,0:T(8,128)(2,1)S(1)}, bf16[192,768]{1,0:T(8,128)(2,1)S(1)}, u32[]{:S(2)}, u32[]{:S(2)}) collective-permute-start(bf16[192,768]{1,0:T(8,128)(2,1)S(1)} %get-tuple-element.236), channel_id=1, source_target_pairs={{0,16},{1,17},{2,18},{3,19},{4,20},{5,21},{6,22},{7,23},{8,24},{9,... | collective-permute-start | bytes 884744 | tf_op jit(solution)/shard_map/ppermute | solution.py:49
  207.1 33.0 %collective-permute-start.29 = (bf16[384,768]{1,0:T(8,128)(2,1)S(1)}, bf16[384,768]{1,0:T(8,128)(2,1)S(1)}, u32[]{:S(2)}, u32[]{:S(2)}) collective-permute-start(bf16[384,768]{1,0:T(8,128)(2,1)S(1)} %add_convert_fusion), channel_id=1, source_target_pairs={{0,2},{1,3},{2,0},{3,1},{4,6},{5,7},{6,4},{7,5},{8,10},{9,11},{10,... | collective-permute-start | bytes 1769480 | tf_op jit(solution)/shard_map/ppermute | solution.py:49
  208.1 13.6 %copy-start.23 = (f32[768,768]{1,0:T(8,128)S(1)}, f32[768,768]{1,0:T(8,128)}, u32[]{:S(2)}) copy-start(f32[768,768]{1,0:T(8,128)} %get-tuple-element.189) | copy-start | bytes 7077892
  221.8 6.5 %collective-permute-start.28 = (bf16[384,768]{1,0:T(8,128)(2,1)S(1)}, bf16[384,768]{1,0:T(8,128)(2,1)S(1)}, u32[]{:S(2)}, u32[]{:S(2)}) collective-permute-start(bf16[384,768]{1,0:T(8,128)(2,1)S(1)} %fusion.12), channel_id=1, source_target_pairs={{0,1},{1,0},{2,3},{3,2},{4,5},{5,4},{6,7},{7,6},{8,9},{9,8},{10,11... | collective-permute-start | bytes 1769480 | tf_op jit(solution)/shard_map/ppermute | solution.py:49
  222.0 6.3 %copy-start.28 = (f32[768,768]{1,0:T(8,128)S(1)}, f32[768,768]{1,0:T(8,128)}, u32[]{:S(2)}) copy-start(f32[768,768]{1,0:T(8,128)} %get-tuple-element.190) | copy-start | bytes 7077892
  222.1 2.8 %collective-permute-start.36 = (bf16[96,768]{1,0:T(8,128)(2,1)S(1)}, bf16[96,768]{1,0:T(8,128)(2,1)S(1)}, u32[]{:S(2)}, u32[]{:S(2)}) collective-permute-start(bf16[96,768]{1,0:T(8,128)(2,1)S(1)} %slice.393), channel_id=1, source_target_pairs={{0,1},{1,0},{2,3},{3,2},{4,5},{5,4},{6,7},{7,6},{8,9},{9,8},{10,11... | collective-permute-start | bytes 442376 | tf_op jit(solution)/shard_map/ppermute | solution.py:49
  222.7 9.2 %collective-permute-start.32 = (bf16[224,384]{1,0:T(8,128)(2,1)S(1)}, bf16[224,384]{1,0:T(8,128)(2,1)S(1)}, u32[]{:S(2)}, u32[]{:S(2)}) collective-permute-start(bf16[224,384]{1,0:T(8,128)(2,1)S(1)} %get-tuple-element.243), channel_id=1, source_target_pairs={{0,8},{1,9},{2,10},{3,11},{4,12},{5,13},{6,14},{7,15},{8,16},{9,17... | collective-permute-start | bytes 516104 | tf_op jit(solution)/shard_map/ppermute | solution.py:49
  222.8 15.6 %collective-permute-start.33 = (bf16[224,384]{1,0:T(8,128)(2,1)S(1)}, bf16[224,384]{1,0:T(8,128)(2,1)S(1)}, u32[]{:S(2)}, u32[]{:S(2)}) collective-permute-start(bf16[224,384]{1,0:T(8,128)(2,1)S(1)} %get-tuple-element.242), channel_id=1, source_target_pairs={{0,16},{1,17},{2,18},{3,19},{4,20},{5,21},{6,22},{7,23},{8,24},{9,... | collective-permute-start | bytes 516104 | tf_op jit(solution)/shard_map/ppermute | solution.py:49
  224.8 13.5 %collective-permute-start.34 = (bf16[224,384]{1,0:T(8,128)(2,1)S(1)}, bf16[224,384]{1,0:T(8,128)(2,1)S(1)}, u32[]{:S(2)}, u32[]{:S(2)}) collective-permute-start(bf16[224,384]{1,0:T(8,128)(2,1)S(1)} %get-tuple-element.241), channel_id=1, source_target_pairs={{0,24},{1,25},{2,26},{3,27},{4,28},{5,29},{6,30},{7,31},{8,0},{9,1... | collective-permute-start | bytes 516104 | tf_op jit(solution)/shard_map/ppermute | solution.py:49
  229.3 10.8 %copy-start.15 = (f32[1536,1]{1,0:T(8,128)S(1)}, f32[1536,1]{1,0:T(8,128)}, u32[]{:S(2)}) copy-start(f32[1536,1]{1,0:T(8,128)} %get-tuple-element.191.refs_4_) | copy-start | bytes 18436
  238.5 9.9 %collective-permute-start.37 = (bf16[4,48,384]{2,1,0:T(8,128)(2,1)S(1)}, bf16[4,48,384]{2,1,0:T(8,128)(2,1)S(1)}, u32[]{:S(2)}, u32[]{:S(2)}) collective-permute-start(bf16[4,48,384]{2,1,0:T(8,128)(2,1)S(1)} %get-tuple-element.218), channel_id=1, source_target_pairs={{0,1},{1,0},{2,3},{3,2},{4,5},{5,4},{6,7},{7,6},{8,9},{9,8},{10,11... | collective-permute-start | bytes 442376 | tf_op jit(solution)/shard_map/ppermute | solution.py:49
  238.6 5.6 %collective-permute-start.38 = (f32[32,384]{1,0:T(8,128)S(1)}, f32[32,384]{1,0:T(8,128)S(1)}, u32[]{:S(2)}, u32[]{:S(2)}) collective-permute-start(f32[32,384]{1,0:T(8,128)S(1)} %convert_add_fusion.10), channel_id=1, source_target_pairs={{0,4},{1,5},{2,6},{3,7},{4,0},{5,1},{6,2},{7,3},{8,12},{9,13},{10,... | collective-permute-start | bytes 147464 | tf_op jit(solution)/shard_map/ppermute | solution.py:49
  244.2 4.2 %collective-permute-start.39 = (f32[32,384]{1,0:T(8,128)S(1)}, f32[32,384]{1,0:T(8,128)S(1)}, u32[]{:S(2)}, u32[]{:S(2)}) collective-permute-start(f32[32,384]{1,0:T(8,128)S(1)} %add.206), channel_id=1, source_target_pairs={{0,2},{1,3},{2,0},{3,1},{4,6},{5,7},{6,4},{7,5},{8,10},{9,11},{10,... | collective-permute-start | bytes 147464 | tf_op jit(solution)/shard_map/ppermute | solution.py:49
  (22 other events, 62.8 us)
Sparse Core Ops, SparseCore 0:
  11.0 85.0 all-gather.2

commit v3 on v2

--- a/solution.py
+++ b/solution.py
@@ -341,7 +341,7 @@
             pl.BlockSpec((1, 2, block), lambda p, i: (p, 0, i)),
         ],
         out_shape=[
-            jax.ShapeDtypeStruct((rows, width), f32),
+            pltpu.HBM((rows, width), f32),
             jax.ShapeDtypeStruct((rows, width), bf16),
             jax.ShapeDtypeStruct((pairs, 2, rows), f32),
         ],
@@ -507,9 +507,9 @@
             pl.BlockSpec(shape, lambda i, s: (0, 0, 0)),
         ],
         out_shape=[
-            jax.ShapeDtypeStruct((2 * local, half), bf16),
-            jax.ShapeDtypeStruct((rows, half), bf16),
-            jax.ShapeDtypeStruct((rows, half), bf16),
+            pltpu.HBM((2 * local, half), bf16),
+            pltpu.HBM((rows, half), bf16),
+            pltpu.HBM((rows, half), bf16),
             pltpu.HBM((width, rows), bf16),
             pltpu.HBM((rows, width), bf16),
             pltpu.HBM((rows, 1), f32),
@@ -609,7 +609,7 @@
     return call(
         out_back_kernel,
         grid.place,
-        [mine, got, hbm(dy), hbm(n2), hbm(rstd), vec, hbm(w)],
+        [mine, got, dy, n2, rstd, vec, w],
         grid=(rows // block,),
         in_specs=[
             line(width),
@@ -1154,12 +1154,13 @@
     dy = in_order(first, dy_mine, dy_near).reshape(chip_rows, width)
 
     queries, keys, values, h1t, n1, rstd1, full_qkv = project_qkv(
-        grid, token_rows, vec, qkv_weights, local
+        grid, behind(token_rows, dy), vec, qkv_weights, local
     )
     pairs = half // 128
     if fast:
         queries, up_line = lock(queries, up_line)
         up_over, up_sides = grid.shift(up_line, "x", 1), grid.along(up_line, "q")
+    queries, keys, values = hbm(queries), hbm(keys), hbm(values)
     attended, att, lse = attn_fwd(queries, keys, values, hot, pen, 0, pairs)
     if fast:
         up_over, up_sides = behind((up_over, up_sides), att)
@@ -1173,7 +1174,7 @@
     d_after, d_branch, d_att, sums2 = out_back(grid, dh, swap(dh_b), dy, n2, rstd2, vec, out_rows)
 
     def back(d, a, n):
-        return attn_bwd(queries, keys, values, hot, pen, attended, d, lse, a, n)
+        return attn_bwd(queries, keys, values, hot, pen, hbm(attended), d, lse, a, n)
 
     by_core = lambda v: v.reshape(2, local, width)
     up_sums = gbias.reshape(2, width)

time: 263 us -> 254 us (0.966)
  the two profiles are of different devices: /device:TPU:0 before, /device:TPU:10 now
where the time goes in v3:
time: 254 us; the launch traced here: 249 us
  Pallas kernels  97.2 us (38%)
  waiting for transfers between devices  67.3 us (26%)
  starting transfers between devices  44.3 us (17%)
  between operations  15.2 us (6%)
  local copies, waits for them, and re-layouts  14.7 us (6%)
  other arithmetic  10.3 us (4%)
    ppermute x40, waiting for transfers between devices, shift(): return lax.ppermute(value, AXES, pairs)  67.3 us
    pallas_call x11, Pallas kernels, call(): pl.pallas_call(kernel, grid_spec=spec, compiler_params=pltpu.CompilerPara...  63.6 us
    ppermute x40, starting transfers between devices, shift(): return lax.ppermute(value, AXES, pairs)  38.6 us
    pallas_call x2, Pallas kernels, attn_bwd(): pl.pallas_call(attn_bwd_kernel, grid=(pairs, rows // block), in_specs=[by...  21 us
    pallas_call x1, Pallas kernels, attn_fwd(): pl.pallas_call(attn_fwd_kernel, grid=(pairs, rows // block), in_specs=[pl...  12.6 us
    all_to_all x1, starting transfers between devices, exchange(): lax.all_to_all(blocks, AXES, 0, 0, axis_index_groups=self.groups(('z',)),...  5.61 us
  transfers between devices with their start and end apart: 42, of which 19 were waited for; matrix products, arithmetic and copies ran while one was open for 8% of the time, Pallas kernels for 30%

profile of v3, /device:TPU:10, one launch (start us, length us, event | category | flops | bytes accessed | tf_op | source)
XLA Modules:
  0.0 249.0 jit_solution(14455402699987066519)
XLA Ops:
  7.3 1.7 pad_maximum_fusion.7
  9.0 1.2 reshape.216
  10.2 1.3 dynamic-slice_reduce_fusion.1
  11.8 0.7 dynamic-slice_reduce_fusion.3
  14.8 1.6 collective-permute-start.4
  16.5 1.6 collective-permute-start.1
  18.1 1.2 collective-permute-start.2
  19.4 1.8 collective-permute-start.3
  21.2 2.5 collective-permute-done.1
  23.7 11.1 %collective-permute-done.2 = bf16[64,1152]{1,0:T(8,128)(2,1)S(1)} collective-permute-done((bf16[64,1152]{1,0:T(8,128)(2,1)S(1)}, bf16[64,1152]{1,0:T(8,128)(2,1)S(1)}, u32[]{:S(2)}, u32[]{:S(2)}) %collective-permute-start.2) | collective-permute-done | bytes 147488 | tf_op jit(solution)/shard_map/ppermute | solution.py:49
  34.8 1.2 collective-permute-done.3
  36.2 0.7 copy-done.18
  38.2 0.9 broadcast_in_dim.35
  39.1 5.6 %all-to-all-start = ((bf16[4,96,768]{2,1,0:T(8,128)(2,1)}), bf16[4,96,768]{2,1,0:T(8,128)(2,1)}, u32[]{:S(2)}, u32[]{:S(2)}) async-start(bf16[4,96,768]{2,1,0:T(8,128)(2,1)} %broadcast_in_dim.35), calls=%async_computation | async-start | bytes 1179648 | tf_op jit(solution)/shard_map/all_to_all | solution.py:137
  44.7 13.0 %collective-permute-done.7.refs_1_ = bf16[4,64,1152]{2,1,0:T(8,128)(2,1)S(1)} collective-permute-done((bf16[4,64,1152]{2,1,0:T(8,128)(2,1)S(1)}, bf16[4,64,1152]{2,1,0:T(8,128)(2,1)S(1)}, u32[]{:S(2)}, u32[]{:S(2)}) %collective-permute-start.7) | collective-permute-done | bytes 589856 | tf_op jit(solution)/shard_map/ppermute | solution.py:49
  57.7 0.8 slice.267
  58.5 0.7 slice.269
  59.3 1.2 select_bitcast_fusion
  62.0 1.3 select_bitcast_fusion.5
  63.3 1.2 pad_maximum_fusion.1
  65.0 4.2 %collective-permute-done.11.refs_3_ = bf16[2,64,1152]{2,1,0:T(8,128)(2,1)S(1)} collective-permute-done((bf16[2,64,1152]{2,1,0:T(8,128)(2,1)}, bf16[2,64,1152]{2,1,0:T(8,128)(2,1)S(1)}, u32[]{:S(2)}, u32[]{:S(2)}) %collective-permute-start.11) | collective-permute-done | bytes 294944 | tf_op jit(solution)/shard_map/ppermute | solution.py:49
  70.0 0.9 vectors.1.vec_ref.refs_6_
  70.9 9.1 %qkv.1 = (bf16[768,384]{1,0:T(8,128)(2,1)}, bf16[1536,384]{1,0:T(8,128)(2,1)}, bf16[1536,384]{1,0:T(8,128)(2,1)}, bf16[768,1536]{1,0:T(8,128)(2,1)}, bf16[1536,7...) custom-call(s32[4]{0:T(128)S(1)} %pad_add_fusion.place, ...), custom_call_target="tpu_custom_call" | custom-call | flops 1000 | bytes 1000 | tf_op jit(solution)/shard_map/qkv/pallas_call | solution.py:171
  80.9 1.6 collective-permute-start.15
  82.8 12.6 %attn_fwd.1 = (f32[768,384]{1,0:T(8,128)}, bf16[768,384]{1,0:T(8,128)(2,1)S(1)}, f32[3,2,768]{2,1,0:T(2,128)S(1)}) custom-call(bf16[768,384]{1,0:T(8,128)(2,1)} %get-tuple-element.144.q_ref, bf16[1536,384]{1,0:T(8,128)(2,1)} %get-tuple-element.145.k_ref, bf16[1536,384]{1,0:T(8,128)(2,1)} %get-tuple-element.146.v_ref, ...), custom_call_target="tpu_custom_call" | custom-call | flops 1000 | bytes 1000 | tf_op jit(solution)/shard_map/attn_fwd/pallas_call | solution.py:328
  96.0 0.8 copy-done.14
  96.8 0.8 slice.274
  98.2 0.7 slice.275
  98.9 1.6 collective-permute-start.17
  100.5 1.4 slice.333
  101.9 5.4 %out_proj.1 = (f32[768,768]{1,0:T(8,128)}, bf16[768,768]{1,0:T(8,128)(2,1)}, bf16[768,768]{1,0:T(8,128)(2,1)}, f32[768,128]{1,0:T(8,128)}) custom-call(s32[4]{0:T(128)S(1)} %pad_add_fusion.place, bf16[1536,768]{1,0:T(8,128)(2,1)S(1)} %pad_maximum_fusion.x_ref, bf16[2,384,768]{2,1,0:T(8,128)(2,1)S(1)} %bitcast.159, f32[16,768]{1,0:T(8,128)S(1)} %copy-done.2, ...), custom_call_target="tpu_custom_call" | custom-call | flops 1000 | bytes 1000 | tf_op jit(solution)/shard_map/out_proj/pallas_call | solution.py:171
  107.3 0.9 collective-permute-done.17.refs_4_
  108.2 20.7 %feed_forward.1 = (bf16[4,4,192,768]{3,2,1,0:T(8,128)(2,1)}, f32[2,1,768]{2,1,0:T(1,128)S(1)}, f32[768,768]{1,0:T(8,128)}, f32[768,768]{1,0:T(8,128)S(1)}, bf16[768,768]{1,0:T(8,128)(2,1)S(1)}) custom-call(s32[4]{0:T(128)S(1)} %pad_add_fusion.place, bf16[768,768]{1,0:T(8,128)(2,1)} %get-tuple-element.148.h2_ref, bf16[768,768]{1,0:T(8,128)(2,1)} %bitcast.161, ...), custom_call_target="tpu_custom_call" | custom-call | flops 1000 | bytes 1000 | tf_op jit(solution)/shard_map/feed_forward/pallas_call | solution.py:171
  129.0 1.9 slice_bitcast_fusion.1
  130.9 1.7 collective-permute-start.19
  132.6 1.7 collective-permute-start.20
  134.4 4.3 %out_back.1 = (f32[768,768]{1,0:T(8,128)}, bf16[768,768]{1,0:T(8,128)(2,1)S(1)}, bf16[768,384]{1,0:T(8,128)(2,1)S(1)}, f32[8,768]{1,0:T(8,128)S(1)}) custom-call(s32[4]{0:T(128)S(1)} %pad_add_fusion.place, f32[768,768]{1,0:T(8,128)S(1)} %get-tuple-element.154.mine_ref, bf16[768,768]{1,0:T(8,128)(2,1)S(1)} %collective-permute-done.18.got_ref, ...), custom_call_target="tpu_custom_call" | custom-call | flops 1000 | bytes 1000 | tf_op jit(solution)/shard_map/out_back/pallas_call | solution.py:171
  138.7 7.2 %attn_bwd.2 = (bf16[768,128]{1,0:T(8,128)(2,1)S(1)}, bf16[1536,128]{1,0:T(8,128)(2,1)S(1)}, bf16[1536,128]{1,0:T(8,128)(2,1)S(1)}) custom-call(bf16[768,384]{1,0:T(8,128)(2,1)} %get-tuple-element.144.q_ref, bf16[1536,384]{1,0:T(8,128)(2,1)} %get-tuple-element.145.k_ref, bf16[1536,384]{1,0:T(8,128)(2,1)} %get-tuple-element.146.v_ref, ...), custom_call_target="tpu_custom_call" | custom-call | flops 1000 | bytes 1000 | tf_op jit(solution)/shard_map/attn_bwd/pallas_call | solution.py:406
  145.9 0.8 collective-permute-done.19
  146.7 1.3 collective-permute-done.20
  149.0 1.8 collective-permute-start.21
  150.8 13.8 %attn_bwd.3 = (bf16[768,256]{1,0:T(8,128)(2,1)S(1)}, bf16[1536,256]{1,0:T(8,128)(2,1)S(1)}, bf16[1536,256]{1,0:T(8,128)(2,1)S(1)}) custom-call(bf16[768,384]{1,0:T(8,128)(2,1)} %get-tuple-element.144.q_ref, bf16[1536,384]{1,0:T(8,128)(2,1)} %get-tuple-element.145.k_ref, bf16[1536,384]{1,0:T(8,128)(2,1)} %get-tuple-element.146.v_ref, ...), custom_call_target="tpu_custom_call" | custom-call | flops 1000 | bytes 1000 | tf_op jit(solution)/shard_map/attn_bwd/pallas_call | solution.py:406
  164.6 7.3 %matrix_grads.1 = bf16[4,4,4,48,384]{4,3,2,1,0:T(8,128)(2,1)} custom-call(s32[4]{0:T(128)S(1)} %pad_add_fusion.place, bf16[768,1536]{1,0:T(8,128)(2,1)} %get-tuple-element.170.h1t_ref, bf16[768,768]{1,0:T(8,128)(2,1)S(1)} %get-tuple-element.171.d_ref, bf16[768,384]{1,0:T(8,128)(2,1)S(1)} %get-tuple-element.147.refs_0_, ...), custom_call_target="tpu_custom_call" | custom-call | flops 1000 | bytes 1000 | tf_op jit(solution)/shard_map/matrix_grads/pallas_call | solution.py:171
  172.0 3.8 %collective-permute-done.22 = bf16[4,192,768]{2,1,0:T(8,128)(2,1)S(1)} collective-permute-done((bf16[4,192,768]{2,1,0:T(8,128)(2,1)S(1)}, bf16[4,192,768]{2,1,0:T(8,128)(2,1)S(1)}, u32[]{:S(2)}, u32[]{:S(2)}) %collective-permute-start.22) | collective-permute-done | bytes 1179680 | tf_op jit(solution)/shard_map/ppermute | solution.py:49
  176.9 1.5 collective-permute-start.23
  178.3 1.7 collective-permute-start.24
  180.2 2.0 collective-permute-start.26
  182.2 7.8 %input_back.1 = (f32[768,768]{1,0:T(8,128)}, bf16[784,768]{1,0:T(8,128)(2,1)S(1)}, f32[16,768]{1,0:T(8,128)S(1)}) custom-call(s32[4]{0:T(128)S(1)} %pad_add_fusion.place, bf16[768,128]{1,0:T(8,128)(2,1)S(1)} %get-tuple-element.174.refs_2_.refs_0_, bf16[1536,128]{1,0:T(8,128)(2,1)S(1)} %get-tuple-element.175.refs_3_.refs_1_, ...), custom_call_target="tpu_custom_call" | custom-call | flops 1000 | bytes 1000 | tf_op jit(solution)/shard_map/input_back/pallas_call | solution.py:171
  190.3 2.1 collective-permute-done.26
  192.7 0.8 collective-permute-start.31
  193.6 3.0 %collective-permute-start.35 = (bf16[192,768]{1,0:T(8,128)(2,1)S(1)}, bf16[192,768]{1,0:T(8,128)(2,1)S(1)}, u32[]{:S(2)}, u32[]{:S(2)}) collective-permute-start(bf16[192,768]{1,0:T(8,128)(2,1)S(1)} %get-tuple-element.238), channel_id=1, source_target_pairs={{0,16},{1,17},{2,18},{3,19},{4,20},{5,21},{6,22},{7,23},{8,24},{9,... | collective-permute-start | bytes 884744 | tf_op jit(solution)/shard_map/ppermute | solution.py:49
  196.7 1.3 collective-permute-start.29
  198.0 10.2 %collective-permute-done.30 = bf16[4,4,48,384]{3,2,1,0:T(8,128)(2,1)S(1)} collective-permute-done((bf16[4,4,48,384]{3,2,1,0:T(8,128)(2,1)S(1)}, bf16[4,4,48,384]{3,2,1,0:T(8,128)(2,1)S(1)}, u32[]{:S(2)}, u32[]{:S(2)}) %collective-permute-start.30) | collective-permute-done | bytes 589856 | tf_op jit(solution)/shard_map/ppermute | solution.py:49
  208.2 0.7 collective-permute-done.31
  210.8 3.8 %collective-permute-start.33 = (bf16[224,384]{1,0:T(8,128)(2,1)S(1)}, bf16[224,384]{1,0:T(8,128)(2,1)S(1)}, u32[]{:S(2)}, u32[]{:S(2)}) collective-permute-start(bf16[224,384]{1,0:T(8,128)(2,1)S(1)} %get-tuple-element.244), channel_id=1, source_target_pairs={{0,16},{1,17},{2,18},{3,19},{4,20},{5,21},{6,22},{7,23},{8,24},{9,... | collective-permute-start | bytes 516104 | tf_op jit(solution)/shard_map/ppermute | solution.py:49
  215.2 1.7 last_ff.1
  216.9 1.0 fusion.13
  217.9 7.8 %collective-permute-done.33 = bf16[224,384]{1,0:T(8,128)(2,1)S(1)} collective-permute-done((bf16[224,384]{1,0:T(8,128)(2,1)S(1)}, bf16[224,384]{1,0:T(8,128)(2,1)S(1)}, u32[]{:S(2)}, u32[]{:S(2)}) %collective-permute-start.33) | collective-permute-done | bytes 172064 | tf_op jit(solution)/shard_map/ppermute | solution.py:49
  225.7 3.5 %collective-permute-done.34 = bf16[224,384]{1,0:T(8,128)(2,1)S(1)} collective-permute-done((bf16[224,384]{1,0:T(8,128)(2,1)S(1)}, bf16[224,384]{1,0:T(8,128)(2,1)S(1)}, u32[]{:S(2)}, u32[]{:S(2)}) %collective-permute-start.34) | collective-permute-done | bytes 172064 | tf_op jit(solution)/shard_map/ppermute | solution.py:49
  229.4 1.8 collective-permute-start.38
  231.2 4.1 %finish.1 = f32[384,768]{1,0:T(8,128)} custom-call(s32[4]{0:T(128)S(1)} %pad_add_fusion.place, f32[768,768]{1,0:T(8,128)} %get-tuple-element.184.refs_0_, bf16[784,768]{1,0:T(8,128)(2,1)S(1)} %collective-permute-done.27.refs_1_, bf16[384,768]{1,0:T(8,128)(2,1)S(1)} %collective-permute-done.29.refs_2_, bf16[1536,768]{1,0:T(8,128)(2,1)} %get-tuple-element.181.refs_7_.refs_3_, ...), custom_call_target="tpu_custom_call" | custom-call | flops 1000 | bytes 1000 | tf_op jit(solution)/shard_map/finish/pallas_call | solution.py:171
  235.3 1.3 collective-permute-start.39
  236.6 2.9 %collective-permute-done.39 = f32[32,384]{1,0:T(8,128)S(1)} collective-permute-done((f32[32,384]{1,0:T(8,128)S(1)}, f32[32,384]{1,0:T(8,128)S(1)}, u32[]{:S(2)}, u32[]{:S(2)}) %collective-permute-start.39) | collective-permute-done | bytes 49184 | tf_op jit(solution)/shard_map/ppermute | solution.py:49
  239.5 1.8 last_rest.1
  (207 shorter events, 15.4 us)
Async XLA Ops:
  7.2 5.4 %copy-start.26 = (bf16[48]{0:T(256)(128)(2,1)S(1)}, bf16[48]{0:T(256)(128)(2,1)}, u32[]{:S(2)}) copy-start(bf16[48]{0:T(256)(128)(2,1)} %param.24) | copy-start | bytes 292
  7.2 5.4 %copy-start.27 = (bf16[24]{0:T(256)(128)(2,1)S(1)}, bf16[24]{0:T(256)(128)(2,1)}, u32[]{:S(2)}) copy-start(bf16[24]{0:T(256)(128)(2,1)} %param.32) | copy-start | bytes 148
  7.2 5.5 %copy-start.28 = (bf16[24]{0:T(256)(128)(2,1)S(1)}, bf16[24]{0:T(256)(128)(2,1)}, u32[]{:S(2)}) copy-start(bf16[24]{0:T(256)(128)(2,1)} %param.28) | copy-start | bytes 148
  7.2 5.6 %copy-start.29 = (bf16[24]{0:T(256)(128)(2,1)S(1)}, bf16[24]{0:T(256)(128)(2,1)}, u32[]{:S(2)}) copy-start(bf16[24]{0:T(256)(128)(2,1)} %param.27) | copy-start | bytes 148
  7.2 5.7 %copy-start.30 = (bf16[24]{0:T(256)(128)(2,1)S(1)}, bf16[24]{0:T(256)(128)(2,1)}, u32[]{:S(2)}) copy-start(bf16[24]{0:T(256)(128)(2,1)} %param.26) | copy-start | bytes 148
  7.2 5.8 %copy-start.31 = (bf16[24]{0:T(256)(128)(2,1)S(1)}, bf16[24]{0:T(256)(128)(2,1)}, u32[]{:S(2)}) copy-start(bf16[24]{0:T(256)(128)(2,1)} %param.22) | copy-start | bytes 148
  7.3 5.8 %copy-start.32 = (bf16[24]{0:T(256)(128)(2,1)S(1)}, bf16[24]{0:T(256)(128)(2,1)}, u32[]{:S(2)}) copy-start(bf16[24]{0:T(256)(128)(2,1)} %param.21) | copy-start | bytes 148
  7.3 93.2 %all-gather.3.cloned.1.call-start = ((), (), s32[]{:S(2)}) async-start(), calls=%async_computation.1 | async-start | bytes 6082560 | tf_op jit(solution)/shard_map/all_gather | solution.py:1106
  9.0 5.0 %copy-start.33 = (bf16[96]{0:T(256)(128)(2,1)S(1)}, bf16[96]{0:T(256)(128)(2,1)}, u32[]{:S(2)}) copy-start(bf16[96]{0:T(256)(128)(2,1)} %param.30) | copy-start | bytes 580
  9.0 5.0 %copy-start.25 = (s32[1,384]{1,0:T(1,128)S(1)}, s32[1,384]{1,0:T(1,128)}, u32[]{:S(2)}) copy-start(s32[1,384]{1,0:T(1,128)} %param.20) | copy-start | bytes 4612
  9.0 5.0 %copy-start.21 = (bf16[1,384,768]{2,1,0:T(8,128)(2,1)S(1)}, bf16[1,384,768]{2,1,0:T(8,128)(2,1)}, u32[]{:S(2)}) copy-start(bf16[1,384,768]{2,1,0:T(8,128)(2,1)} %param.19) | copy-start | bytes 1769476
  11.7 4.8 %collective-permute-start.6 = (bf16[24,1536]{1,0:T(8,128)(2,1)S(1)}, bf16[24,1536]{1,0:T(8,128)(2,1)S(1)}, u32[]{:S(2)}, u32[]{:S(2)}) collective-permute-start(bf16[24,1536]{1,0:T(8,128)(2,1)S(1)} %reshape.218), channel_id=1, source_target_pairs={{0,1},{1,0},{2,3},{3,2},{4,5},{5,4},{6,7},{7,6},{8,9},{9,8},{10,11... | collective-permute-start | bytes 221192 | tf_op jit(solution)/shard_map/ppermute | solution.py:49
  13.2 1.5 collective-permute-start
  14.8 21.2 %collective-permute-start.4 = (bf16[400,768]{1,0:T(8,128)(2,1)S(1)}, bf16[400,768]{1,0:T(8,128)(2,1)S(1)}, u32[]{:S(2)}, u32[]{:S(2)}) collective-permute-start(bf16[400,768]{1,0:T(8,128)(2,1)S(1)} %fusion.11), channel_id=1, source_target_pairs={{0,2},{1,3},{2,0},{3,1},{4,6},{5,7},{6,4},{7,5},{8,10},{9,11},{10,... | collective-permute-start | bytes 1843208 | tf_op jit(solution)/shard_map/ppermute | solution.py:49
  16.4 19.6 %collective-permute-start.5 = (bf16[400,768]{1,0:T(8,128)(2,1)S(1)}, bf16[400,768]{1,0:T(8,128)(2,1)S(1)}, u32[]{:S(2)}, u32[]{:S(2)}) collective-permute-start(bf16[400,768]{1,0:T(8,128)(2,1)S(1)} %fusion.11), channel_id=1, source_target_pairs={{0,1},{1,0},{2,3},{3,2},{4,5},{5,4},{6,7},{7,6},{8,9},{9,8},{10,11... | collective-permute-start | bytes 1843208 | tf_op jit(solution)/shard_map/ppermute | solution.py:49
  16.5 7.2 %collective-permute-start.1 = (bf16[64,1152]{1,0:T(8,128)(2,1)S(1)}, bf16[64,1152]{1,0:T(8,128)(2,1)S(1)}, u32[]{:S(2)}, u32[]{:S(2)}) collective-permute-start(bf16[64,1152]{1,0:T(8,128)(2,1)S(1)} %fusion.21), channel_id=1, source_target_pairs={{0,8},{1,9},{2,10},{3,11},{4,12},{5,13},{6,14},{7,15},{8,16},{9,17... | collective-permute-start | bytes 442376 | tf_op jit(solution)/shard_map/ppermute | solution.py:49
  18.1 16.6 %collective-permute-start.2 = (bf16[64,1152]{1,0:T(8,128)(2,1)S(1)}, bf16[64,1152]{1,0:T(8,128)(2,1)S(1)}, u32[]{:S(2)}, u32[]{:S(2)}) collective-permute-start(bf16[64,1152]{1,0:T(8,128)(2,1)S(1)} %fusion.21), channel_id=1, source_target_pairs={{0,16},{1,17},{2,18},{3,19},{4,20},{5,21},{6,22},{7,23},{8,24},{9,... | collective-permute-start | bytes 442376 | tf_op jit(solution)/shard_map/ppermute | solution.py:49
  19.4 16.6 %collective-permute-start.3 = (bf16[64,1152]{1,0:T(8,128)(2,1)S(1)}, bf16[64,1152]{1,0:T(8,128)(2,1)S(1)}, u32[]{:S(2)}, u32[]{:S(2)}) collective-permute-start(bf16[64,1152]{1,0:T(8,128)(2,1)S(1)} %fusion.21), channel_id=1, source_target_pairs={{0,24},{1,25},{2,26},{3,27},{4,28},{5,29},{6,30},{7,31},{8,0},{9,1... | collective-permute-start | bytes 442376 | tf_op jit(solution)/shard_map/ppermute | solution.py:49
  23.7 21.1 %collective-permute-start.10 = (bf16[384,768]{1,0:T(8,128)(2,1)}, bf16[384,768]{1,0:T(8,128)(2,1)}, u32[]{:S(2)}, u32[]{:S(2)}) collective-permute-start(bf16[384,768]{1,0:T(8,128)(2,1)} %bitcast.23), channel_id=1, source_target_pairs={{0,1},{1,0},{2,3},{3,2},{4,5},{5,4},{6,7},{7,6},{8,9},{9,8},{10,11... | collective-permute-start | bytes 1769480 | tf_op jit(solution)/shard_map/ppermute | solution.py:49
  36.0 21.7 %collective-permute-start.9 = (bf16[400,768]{1,0:T(8,128)(2,1)S(1)}, bf16[400,768]{1,0:T(8,128)(2,1)}, u32[]{:S(2)}, u32[]{:S(2)}) collective-permute-start(bf16[400,768]{1,0:T(8,128)(2,1)S(1)} %collective-permute-done.4), channel_id=1, source_target_pairs={{0,1},{1,0},{2,3},{3,2},{4,5},{5,4},{6,7},{7,6},{8,9},{9,8},{10,11... | collective-permute-start | bytes 1843208 | tf_op jit(solution)/shard_map/ppermute | solution.py:49
  37.0 20.7 %copy-start.10 = (bf16[4,64,1152]{2,1,0:T(8,128)(2,1)}, bf16[4,64,1152]{2,1,0:T(8,128)(2,1)S(1)}, u32[]{:S(2)}) copy-start(bf16[4,64,1152]{2,1,0:T(8,128)(2,1)S(1)} %pad_maximum_fusion.4.refs_0_) | copy-start | bytes 1769476
  37.0 20.7 %collective-permute-start.7 = (bf16[4,64,1152]{2,1,0:T(8,128)(2,1)S(1)}, bf16[4,64,1152]{2,1,0:T(8,128)(2,1)S(1)}, u32[]{:S(2)}, u32[]{:S(2)}) collective-permute-start(bf16[4,64,1152]{2,1,0:T(8,128)(2,1)S(1)} %pad_maximum_fusion.4.refs_0_), channel_id=1, source_target_pairs={{0,4},{1,5},{2,6},{3,7},{4,0},{5,1},{6,2},{7,3},{8,12},{9,13},{10,... | collective-permute-start | bytes 1769480 | tf_op jit(solution)/shard_map/ppermute | solution.py:49
  37.6 20.1 %collective-permute-start.8 = (bf16[4,64,1152]{2,1,0:T(8,128)(2,1)S(1)}, bf16[4,64,1152]{2,1,0:T(8,128)(2,1)S(1)}, u32[]{:S(2)}, u32[]{:S(2)}) collective-permute-start(bf16[4,64,1152]{2,1,0:T(8,128)(2,1)S(1)} %pad_maximum_fusion.4.refs_0_), channel_id=1, source_target_pairs={{0,2},{1,3},{2,0},{3,1},{4,6},{5,7},{6,4},{7,5},{8,10},{9,11},{10,... | collective-permute-start | bytes 1769480 | tf_op jit(solution)/shard_map/ppermute | solution.py:49
  39.1 41.5 %all-to-all-start = ((bf16[4,96,768]{2,1,0:T(8,128)(2,1)}), bf16[4,96,768]{2,1,0:T(8,128)(2,1)}, u32[]{:S(2)}, u32[]{:S(2)}) async-start(bf16[4,96,768]{2,1,0:T(8,128)(2,1)} %broadcast_in_dim.35), calls=%async_computation | async-start | bytes 1179648 | tf_op jit(solution)/shard_map/all_to_all | solution.py:137
  44.7 14.6 %copy-start.17 = (bf16[400,768]{1,0:T(8,128)(2,1)S(1)}, bf16[400,768]{1,0:T(8,128)(2,1)}, u32[]{:S(2)}) copy-start(bf16[400,768]{1,0:T(8,128)(2,1)} %copy-done.16) | copy-start | bytes 1843204
  44.7 14.6 %copy-start.19 = (bf16[400,768]{1,0:T(8,128)(2,1)S(1)}, bf16[400,768]{1,0:T(8,128)(2,1)}, u32[]{:S(2)}) copy-start(bf16[400,768]{1,0:T(8,128)(2,1)} %copy-done.18) | copy-start | bytes 1843204
  60.6 8.6 %collective-permute-start.11 = (bf16[2,64,1152]{2,1,0:T(8,128)(2,1)}, bf16[2,64,1152]{2,1,0:T(8,128)(2,1)S(1)}, u32[]{:S(2)}, u32[]{:S(2)}) collective-permute-start(bf16[2,64,1152]{2,1,0:T(8,128)(2,1)} %slice.267), channel_id=1, source_target_pairs={{0,2},{1,3},{2,0},{3,1},{4,6},{5,7},{6,4},{7,5},{8,10},{9,11},{10,... | collective-permute-start | bytes 884744 | tf_op jit(solution)/shard_map/ppermute | solution.py:49
  61.2 8.2 %collective-permute-start.12 = (bf16[2,64,1152]{2,1,0:T(8,128)(2,1)}, bf16[2,64,1152]{2,1,0:T(8,128)(2,1)S(1)}, u32[]{:S(2)}, u32[]{:S(2)}) collective-permute-start(bf16[2,64,1152]{2,1,0:T(8,128)(2,1)} %slice.269), channel_id=1, source_target_pairs={{0,4},{1,5},{2,6},{3,7},{4,0},{5,1},{6,2},{7,3},{8,12},{9,13},{10,... | collective-permute-start | bytes 884744 | tf_op jit(solution)/shard_map/ppermute | solution.py:49
  80.6 15.4 %collective-permute-start.14 = (bf16[4,96,768]{2,1,0:T(8,128)(2,1)}, bf16[4,96,768]{2,1,0:T(8,128)(2,1)S(1)}, u32[]{:S(2)}, u32[]{:S(2)}) collective-permute-start(bf16[4,96,768]{2,1,0:T(8,128)(2,1)} %all-to-all-done.refs_0_), channel_id=1, source_target_pairs={{0,4},{1,5},{2,6},{3,7},{4,0},{5,1},{6,2},{7,3},{8,12},{9,13},{10,... | collective-permute-start | bytes 1769480 | tf_op jit(solution)/shard_map/ppermute | solution.py:49
  80.9 15.1 %collective-permute-start.15 = (bf16[4,96,768]{2,1,0:T(8,128)(2,1)}, bf16[4,96,768]{2,1,0:T(8,128)(2,1)S(1)}, u32[]{:S(2)}, u32[]{:S(2)}) collective-permute-start(bf16[4,96,768]{2,1,0:T(8,128)(2,1)} %all-to-all-done.refs_0_), channel_id=1, source_target_pairs={{0,2},{1,3},{2,0},{3,1},{4,6},{5,7},{6,4},{7,5},{8,10},{9,11},{10,... | collective-permute-start | bytes 1769480 | tf_op jit(solution)/shard_map/ppermute | solution.py:49
  96.0 5.9 %collective-permute-start.13 = (bf16[768,384]{1,0:T(8,128)(2,1)S(1)}, bf16[768,384]{1,0:T(8,128)(2,1)}, u32[]{:S(2)}, u32[]{:S(2)}) collective-permute-start(bf16[768,384]{1,0:T(8,128)(2,1)S(1)} %get-tuple-element.147.refs_0_), channel_id=1, source_target_pairs={{0,1},{1,0},{2,3},{3,2},{4,5},{5,4},{6,7},{7,6},{8,9},{9,8},{10,11... | collective-permute-start | bytes 1769480 | tf_op jit(solution)/shard_map/ppermute | solution.py:49
  97.6 9.7 %collective-permute-start.16 = (bf16[2,96,768]{2,1,0:T(8,128)(2,1)}, bf16[2,96,768]{2,1,0:T(8,128)(2,1)}, u32[]{:S(2)}, u32[]{:S(2)}) collective-permute-start(bf16[2,96,768]{2,1,0:T(8,128)(2,1)} %slice.274), channel_id=1, source_target_pairs={{0,2},{1,3},{2,0},{3,1},{4,6},{5,7},{6,4},{7,5},{8,10},{9,11},{10,... | collective-permute-start | bytes 884744 | tf_op jit(solution)/shard_map/ppermute | solution.py:49
  98.9 9.3 %collective-permute-start.17 = (bf16[2,96,768]{2,1,0:T(8,128)(2,1)}, bf16[2,96,768]{2,1,0:T(8,128)(2,1)}, u32[]{:S(2)}, u32[]{:S(2)}) collective-permute-start(bf16[2,96,768]{2,1,0:T(8,128)(2,1)} %slice.275), channel_id=1, source_target_pairs={{0,4},{1,5},{2,6},{3,7},{4,0},{5,1},{6,2},{7,3},{8,12},{9,13},{10,... | collective-permute-start | bytes 884744 | tf_op jit(solution)/shard_map/ppermute | solution.py:49
  128.9 5.5 %collective-permute-start.18 = (bf16[768,768]{1,0:T(8,128)(2,1)S(1)}, bf16[768,768]{1,0:T(8,128)(2,1)S(1)}, u32[]{:S(2)}, u32[]{:S(2)}) collective-permute-start(bf16[768,768]{1,0:T(8,128)(2,1)S(1)} %get-tuple-element.155), channel_id=1, source_target_pairs={{0,1},{1,0},{2,3},{3,2},{4,5},{5,4},{6,7},{7,6},{8,9},{9,8},{10,11... | collective-permute-start | bytes 3538952 | tf_op jit(solution)/shard_map/ppermute | solution.py:49
  129.0 5.4 %copy-start = (bf16[2,384,768]{2,1,0:T(8,128)(2,1)S(1)}, bf16[2,384,768]{2,1,0:T(8,128)(2,1)}, u32[]{:S(2)}) copy-start(bf16[2,384,768]{2,1,0:T(8,128)(2,1)} %pad_maximum_fusion.1) | copy-start | bytes 3538948
  129.0 5.4 %copy-start.3 = (bf16[768,768]{1,0:T(8,128)(2,1)S(1)}, bf16[768,768]{1,0:T(8,128)(2,1)}, u32[]{:S(2)}) copy-start(bf16[768,768]{1,0:T(8,128)(2,1)} %get-tuple-element.156.n2_ref) | copy-start | bytes 3538948
  129.0 5.4 %copy-start.5 = (f32[768,128]{1,0:T(8,128)S(1)}, f32[768,128]{1,0:T(8,128)}, u32[]{:S(2)}) copy-start(f32[768,128]{1,0:T(8,128)} %get-tuple-element.157.rstd_ref) | copy-start | bytes 1179652
  129.0 19.0 %slice-start = ((s8[4718592]{0:T(1024)(128)(4,1)}), s8[4194304]{0:T(1024)(128)(4,1)S(1)}, s32[]{:S(2)}) async-start(s8[4718592]{0:T(1024)(128)(4,1)} %bitcast.167), calls=%async_computation.2 | async-start | bytes 8388608
  130.9 15.8 %collective-permute-start.19 = (bf16[2,192,768]{2,1,0:T(8,128)(2,1)S(1)}, bf16[2,192,768]{2,1,0:T(8,128)(2,1)S(1)}, u32[]{:S(2)}, u32[]{:S(2)}) collective-permute-start(bf16[2,192,768]{2,1,0:T(8,128)(2,1)S(1)} %get-tuple-element.226), channel_id=1, source_target_pairs={{0,2},{1,3},{2,0},{3,1},{4,6},{5,7},{6,4},{7,5},{8,10},{9,11},{10,... | collective-permute-start | bytes 1769480 | tf_op jit(solution)/shard_map/ppermute | solution.py:49
  132.6 15.4 %collective-permute-start.20 = (bf16[2,192,768]{2,1,0:T(8,128)(2,1)S(1)}, bf16[2,192,768]{2,1,0:T(8,128)(2,1)S(1)}, u32[]{:S(2)}, u32[]{:S(2)}) collective-permute-start(bf16[2,192,768]{2,1,0:T(8,128)(2,1)S(1)} %get-tuple-element.224), channel_id=1, source_target_pairs={{0,4},{1,5},{2,6},{3,7},{4,0},{5,1},{6,2},{7,3},{8,12},{9,13},{10,... | collective-permute-start | bytes 1769480 | tf_op jit(solution)/shard_map/ppermute | solution.py:49
  134.4 13.7 %slice-start.1 = ((s8[4718592]{0:T(1024)(128)(4,1)}), s8[524288]{0:T(1024)(128)(4,1)S(1)}, s32[]{:S(2)}) async-start(s8[4718592]{0:T(1024)(128)(4,1)} %bitcast.167), calls=%async_computation.3 | async-start | bytes 1048576
  148.5 27.3 %collective-permute-start.22 = (bf16[4,192,768]{2,1,0:T(8,128)(2,1)S(1)}, bf16[4,192,768]{2,1,0:T(8,128)(2,1)S(1)}, u32[]{:S(2)}, u32[]{:S(2)}) collective-permute-start(bf16[4,192,768]{2,1,0:T(8,128)(2,1)S(1)} %pad_maximum_fusion.3), channel_id=1, source_target_pairs={{0,2},{1,3},{2,0},{3,1},{4,6},{5,7},{6,4},{7,5},{8,10},{9,11},{10,... | collective-permute-start | bytes 3538952 | tf_op jit(solution)/shard_map/ppermute | solution.py:49
  149.0 27.2 %collective-permute-start.21 = (bf16[4,192,768]{2,1,0:T(8,128)(2,1)S(1)}, bf16[4,192,768]{2,1,0:T(8,128)(2,1)S(1)}, u32[]{:S(2)}, u32[]{:S(2)}) collective-permute-start(bf16[4,192,768]{2,1,0:T(8,128)(2,1)S(1)} %pad_maximum_fusion.2), channel_id=1, source_target_pairs={{0,4},{1,5},{2,6},{3,7},{4,0},{5,1},{6,2},{7,3},{8,12},{9,13},{10,... | collective-permute-start | bytes 3538952 | tf_op jit(solution)/shard_map/ppermute | solution.py:49
  176.9 13.1 %collective-permute-start.23 = (bf16[2,4,48,384]{3,2,1,0:T(8,128)(2,1)S(1)}, bf16[2,4,48,384]{3,2,1,0:T(8,128)(2,1)S(1)}, u32[]{:S(2)}, u32[]{:S(2)}) collective-permute-start(bf16[2,4,48,384]{3,2,1,0:T(8,128)(2,1)S(1)} %get-tuple-element.232), channel_id=1, source_target_pairs={{0,2},{1,3},{2,0},{3,1},{4,6},{5,7},{6,4},{7,5},{8,10},{9,11},{10,... | collective-permute-start | bytes 884744 | tf_op jit(solution)/shard_map/ppermute | solution.py:49
  178.3 11.6 %collective-permute-start.24 = (bf16[2,4,48,384]{3,2,1,0:T(8,128)(2,1)S(1)}, bf16[2,4,48,384]{3,2,1,0:T(8,128)(2,1)S(1)}, u32[]{:S(2)}, u32[]{:S(2)}) collective-permute-start(bf16[2,4,48,384]{3,2,1,0:T(8,128)(2,1)S(1)} %get-tuple-element.230), channel_id=1, source_target_pairs={{0,4},{1,5},{2,6},{3,7},{4,0},{5,1},{6,2},{7,3},{8,12},{9,13},{10,... | collective-permute-start | bytes 884744 | tf_op jit(solution)/shard_map/ppermute | solution.py:49
  180.1 10.2 %collective-permute-start.25 = (bf16[192,768]{1,0:T(8,128)(2,1)S(1)}, bf16[192,768]{1,0:T(8,128)(2,1)S(1)}, u32[]{:S(2)}, u32[]{:S(2)}) collective-permute-start(bf16[192,768]{1,0:T(8,128)(2,1)S(1)} %get-tuple-element.240), channel_id=1, source_target_pairs={{0,8},{1,9},{2,10},{3,11},{4,12},{5,13},{6,14},{7,15},{8,16},{9,17... | collective-permute-start | bytes 884744 | tf_op jit(solution)/shard_map/ppermute | solution.py:49
  180.2 12.2 %collective-permute-start.26 = (bf16[192,768]{1,0:T(8,128)(2,1)S(1)}, bf16[192,768]{1,0:T(8,128)(2,1)S(1)}, u32[]{:S(2)}, u32[]{:S(2)}) collective-permute-start(bf16[192,768]{1,0:T(8,128)(2,1)S(1)} %get-tuple-element.239), channel_id=1, source_target_pairs={{0,24},{1,25},{2,26},{3,27},{4,28},{5,29},{6,30},{7,31},{8,0},{9,1... | collective-permute-start | bytes 884744 | tf_op jit(solution)/shard_map/ppermute | solution.py:49
  190.1 6.4 %copy-start.9 = (f32[768,768]{1,0:T(8,128)S(1)}, f32[768,768]{1,0:T(8,128)}, u32[]{:S(2)}) copy-start(f32[768,768]{1,0:T(8,128)} %get-tuple-element.184.refs_0_) | copy-start | bytes 7077892
  192.4 4.1 %collective-permute-start.27 = (bf16[784,768]{1,0:T(8,128)(2,1)S(1)}, bf16[784,768]{1,0:T(8,128)(2,1)S(1)}, u32[]{:S(2)}, u32[]{:S(2)}) collective-permute-start(bf16[784,768]{1,0:T(8,128)(2,1)S(1)} %get-tuple-element.190), channel_id=1, source_target_pairs={{0,1},{1,0},{2,3},{3,2},{4,5},{5,4},{6,7},{7,6},{8,9},{9,8},{10,11... | collective-permute-start | bytes 3612680 | tf_op jit(solution)/shard_map/ppermute | solution.py:49
  192.4 15.7 %collective-permute-start.30 = (bf16[4,4,48,384]{3,2,1,0:T(8,128)(2,1)S(1)}, bf16[4,4,48,384]{3,2,1,0:T(8,128)(2,1)S(1)}, u32[]{:S(2)}, u32[]{:S(2)}) collective-permute-start(bf16[4,4,48,384]{3,2,1,0:T(8,128)(2,1)S(1)} %pad_maximum_fusion.5), channel_id=1, source_target_pairs={{0,4},{1,5},{2,6},{3,7},{4,0},{5,1},{6,2},{7,3},{8,12},{9,13},{10,... | collective-permute-start | bytes 1769480 | tf_op jit(solution)/shard_map/ppermute | solution.py:49
  192.7 16.2 %collective-permute-start.31 = (bf16[4,4,48,384]{3,2,1,0:T(8,128)(2,1)S(1)}, bf16[4,4,48,384]{3,2,1,0:T(8,128)(2,1)S(1)}, u32[]{:S(2)}, u32[]{:S(2)}) collective-permute-start(bf16[4,4,48,384]{3,2,1,0:T(8,128)(2,1)S(1)} %pad_maximum_fusion.6), channel_id=1, source_target_pairs={{0,2},{1,3},{2,0},{3,1},{4,6},{5,7},{6,4},{7,5},{8,10},{9,11},{10,... | collective-permute-start | bytes 1769480 | tf_op jit(solution)/shard_map/ppermute | solution.py:49
  193.6 15.5 %collective-permute-start.35 = (bf16[192,768]{1,0:T(8,128)(2,1)S(1)}, bf16[192,768]{1,0:T(8,128)(2,1)S(1)}, u32[]{:S(2)}, u32[]{:S(2)}) collective-permute-start(bf16[192,768]{1,0:T(8,128)(2,1)S(1)} %get-tuple-element.238), channel_id=1, source_target_pairs={{0,16},{1,17},{2,18},{3,19},{4,20},{5,21},{6,22},{7,23},{8,24},{9,... | collective-permute-start | bytes 884744 | tf_op jit(solution)/shard_map/ppermute | solution.py:49
  196.7 34.5 %collective-permute-start.29 = (bf16[384,768]{1,0:T(8,128)(2,1)S(1)}, bf16[384,768]{1,0:T(8,128)(2,1)S(1)}, u32[]{:S(2)}, u32[]{:S(2)}) collective-permute-start(bf16[384,768]{1,0:T(8,128)(2,1)S(1)} %add_convert_fusion), channel_id=1, source_target_pairs={{0,2},{1,3},{2,0},{3,1},{4,6},{5,7},{6,4},{7,5},{8,10},{9,11},{10,... | collective-permute-start | bytes 1769480 | tf_op jit(solution)/shard_map/ppermute | solution.py:49
  198.0 11.1 %copy-start.13 = (f32[768,768]{1,0:T(8,128)S(1)}, f32[768,768]{1,0:T(8,128)}, u32[]{:S(2)}) copy-start(f32[768,768]{1,0:T(8,128)} %get-tuple-element.191) | copy-start | bytes 7077892
  209.2 7.6 %collective-permute-start.28 = (bf16[384,768]{1,0:T(8,128)(2,1)S(1)}, bf16[384,768]{1,0:T(8,128)(2,1)S(1)}, u32[]{:S(2)}, u32[]{:S(2)}) collective-permute-start(bf16[384,768]{1,0:T(8,128)(2,1)S(1)} %fusion.12), channel_id=1, source_target_pairs={{0,1},{1,0},{2,3},{3,2},{4,5},{5,4},{6,7},{7,6},{8,9},{9,8},{10,11... | collective-permute-start | bytes 1769480 | tf_op jit(solution)/shard_map/ppermute | solution.py:49
  209.5 7.4 %copy-start.20 = (f32[768,768]{1,0:T(8,128)S(1)}, f32[768,768]{1,0:T(8,128)}, u32[]{:S(2)}) copy-start(f32[768,768]{1,0:T(8,128)} %get-tuple-element.192) | copy-start | bytes 7077892
  209.5 5.1 %collective-permute-start.36 = (bf16[96,768]{1,0:T(8,128)(2,1)S(1)}, bf16[96,768]{1,0:T(8,128)(2,1)S(1)}, u32[]{:S(2)}, u32[]{:S(2)}) collective-permute-start(bf16[96,768]{1,0:T(8,128)(2,1)S(1)} %slice.393), channel_id=1, source_target_pairs={{0,1},{1,0},{2,3},{3,2},{4,5},{5,4},{6,7},{7,6},{8,9},{9,8},{10,11... | collective-permute-start | bytes 442376 | tf_op jit(solution)/shard_map/ppermute | solution.py:49
  210.1 7.7 %collective-permute-start.32 = (bf16[224,384]{1,0:T(8,128)(2,1)S(1)}, bf16[224,384]{1,0:T(8,128)(2,1)S(1)}, u32[]{:S(2)}, u32[]{:S(2)}) collective-permute-start(bf16[224,384]{1,0:T(8,128)(2,1)S(1)} %get-tuple-element.245), channel_id=1, source_target_pairs={{0,8},{1,9},{2,10},{3,11},{4,12},{5,13},{6,14},{7,15},{8,16},{9,17... | collective-permute-start | bytes 516104 | tf_op jit(solution)/shard_map/ppermute | solution.py:49
  210.8 14.9 %collective-permute-start.33 = (bf16[224,384]{1,0:T(8,128)(2,1)S(1)}, bf16[224,384]{1,0:T(8,128)(2,1)S(1)}, u32[]{:S(2)}, u32[]{:S(2)}) collective-permute-start(bf16[224,384]{1,0:T(8,128)(2,1)S(1)} %get-tuple-element.244), channel_id=1, source_target_pairs={{0,16},{1,17},{2,18},{3,19},{4,20},{5,21},{6,22},{7,23},{8,24},{9,... | collective-permute-start | bytes 516104 | tf_op jit(solution)/shard_map/ppermute | solution.py:49
  214.6 14.6 %collective-permute-start.34 = (bf16[224,384]{1,0:T(8,128)(2,1)S(1)}, bf16[224,384]{1,0:T(8,128)(2,1)S(1)}, u32[]{:S(2)}, u32[]{:S(2)}) collective-permute-start(bf16[224,384]{1,0:T(8,128)(2,1)S(1)} %get-tuple-element.243), channel_id=1, source_target_pairs={{0,24},{1,25},{2,26},{3,27},{4,28},{5,29},{6,30},{7,31},{8,0},{9,1... | collective-permute-start | bytes 516104 | tf_op jit(solution)/shard_map/ppermute | solution.py:49
  217.9 13.4 %copy-start.4 = (f32[1536,1]{1,0:T(8,128)S(1)}, f32[1536,1]{1,0:T(8,128)}, u32[]{:S(2)}) copy-start(f32[1536,1]{1,0:T(8,128)} %get-tuple-element.193.refs_4_) | copy-start | bytes 18436
  229.3 10.2 %collective-permute-start.37 = (bf16[4,48,384]{2,1,0:T(8,128)(2,1)S(1)}, bf16[4,48,384]{2,1,0:T(8,128)(2,1)S(1)}, u32[]{:S(2)}, u32[]{:S(2)}) collective-permute-start(bf16[4,48,384]{2,1,0:T(8,128)(2,1)S(1)} %get-tuple-element.220), channel_id=1, source_target_pairs={{0,1},{1,0},{2,3},{3,2},{4,5},{5,4},{6,7},{7,6},{8,9},{9,8},{10,11... | collective-permute-start | bytes 442376 | tf_op jit(solution)/shard_map/ppermute | solution.py:49
  229.4 5.9 %collective-permute-start.38 = (f32[32,384]{1,0:T(8,128)S(1)}, f32[32,384]{1,0:T(8,128)S(1)}, u32[]{:S(2)}, u32[]{:S(2)}) collective-permute-start(f32[32,384]{1,0:T(8,128)S(1)} %convert_add_fusion.10), channel_id=1, source_target_pairs={{0,4},{1,5},{2,6},{3,7},{4,0},{5,1},{6,2},{7,3},{8,12},{9,13},{10,... | collective-permute-start | bytes 147464 | tf_op jit(solution)/shard_map/ppermute | solution.py:49
  235.3 4.2 %collective-permute-start.39 = (f32[32,384]{1,0:T(8,128)S(1)}, f32[32,384]{1,0:T(8,128)S(1)}, u32[]{:S(2)}, u32[]{:S(2)}) collective-permute-start(f32[32,384]{1,0:T(8,128)S(1)} %add.206), channel_id=1, source_target_pairs={{0,2},{1,3},{2,0},{3,1},{4,6},{5,7},{6,4},{7,5},{8,10},{9,11},{10,... | collective-permute-start | bytes 147464 | tf_op jit(solution)/shard_map/ppermute | solution.py:49
  (14 other events, 28.8 us)
Sparse Core Ops, SparseCore 0:
  11.6 86.1 all-gather.2

commit v4 on v3

--- a/solution.py
+++ b/solution.py
@@ -788,7 +788,7 @@
     return call(
         functools.partial(finish_kernel, len(sides)),
         grid.place,
-        [hbm(mine), got] + sides + [hbm(n1), rstd1, hbm(d_after), vec],
+        [hbm(mine), got] + sides + [n1, rstd1, hbm(d_after), vec],
         grid=(1,),
         in_specs=[first, first]
         + [pl.BlockSpec((rows, width), lambda i, s: (0, 0))] * len(sides)
@@ -1217,8 +1217,8 @@
         own, vectors = lock(own, vectors)
         vectors = jnp.broadcast_to(vectors, (grid.z,) + vectors.shape)
         w_up_g, w_down_g = last_ff(grid, ff, swap(ff[per_chip:].astype(bf16)), shard)
-        own, vectors = grid.column_near(own, vectors, (output, w_up_g))
-        vectors = vectors + behind(grid.shift(vectors, "x", 1), input_grad)
+        own, vectors = grid.column_near(own, vectors, (output, w_up_g, input_grad))
+        vectors = vectors + grid.shift(vectors, "x", 1)
         vectors = vectors + sum(grid.along(vectors, "q"))
         w_qkv_g, w_out_g, six, qv_g, up_g = last_rest(
             grid, own, swap(own.astype(bf16)), vectors, shard, per_chip

time: 254 us -> 253 us (level)
  the two profiles are of different devices: /device:TPU:10 before, /device:TPU:0 now
where the time goes in v4:
time: 253 us; the launch traced here: 248 us
  Pallas kernels  97 us (38%)
  waiting for transfers between devices  63.2 us (25%)
  starting transfers between devices  47.5 us (19%)
  between operations  15.2 us (6%)
  local copies, waits for them, and re-layouts  14.8 us (6%)
  other arithmetic  10.3 us (4%)
    pallas_call x11, Pallas kernels, call(): pl.pallas_call(kernel, grid_spec=spec, compiler_params=pltpu.CompilerPara...  63.5 us
    ppermute x40, waiting for transfers between devices, shift(): return lax.ppermute(value, AXES, pairs)  63.2 us
    ppermute x40, starting transfers between devices, shift(): return lax.ppermute(value, AXES, pairs)  39.7 us
    pallas_call x2, Pallas kernels, attn_bwd(): pl.pallas_call(attn_bwd_kernel, grid=(pairs, rows // block), in_specs=[by...  21 us
    pallas_call x1, Pallas kernels, attn_fwd(): pl.pallas_call(attn_fwd_kernel, grid=(pairs, rows // block), in_specs=[pl...  12.5 us
    all_to_all x1, starting transfers between devices, exchange(): lax.all_to_all(blocks, AXES, 0, 0, axis_index_groups=self.groups(('z',)),...  7.77 us
  transfers between devices with their start and end apart: 42, of which 20 were waited for; matrix products, arithmetic and copies ran while one was open for 8% of the time, Pallas kernels for 30%

profile of v4, /device:TPU:0, one launch (start us, length us, event | category | flops | bytes accessed | tf_op | source)
XLA Modules:
  0.0 248.1 jit_solution(12263836538339986506)
XLA Ops:
  7.3 1.7 pad_maximum_fusion.7
  9.0 1.2 reshape.216
  10.2 1.3 dynamic-slice_reduce_fusion.1
  14.1 0.9 collective-permute-done
  15.1 2.7 %collective-permute-start.4 = (bf16[400,768]{1,0:T(8,128)(2,1)S(1)}, bf16[400,768]{1,0:T(8,128)(2,1)S(1)}, u32[]{:S(2)}, u32[]{:S(2)}) collective-permute-start(bf16[400,768]{1,0:T(8,128)(2,1)S(1)} %fusion.11), channel_id=1, source_target_pairs={{0,2},{1,3},{2,0},{3,1},{4,6},{5,7},{6,4},{7,5},{8,10},{9,11},{10,... | collective-permute-start | bytes 1843208 | tf_op jit(solution)/shard_map/ppermute | solution.py:49
  17.9 1.6 collective-permute-start.1
  19.6 2.6 %collective-permute-start.2 = (bf16[64,1152]{1,0:T(8,128)(2,1)S(1)}, bf16[64,1152]{1,0:T(8,128)(2,1)S(1)}, u32[]{:S(2)}, u32[]{:S(2)}) collective-permute-start(bf16[64,1152]{1,0:T(8,128)(2,1)S(1)} %fusion.21), channel_id=1, source_target_pairs={{0,16},{1,17},{2,18},{3,19},{4,20},{5,21},{6,22},{7,23},{8,24},{9,... | collective-permute-start | bytes 442376 | tf_op jit(solution)/shard_map/ppermute | solution.py:49
  22.2 1.3 collective-permute-start.3
  23.5 3.0 %collective-permute-done.1 = bf16[64,1152]{1,0:T(8,128)(2,1)S(1)} collective-permute-done((bf16[64,1152]{1,0:T(8,128)(2,1)S(1)}, bf16[64,1152]{1,0:T(8,128)(2,1)S(1)}, u32[]{:S(2)}, u32[]{:S(2)}) %collective-permute-start.1) | collective-permute-done | bytes 147488 | tf_op jit(solution)/shard_map/ppermute | solution.py:49
  26.5 8.4 %collective-permute-done.2 = bf16[64,1152]{1,0:T(8,128)(2,1)S(1)} collective-permute-done((bf16[64,1152]{1,0:T(8,128)(2,1)S(1)}, bf16[64,1152]{1,0:T(8,128)(2,1)S(1)}, u32[]{:S(2)}, u32[]{:S(2)}) %collective-permute-start.2) | collective-permute-done | bytes 147488 | tf_op jit(solution)/shard_map/ppermute | solution.py:49
  35.0 0.8 copy-done.19
  36.0 1.6 collective-permute-start.7
  38.0 0.9 broadcast_in_dim.35
  38.9 7.8 %all-to-all-start = ((bf16[4,96,768]{2,1,0:T(8,128)(2,1)}), bf16[4,96,768]{2,1,0:T(8,128)(2,1)}, u32[]{:S(2)}, u32[]{:S(2)}) async-start(bf16[4,96,768]{2,1,0:T(8,128)(2,1)} %broadcast_in_dim.35), calls=%async_computation | async-start | bytes 1179648 | tf_op jit(solution)/shard_map/all_to_all | solution.py:137
  46.7 8.9 %collective-permute-done.7.refs_1_ = bf16[4,64,1152]{2,1,0:T(8,128)(2,1)S(1)} collective-permute-done((bf16[4,64,1152]{2,1,0:T(8,128)(2,1)S(1)}, bf16[4,64,1152]{2,1,0:T(8,128)(2,1)S(1)}, u32[]{:S(2)}, u32[]{:S(2)}) %collective-permute-start.7) | collective-permute-done | bytes 589856 | tf_op jit(solution)/shard_map/ppermute | solution.py:49
  55.6 0.8 slice.267
  57.2 1.2 select_bitcast_fusion
  58.6 2.5 %collective-permute-start.12 = (bf16[2,64,1152]{2,1,0:T(8,128)(2,1)}, bf16[2,64,1152]{2,1,0:T(8,128)(2,1)S(1)}, u32[]{:S(2)}, u32[]{:S(2)}) collective-permute-start(bf16[2,64,1152]{2,1,0:T(8,128)(2,1)} %slice.269), channel_id=1, source_target_pairs={{0,4},{1,5},{2,6},{3,7},{4,0},{5,1},{6,2},{7,3},{8,12},{9,13},{10,... | collective-permute-start | bytes 884744 | tf_op jit(solution)/shard_map/ppermute | solution.py:49
  61.4 1.3 select_bitcast_fusion.5
  62.7 1.2 pad_maximum_fusion.1
  64.4 1.9 collective-permute-done.11.refs_3_
  67.0 0.9 vectors.1.vec_ref.refs_6_
  67.9 9.0 %qkv.1 = (bf16[768,384]{1,0:T(8,128)(2,1)}, bf16[1536,384]{1,0:T(8,128)(2,1)}, bf16[1536,384]{1,0:T(8,128)(2,1)}, bf16[768,1536]{1,0:T(8,128)(2,1)}, bf16[1536,7...) custom-call(s32[4]{0:T(128)S(1)} %pad_add_fusion.place, ...), custom_call_target="tpu_custom_call" | custom-call | flops 1000 | bytes 1000 | tf_op jit(solution)/shard_map/qkv/pallas_call | solution.py:171
  77.6 1.7 collective-permute-start.14
  79.3 1.9 collective-permute-start.15
  81.6 12.5 %attn_fwd.1 = (f32[768,384]{1,0:T(8,128)}, bf16[768,384]{1,0:T(8,128)(2,1)S(1)}, f32[3,2,768]{2,1,0:T(2,128)S(1)}) custom-call(bf16[768,384]{1,0:T(8,128)(2,1)} %get-tuple-element.143.q_ref, bf16[1536,384]{1,0:T(8,128)(2,1)} %get-tuple-element.144.k_ref, bf16[1536,384]{1,0:T(8,128)(2,1)} %get-tuple-element.145.v_ref, ...), custom_call_target="tpu_custom_call" | custom-call | flops 1000 | bytes 1000 | tf_op jit(solution)/shard_map/attn_fwd/pallas_call | solution.py:328
  94.7 2.8 %collective-permute-done.14.refs_1_ = bf16[4,96,768]{2,1,0:T(8,128)(2,1)S(1)} collective-permute-done((bf16[4,96,768]{2,1,0:T(8,128)(2,1)}, bf16[4,96,768]{2,1,0:T(8,128)(2,1)S(1)}, u32[]{:S(2)}, u32[]{:S(2)}) %collective-permute-start.14) | collective-permute-done | bytes 589856 | tf_op jit(solution)/shard_map/ppermute | solution.py:49
  97.6 0.8 copy-done.15
  98.3 0.8 slice.274
  99.1 1.5 collective-permute-start.16
  101.9 1.4 slice.333
  103.3 5.4 %out_proj.1 = (f32[768,768]{1,0:T(8,128)}, bf16[768,768]{1,0:T(8,128)(2,1)}, bf16[768,768]{1,0:T(8,128)(2,1)}, f32[768,128]{1,0:T(8,128)}) custom-call(s32[4]{0:T(128)S(1)} %pad_add_fusion.place, bf16[1536,768]{1,0:T(8,128)(2,1)S(1)} %pad_maximum_fusion.x_ref, bf16[2,384,768]{2,1,0:T(8,128)(2,1)S(1)} %bitcast.159, f32[16,768]{1,0:T(8,128)S(1)} %copy-done.3, ...), custom_call_target="tpu_custom_call" | custom-call | flops 1000 | bytes 1000 | tf_op jit(solution)/shard_map/out_proj/pallas_call | solution.py:171
  109.3 20.7 %feed_forward.1 = (bf16[4,4,192,768]{3,2,1,0:T(8,128)(2,1)}, f32[2,1,768]{2,1,0:T(1,128)S(1)}, f32[768,768]{1,0:T(8,128)}, f32[768,768]{1,0:T(8,128)S(1)}, bf16[768,768]{1,0:T(8,128)(2,1)S(1)}) custom-call(s32[4]{0:T(128)S(1)} %pad_add_fusion.place, bf16[768,768]{1,0:T(8,128)(2,1)} %get-tuple-element.147.h2_ref, bf16[768,768]{1,0:T(8,128)(2,1)} %bitcast.161, ...), custom_call_target="tpu_custom_call" | custom-call | flops 1000 | bytes 1000 | tf_op jit(solution)/shard_map/feed_forward/pallas_call | solution.py:171
  130.1 1.9 slice_bitcast_fusion.1
  132.0 0.8 collective-permute-start.19
  133.5 4.3 %out_back.1 = (f32[768,768]{1,0:T(8,128)}, bf16[768,768]{1,0:T(8,128)(2,1)S(1)}, bf16[768,384]{1,0:T(8,128)(2,1)S(1)}, f32[8,768]{1,0:T(8,128)S(1)}) custom-call(s32[4]{0:T(128)S(1)} %pad_add_fusion.place, f32[768,768]{1,0:T(8,128)S(1)} %get-tuple-element.153.mine_ref, bf16[768,768]{1,0:T(8,128)(2,1)S(1)} %collective-permute-done.18.got_ref, ...), custom_call_target="tpu_custom_call" | custom-call | flops 1000 | bytes 1000 | tf_op jit(solution)/shard_map/out_back/pallas_call | solution.py:171
  137.8 7.2 %attn_bwd.2 = (bf16[768,128]{1,0:T(8,128)(2,1)S(1)}, bf16[1536,128]{1,0:T(8,128)(2,1)S(1)}, bf16[1536,128]{1,0:T(8,128)(2,1)S(1)}) custom-call(bf16[768,384]{1,0:T(8,128)(2,1)} %get-tuple-element.143.q_ref, bf16[1536,384]{1,0:T(8,128)(2,1)} %get-tuple-element.144.k_ref, bf16[1536,384]{1,0:T(8,128)(2,1)} %get-tuple-element.145.v_ref, ...), custom_call_target="tpu_custom_call" | custom-call | flops 1000 | bytes 1000 | tf_op jit(solution)/shard_map/attn_bwd/pallas_call | solution.py:406
  145.0 2.7 %collective-permute-done.19 = bf16[2,192,768]{2,1,0:T(8,128)(2,1)S(1)} collective-permute-done((bf16[2,192,768]{2,1,0:T(8,128)(2,1)S(1)}, bf16[2,192,768]{2,1,0:T(8,128)(2,1)S(1)}, u32[]{:S(2)}, u32[]{:S(2)}) %collective-permute-start.19) | collective-permute-done | bytes 589856 | tf_op jit(solution)/shard_map/ppermute | solution.py:49
  148.6 1.4 collective-permute-start.22
  150.1 0.9 collective-permute-start.21
  151.0 13.8 %attn_bwd.3 = (bf16[768,256]{1,0:T(8,128)(2,1)S(1)}, bf16[1536,256]{1,0:T(8,128)(2,1)S(1)}, bf16[1536,256]{1,0:T(8,128)(2,1)S(1)}) custom-call(bf16[768,384]{1,0:T(8,128)(2,1)} %get-tuple-element.143.q_ref, bf16[1536,384]{1,0:T(8,128)(2,1)} %get-tuple-element.144.k_ref, bf16[1536,384]{1,0:T(8,128)(2,1)} %get-tuple-element.145.v_ref, ...), custom_call_target="tpu_custom_call" | custom-call | flops 1000 | bytes 1000 | tf_op jit(solution)/shard_map/attn_bwd/pallas_call | solution.py:406
  164.8 7.3 %matrix_grads.1 = bf16[4,4,4,48,384]{4,3,2,1,0:T(8,128)(2,1)} custom-call(s32[4]{0:T(128)S(1)} %pad_add_fusion.place, bf16[768,1536]{1,0:T(8,128)(2,1)} %get-tuple-element.169.h1t_ref, bf16[768,768]{1,0:T(8,128)(2,1)S(1)} %get-tuple-element.170.d_ref, bf16[768,384]{1,0:T(8,128)(2,1)S(1)} %get-tuple-element.146.refs_0_, ...), custom_call_target="tpu_custom_call" | custom-call | flops 1000 | bytes 1000 | tf_op jit(solution)/shard_map/matrix_grads/pallas_call | solution.py:171
  172.1 3.8 %collective-permute-done.22 = bf16[4,192,768]{2,1,0:T(8,128)(2,1)S(1)} collective-permute-done((bf16[4,192,768]{2,1,0:T(8,128)(2,1)S(1)}, bf16[4,192,768]{2,1,0:T(8,128)(2,1)S(1)}, u32[]{:S(2)}, u32[]{:S(2)}) %collective-permute-start.22) | collective-permute-done | bytes 1179680 | tf_op jit(solution)/shard_map/ppermute | solution.py:49
  175.9 1.2 collective-permute-done.21
  177.7 0.8 collective-permute-start.23
  178.5 0.8 collective-permute-start.24
  179.3 3.6 %collective-permute-start.25 = (bf16[192,768]{1,0:T(8,128)(2,1)S(1)}, bf16[192,768]{1,0:T(8,128)(2,1)S(1)}, u32[]{:S(2)}, u32[]{:S(2)}) collective-permute-start(bf16[192,768]{1,0:T(8,128)(2,1)S(1)} %get-tuple-element.238), channel_id=1, source_target_pairs={{0,8},{1,9},{2,10},{3,11},{4,12},{5,13},{6,14},{7,15},{8,16},{9,17... | collective-permute-start | bytes 884744 | tf_op jit(solution)/shard_map/ppermute | solution.py:49
  183.6 7.8 %input_back.1 = (f32[768,768]{1,0:T(8,128)}, bf16[784,768]{1,0:T(8,128)(2,1)S(1)}, f32[16,768]{1,0:T(8,128)S(1)}) custom-call(s32[4]{0:T(128)S(1)} %pad_add_fusion.place, bf16[768,128]{1,0:T(8,128)(2,1)S(1)} %get-tuple-element.173.refs_2_.refs_0_, bf16[1536,128]{1,0:T(8,128)(2,1)S(1)} %get-tuple-element.174.refs_3_.refs_1_, ...), custom_call_target="tpu_custom_call" | custom-call | flops 1000 | bytes 1000 | tf_op jit(solution)/shard_map/input_back/pallas_call | solution.py:171
  191.7 2.9 %collective-permute-done.26 = bf16[192,768]{1,0:T(8,128)(2,1)S(1)} collective-permute-done((bf16[192,768]{1,0:T(8,128)(2,1)S(1)}, bf16[192,768]{1,0:T(8,128)(2,1)S(1)}, u32[]{:S(2)}, u32[]{:S(2)}) %collective-permute-start.26) | collective-permute-done | bytes 294944 | tf_op jit(solution)/shard_map/ppermute | solution.py:49
  194.6 1.7 collective-permute-start.30
  196.4 0.8 collective-permute-start.31
  198.0 1.3 collective-permute-start.29
  199.3 11.1 %collective-permute-done.30 = bf16[4,4,48,384]{3,2,1,0:T(8,128)(2,1)S(1)} collective-permute-done((bf16[4,4,48,384]{3,2,1,0:T(8,128)(2,1)S(1)}, bf16[4,4,48,384]{3,2,1,0:T(8,128)(2,1)S(1)}, u32[]{:S(2)}, u32[]{:S(2)}) %collective-permute-start.30) | collective-permute-done | bytes 589856 | tf_op jit(solution)/shard_map/ppermute | solution.py:49
  210.4 2.2 collective-permute-done.31
  214.4 2.9 %collective-permute-start.33 = (bf16[224,384]{1,0:T(8,128)(2,1)S(1)}, bf16[224,384]{1,0:T(8,128)(2,1)S(1)}, u32[]{:S(2)}, u32[]{:S(2)}) collective-permute-start(bf16[224,384]{1,0:T(8,128)(2,1)S(1)} %get-tuple-element.242), channel_id=1, source_target_pairs={{0,16},{1,17},{2,18},{3,19},{4,20},{5,21},{6,22},{7,23},{8,24},{9,... | collective-permute-start | bytes 516104 | tf_op jit(solution)/shard_map/ppermute | solution.py:49
  217.3 0.9 collective-permute-start.34
  218.2 1.7 last_ff.1
  219.9 4.6 %collective-permute-done.29.refs_2_ = bf16[384,768]{1,0:T(8,128)(2,1)S(1)} collective-permute-done((bf16[384,768]{1,0:T(8,128)(2,1)S(1)}, bf16[384,768]{1,0:T(8,128)(2,1)S(1)}, u32[]{:S(2)}, u32[]{:S(2)}) %collective-permute-start.29) | collective-permute-done | bytes 589856 | tf_op jit(solution)/shard_map/ppermute | solution.py:49
  224.5 4.1 %finish.1 = f32[384,768]{1,0:T(8,128)} custom-call(s32[4]{0:T(128)S(1)} %pad_add_fusion.place, f32[768,768]{1,0:T(8,128)} %get-tuple-element.183.refs_0_, bf16[784,768]{1,0:T(8,128)(2,1)S(1)} %collective-permute-done.27.refs_1_, bf16[384,768]{1,0:T(8,128)(2,1)S(1)} %collective-permute-done.29.refs_2_, bf16[1536,768]{1,0:T(8,128)(2,1)S(1)} %copy-done.1, ...), custom_call_target="tpu_custom_call" | custom-call | flops 1000 | bytes 1000 | tf_op jit(solution)/shard_map/finish/pallas_call | solution.py:171
  228.6 1.1 fusion.13
  230.6 3.9 %collective-permute-done.38 = f32[32,384]{1,0:T(8,128)S(1)} collective-permute-done((f32[32,384]{1,0:T(8,128)S(1)}, f32[32,384]{1,0:T(8,128)S(1)}, u32[]{:S(2)}, u32[]{:S(2)}) %collective-permute-start.38) | collective-permute-done | bytes 49184 | tf_op jit(solution)/shard_map/ppermute | solution.py:49
  234.5 1.3 collective-permute-start.39
  235.7 2.9 %collective-permute-done.39 = f32[32,384]{1,0:T(8,128)S(1)} collective-permute-done((f32[32,384]{1,0:T(8,128)S(1)}, f32[32,384]{1,0:T(8,128)S(1)}, u32[]{:S(2)}, u32[]{:S(2)}) %collective-permute-start.39) | collective-permute-done | bytes 49184 | tf_op jit(solution)/shard_map/ppermute | solution.py:49
  238.6 1.8 last_rest.1
  (209 shorter events, 16.6 us)
Async XLA Ops:
  7.2 5.0 %copy-start.25 = (bf16[24,2304]{1,0:T(8,128)(2,1)S(1)}, bf16[24,2304]{1,0:T(8,128)(2,1)}, u32[]{:S(2)}) copy-start(bf16[24,2304]{1,0:T(8,128)(2,1)} %param.23) | copy-start | bytes 331780
  7.2 5.8 %copy-start.27 = (bf16[48]{0:T(256)(128)(2,1)S(1)}, bf16[48]{0:T(256)(128)(2,1)}, u32[]{:S(2)}) copy-start(bf16[48]{0:T(256)(128)(2,1)} %param.24) | copy-start | bytes 292
  7.2 5.9 %copy-start.28 = (bf16[24]{0:T(256)(128)(2,1)S(1)}, bf16[24]{0:T(256)(128)(2,1)}, u32[]{:S(2)}) copy-start(bf16[24]{0:T(256)(128)(2,1)} %param.32) | copy-start | bytes 148
  7.2 6.0 %copy-start.29 = (bf16[24]{0:T(256)(128)(2,1)S(1)}, bf16[24]{0:T(256)(128)(2,1)}, u32[]{:S(2)}) copy-start(bf16[24]{0:T(256)(128)(2,1)} %param.28) | copy-start | bytes 148
  7.2 6.0 %copy-start.30 = (bf16[24]{0:T(256)(128)(2,1)S(1)}, bf16[24]{0:T(256)(128)(2,1)}, u32[]{:S(2)}) copy-start(bf16[24]{0:T(256)(128)(2,1)} %param.27) | copy-start | bytes 148
  7.2 6.1 %copy-start.31 = (bf16[24]{0:T(256)(128)(2,1)S(1)}, bf16[24]{0:T(256)(128)(2,1)}, u32[]{:S(2)}) copy-start(bf16[24]{0:T(256)(128)(2,1)} %param.26) | copy-start | bytes 148
  7.2 6.2 %copy-start.32 = (bf16[24]{0:T(256)(128)(2,1)S(1)}, bf16[24]{0:T(256)(128)(2,1)}, u32[]{:S(2)}) copy-start(bf16[24]{0:T(256)(128)(2,1)} %param.22) | copy-start | bytes 148
  7.3 6.3 %copy-start.33 = (bf16[24]{0:T(256)(128)(2,1)S(1)}, bf16[24]{0:T(256)(128)(2,1)}, u32[]{:S(2)}) copy-start(bf16[24]{0:T(256)(128)(2,1)} %param.21) | copy-start | bytes 148
  7.3 94.6 %all-gather.3.cloned.1.call-start = ((), (), s32[]{:S(2)}) async-start(), calls=%async_computation.1 | async-start | bytes 6082560 | tf_op jit(solution)/shard_map/all_gather | solution.py:1106
  9.0 5.0 %copy-start.34 = (bf16[96]{0:T(256)(128)(2,1)S(1)}, bf16[96]{0:T(256)(128)(2,1)}, u32[]{:S(2)}) copy-start(bf16[96]{0:T(256)(128)(2,1)} %param.30) | copy-start | bytes 580
  9.0 5.0 %copy-start.26 = (s32[1,384]{1,0:T(1,128)S(1)}, s32[1,384]{1,0:T(1,128)}, u32[]{:S(2)}) copy-start(s32[1,384]{1,0:T(1,128)} %param.20) | copy-start | bytes 4612
  9.0 5.0 %copy-start.22 = (bf16[1,384,768]{2,1,0:T(8,128)(2,1)S(1)}, bf16[1,384,768]{2,1,0:T(8,128)(2,1)}, u32[]{:S(2)}) copy-start(bf16[1,384,768]{2,1,0:T(8,128)(2,1)} %param.19) | copy-start | bytes 1769476
  11.7 6.2 %collective-permute-start.6 = (bf16[24,1536]{1,0:T(8,128)(2,1)S(1)}, bf16[24,1536]{1,0:T(8,128)(2,1)S(1)}, u32[]{:S(2)}, u32[]{:S(2)}) collective-permute-start(bf16[24,1536]{1,0:T(8,128)(2,1)S(1)} %reshape.218), channel_id=1, source_target_pairs={{0,1},{1,0},{2,3},{3,2},{4,5},{5,4},{6,7},{7,6},{8,9},{9,8},{10,11... | collective-permute-start | bytes 221192 | tf_op jit(solution)/shard_map/ppermute | solution.py:49
  13.7 1.4 collective-permute-start
  15.1 19.8 %collective-permute-start.4 = (bf16[400,768]{1,0:T(8,128)(2,1)S(1)}, bf16[400,768]{1,0:T(8,128)(2,1)S(1)}, u32[]{:S(2)}, u32[]{:S(2)}) collective-permute-start(bf16[400,768]{1,0:T(8,128)(2,1)S(1)} %fusion.11), channel_id=1, source_target_pairs={{0,2},{1,3},{2,0},{3,1},{4,6},{5,7},{6,4},{7,5},{8,10},{9,11},{10,... | collective-permute-start | bytes 1843208 | tf_op jit(solution)/shard_map/ppermute | solution.py:49
  17.8 17.1 %collective-permute-start.5 = (bf16[400,768]{1,0:T(8,128)(2,1)S(1)}, bf16[400,768]{1,0:T(8,128)(2,1)S(1)}, u32[]{:S(2)}, u32[]{:S(2)}) collective-permute-start(bf16[400,768]{1,0:T(8,128)(2,1)S(1)} %fusion.11), channel_id=1, source_target_pairs={{0,1},{1,0},{2,3},{3,2},{4,5},{5,4},{6,7},{7,6},{8,9},{9,8},{10,11... | collective-permute-start | bytes 1843208 | tf_op jit(solution)/shard_map/ppermute | solution.py:49
  17.9 8.6 %collective-permute-start.1 = (bf16[64,1152]{1,0:T(8,128)(2,1)S(1)}, bf16[64,1152]{1,0:T(8,128)(2,1)S(1)}, u32[]{:S(2)}, u32[]{:S(2)}) collective-permute-start(bf16[64,1152]{1,0:T(8,128)(2,1)S(1)} %fusion.21), channel_id=1, source_target_pairs={{0,8},{1,9},{2,10},{3,11},{4,12},{5,13},{6,14},{7,15},{8,16},{9,17... | collective-permute-start | bytes 442376 | tf_op jit(solution)/shard_map/ppermute | solution.py:49
  19.6 15.3 %collective-permute-start.2 = (bf16[64,1152]{1,0:T(8,128)(2,1)S(1)}, bf16[64,1152]{1,0:T(8,128)(2,1)S(1)}, u32[]{:S(2)}, u32[]{:S(2)}) collective-permute-start(bf16[64,1152]{1,0:T(8,128)(2,1)S(1)} %fusion.21), channel_id=1, source_target_pairs={{0,16},{1,17},{2,18},{3,19},{4,20},{5,21},{6,22},{7,23},{8,24},{9,... | collective-permute-start | bytes 442376 | tf_op jit(solution)/shard_map/ppermute | solution.py:49
  22.2 12.8 %collective-permute-start.3 = (bf16[64,1152]{1,0:T(8,128)(2,1)S(1)}, bf16[64,1152]{1,0:T(8,128)(2,1)S(1)}, u32[]{:S(2)}, u32[]{:S(2)}) collective-permute-start(bf16[64,1152]{1,0:T(8,128)(2,1)S(1)} %fusion.21), channel_id=1, source_target_pairs={{0,24},{1,25},{2,26},{3,27},{4,28},{5,29},{6,30},{7,31},{8,0},{9,1... | collective-permute-start | bytes 442376 | tf_op jit(solution)/shard_map/ppermute | solution.py:49
  26.5 20.2 %collective-permute-start.10 = (bf16[384,768]{1,0:T(8,128)(2,1)}, bf16[384,768]{1,0:T(8,128)(2,1)}, u32[]{:S(2)}, u32[]{:S(2)}) collective-permute-start(bf16[384,768]{1,0:T(8,128)(2,1)} %bitcast.23), channel_id=1, source_target_pairs={{0,1},{1,0},{2,3},{3,2},{4,5},{5,4},{6,7},{7,6},{8,9},{9,8},{10,11... | collective-permute-start | bytes 1769480 | tf_op jit(solution)/shard_map/ppermute | solution.py:49
  35.0 20.7 %collective-permute-start.9 = (bf16[400,768]{1,0:T(8,128)(2,1)S(1)}, bf16[400,768]{1,0:T(8,128)(2,1)}, u32[]{:S(2)}, u32[]{:S(2)}) collective-permute-start(bf16[400,768]{1,0:T(8,128)(2,1)S(1)} %collective-permute-done.4), channel_id=1, source_target_pairs={{0,1},{1,0},{2,3},{3,2},{4,5},{5,4},{6,7},{7,6},{8,9},{9,8},{10,11... | collective-permute-start | bytes 1843208 | tf_op jit(solution)/shard_map/ppermute | solution.py:49
  36.0 19.7 %copy-start.11 = (bf16[4,64,1152]{2,1,0:T(8,128)(2,1)}, bf16[4,64,1152]{2,1,0:T(8,128)(2,1)S(1)}, u32[]{:S(2)}) copy-start(bf16[4,64,1152]{2,1,0:T(8,128)(2,1)S(1)} %pad_maximum_fusion.4.refs_0_) | copy-start | bytes 1769476
  36.0 19.6 %collective-permute-start.7 = (bf16[4,64,1152]{2,1,0:T(8,128)(2,1)S(1)}, bf16[4,64,1152]{2,1,0:T(8,128)(2,1)S(1)}, u32[]{:S(2)}, u32[]{:S(2)}) collective-permute-start(bf16[4,64,1152]{2,1,0:T(8,128)(2,1)S(1)} %pad_maximum_fusion.4.refs_0_), channel_id=1, source_target_pairs={{0,4},{1,5},{2,6},{3,7},{4,0},{5,1},{6,2},{7,3},{8,12},{9,13},{10,... | collective-permute-start | bytes 1769480 | tf_op jit(solution)/shard_map/ppermute | solution.py:49
  37.5 18.1 %collective-permute-start.8 = (bf16[4,64,1152]{2,1,0:T(8,128)(2,1)S(1)}, bf16[4,64,1152]{2,1,0:T(8,128)(2,1)S(1)}, u32[]{:S(2)}, u32[]{:S(2)}) collective-permute-start(bf16[4,64,1152]{2,1,0:T(8,128)(2,1)S(1)} %pad_maximum_fusion.4.refs_0_), channel_id=1, source_target_pairs={{0,2},{1,3},{2,0},{3,1},{4,6},{5,7},{6,4},{7,5},{8,10},{9,11},{10,... | collective-permute-start | bytes 1769480 | tf_op jit(solution)/shard_map/ppermute | solution.py:49
  38.9 38.6 %all-to-all-start = ((bf16[4,96,768]{2,1,0:T(8,128)(2,1)}), bf16[4,96,768]{2,1,0:T(8,128)(2,1)}, u32[]{:S(2)}, u32[]{:S(2)}) async-start(bf16[4,96,768]{2,1,0:T(8,128)(2,1)} %broadcast_in_dim.35), calls=%async_computation | async-start | bytes 1179648 | tf_op jit(solution)/shard_map/all_to_all | solution.py:137
  46.7 10.5 %copy-start.18 = (bf16[400,768]{1,0:T(8,128)(2,1)S(1)}, bf16[400,768]{1,0:T(8,128)(2,1)}, u32[]{:S(2)}) copy-start(bf16[400,768]{1,0:T(8,128)(2,1)} %copy-done.17) | copy-start | bytes 1843204
  46.7 10.5 %copy-start.20 = (bf16[400,768]{1,0:T(8,128)(2,1)S(1)}, bf16[400,768]{1,0:T(8,128)(2,1)}, u32[]{:S(2)}) copy-start(bf16[400,768]{1,0:T(8,128)(2,1)} %copy-done.19) | copy-start | bytes 1843204
  58.5 7.7 %collective-permute-start.11 = (bf16[2,64,1152]{2,1,0:T(8,128)(2,1)}, bf16[2,64,1152]{2,1,0:T(8,128)(2,1)S(1)}, u32[]{:S(2)}, u32[]{:S(2)}) collective-permute-start(bf16[2,64,1152]{2,1,0:T(8,128)(2,1)} %slice.267), channel_id=1, source_target_pairs={{0,2},{1,3},{2,0},{3,1},{4,6},{5,7},{6,4},{7,5},{8,10},{9,11},{10,... | collective-permute-start | bytes 884744 | tf_op jit(solution)/shard_map/ppermute | solution.py:49
  58.6 7.8 %collective-permute-start.12 = (bf16[2,64,1152]{2,1,0:T(8,128)(2,1)}, bf16[2,64,1152]{2,1,0:T(8,128)(2,1)S(1)}, u32[]{:S(2)}, u32[]{:S(2)}) collective-permute-start(bf16[2,64,1152]{2,1,0:T(8,128)(2,1)} %slice.269), channel_id=1, source_target_pairs={{0,4},{1,5},{2,6},{3,7},{4,0},{5,1},{6,2},{7,3},{8,12},{9,13},{10,... | collective-permute-start | bytes 884744 | tf_op jit(solution)/shard_map/ppermute | solution.py:49
  77.6 20.0 %collective-permute-start.14 = (bf16[4,96,768]{2,1,0:T(8,128)(2,1)}, bf16[4,96,768]{2,1,0:T(8,128)(2,1)S(1)}, u32[]{:S(2)}, u32[]{:S(2)}) collective-permute-start(bf16[4,96,768]{2,1,0:T(8,128)(2,1)} %all-to-all-done.refs_0_), channel_id=1, source_target_pairs={{0,4},{1,5},{2,6},{3,7},{4,0},{5,1},{6,2},{7,3},{8,12},{9,13},{10,... | collective-permute-start | bytes 1769480 | tf_op jit(solution)/shard_map/ppermute | solution.py:49
  79.3 18.3 %collective-permute-start.15 = (bf16[4,96,768]{2,1,0:T(8,128)(2,1)}, bf16[4,96,768]{2,1,0:T(8,128)(2,1)S(1)}, u32[]{:S(2)}, u32[]{:S(2)}) collective-permute-start(bf16[4,96,768]{2,1,0:T(8,128)(2,1)} %all-to-all-done.refs_0_), channel_id=1, source_target_pairs={{0,2},{1,3},{2,0},{3,1},{4,6},{5,7},{6,4},{7,5},{8,10},{9,11},{10,... | collective-permute-start | bytes 1769480 | tf_op jit(solution)/shard_map/ppermute | solution.py:49
  94.7 8.6 %collective-permute-start.13 = (bf16[768,384]{1,0:T(8,128)(2,1)S(1)}, bf16[768,384]{1,0:T(8,128)(2,1)}, u32[]{:S(2)}, u32[]{:S(2)}) collective-permute-start(bf16[768,384]{1,0:T(8,128)(2,1)S(1)} %get-tuple-element.146.refs_0_), channel_id=1, source_target_pairs={{0,1},{1,0},{2,3},{3,2},{4,5},{5,4},{6,7},{7,6},{8,9},{9,8},{10,11... | collective-permute-start | bytes 1769480 | tf_op jit(solution)/shard_map/ppermute | solution.py:49
  99.1 9.5 %collective-permute-start.16 = (bf16[2,96,768]{2,1,0:T(8,128)(2,1)}, bf16[2,96,768]{2,1,0:T(8,128)(2,1)}, u32[]{:S(2)}, u32[]{:S(2)}) collective-permute-start(bf16[2,96,768]{2,1,0:T(8,128)(2,1)} %slice.274), channel_id=1, source_target_pairs={{0,2},{1,3},{2,0},{3,1},{4,6},{5,7},{6,4},{7,5},{8,10},{9,11},{10,... | collective-permute-start | bytes 884744 | tf_op jit(solution)/shard_map/ppermute | solution.py:49
  101.3 7.9 %collective-permute-start.17 = (bf16[2,96,768]{2,1,0:T(8,128)(2,1)}, bf16[2,96,768]{2,1,0:T(8,128)(2,1)}, u32[]{:S(2)}, u32[]{:S(2)}) collective-permute-start(bf16[2,96,768]{2,1,0:T(8,128)(2,1)} %slice.275), channel_id=1, source_target_pairs={{0,4},{1,5},{2,6},{3,7},{4,0},{5,1},{6,2},{7,3},{8,12},{9,13},{10,... | collective-permute-start | bytes 884744 | tf_op jit(solution)/shard_map/ppermute | solution.py:49
  129.9 3.5 %collective-permute-start.18 = (bf16[768,768]{1,0:T(8,128)(2,1)S(1)}, bf16[768,768]{1,0:T(8,128)(2,1)S(1)}, u32[]{:S(2)}, u32[]{:S(2)}) collective-permute-start(bf16[768,768]{1,0:T(8,128)(2,1)S(1)} %get-tuple-element.154), channel_id=1, source_target_pairs={{0,1},{1,0},{2,3},{3,2},{4,5},{5,4},{6,7},{7,6},{8,9},{9,8},{10,11... | collective-permute-start | bytes 3538952 | tf_op jit(solution)/shard_map/ppermute | solution.py:49
  130.0 18.1 %slice-start = ((s8[4718592]{0:T(1024)(128)(4,1)}), s8[4194304]{0:T(1024)(128)(4,1)S(1)}, s32[]{:S(2)}) async-start(s8[4718592]{0:T(1024)(128)(4,1)} %bitcast.167), calls=%async_computation.2 | async-start | bytes 8388608
  132.0 15.8 %collective-permute-start.19 = (bf16[2,192,768]{2,1,0:T(8,128)(2,1)S(1)}, bf16[2,192,768]{2,1,0:T(8,128)(2,1)S(1)}, u32[]{:S(2)}, u32[]{:S(2)}) collective-permute-start(bf16[2,192,768]{2,1,0:T(8,128)(2,1)S(1)} %get-tuple-element.224), channel_id=1, source_target_pairs={{0,2},{1,3},{2,0},{3,1},{4,6},{5,7},{6,4},{7,5},{8,10},{9,11},{10,... | collective-permute-start | bytes 1769480 | tf_op jit(solution)/shard_map/ppermute | solution.py:49
  132.7 15.4 %collective-permute-start.20 = (bf16[2,192,768]{2,1,0:T(8,128)(2,1)S(1)}, bf16[2,192,768]{2,1,0:T(8,128)(2,1)S(1)}, u32[]{:S(2)}, u32[]{:S(2)}) collective-permute-start(bf16[2,192,768]{2,1,0:T(8,128)(2,1)S(1)} %get-tuple-element.222), channel_id=1, source_target_pairs={{0,4},{1,5},{2,6},{3,7},{4,0},{5,1},{6,2},{7,3},{8,12},{9,13},{10,... | collective-permute-start | bytes 1769480 | tf_op jit(solution)/shard_map/ppermute | solution.py:49
  133.5 4.3 %copy-start.8 = (f32[3,2,768]{2,1,0:T(2,128)S(1)}, f32[3,2,768]{2,1,0:T(2,128)}, u32[]{:S(2)}) copy-start(f32[3,2,768]{2,1,0:T(2,128)} %copy-done.7) | copy-start | bytes 55300
  133.5 14.7 %slice-start.1 = ((s8[4718592]{0:T(1024)(128)(4,1)}), s8[524288]{0:T(1024)(128)(4,1)S(1)}, s32[]{:S(2)}) async-start(s8[4718592]{0:T(1024)(128)(4,1)} %bitcast.167), calls=%async_computation.3 | async-start | bytes 1048576
  148.6 27.3 %collective-permute-start.22 = (bf16[4,192,768]{2,1,0:T(8,128)(2,1)S(1)}, bf16[4,192,768]{2,1,0:T(8,128)(2,1)S(1)}, u32[]{:S(2)}, u32[]{:S(2)}) collective-permute-start(bf16[4,192,768]{2,1,0:T(8,128)(2,1)S(1)} %pad_maximum_fusion.3), channel_id=1, source_target_pairs={{0,2},{1,3},{2,0},{3,1},{4,6},{5,7},{6,4},{7,5},{8,10},{9,11},{10,... | collective-permute-start | bytes 3538952 | tf_op jit(solution)/shard_map/ppermute | solution.py:49
  150.1 27.0 %collective-permute-start.21 = (bf16[4,192,768]{2,1,0:T(8,128)(2,1)S(1)}, bf16[4,192,768]{2,1,0:T(8,128)(2,1)S(1)}, u32[]{:S(2)}, u32[]{:S(2)}) collective-permute-start(bf16[4,192,768]{2,1,0:T(8,128)(2,1)S(1)} %pad_maximum_fusion.2), channel_id=1, source_target_pairs={{0,4},{1,5},{2,6},{3,7},{4,0},{5,1},{6,2},{7,3},{8,12},{9,13},{10,... | collective-permute-start | bytes 3538952 | tf_op jit(solution)/shard_map/ppermute | solution.py:49
  172.1 5.4 %copy-start.9 = (bf16[4,4,4,48,384]{4,3,2,1,0:T(8,128)(2,1)S(1)}, bf16[4,4,4,48,384]{4,3,2,1,0:T(8,128)(2,1)}, u32[]{:S(2)}) copy-start(bf16[4,4,4,48,384]{4,3,2,1,0:T(8,128)(2,1)} %matrix_grads.1) | copy-start | bytes 7077892
  177.7 13.6 %collective-permute-start.23 = (bf16[2,4,48,384]{3,2,1,0:T(8,128)(2,1)S(1)}, bf16[2,4,48,384]{3,2,1,0:T(8,128)(2,1)S(1)}, u32[]{:S(2)}, u32[]{:S(2)}) collective-permute-start(bf16[2,4,48,384]{3,2,1,0:T(8,128)(2,1)S(1)} %get-tuple-element.230), channel_id=1, source_target_pairs={{0,2},{1,3},{2,0},{3,1},{4,6},{5,7},{6,4},{7,5},{8,10},{9,11},{10,... | collective-permute-start | bytes 884744 | tf_op jit(solution)/shard_map/ppermute | solution.py:49
  178.5 12.9 %collective-permute-start.24 = (bf16[2,4,48,384]{3,2,1,0:T(8,128)(2,1)S(1)}, bf16[2,4,48,384]{3,2,1,0:T(8,128)(2,1)S(1)}, u32[]{:S(2)}, u32[]{:S(2)}) collective-permute-start(bf16[2,4,48,384]{3,2,1,0:T(8,128)(2,1)S(1)} %get-tuple-element.228), channel_id=1, source_target_pairs={{0,4},{1,5},{2,6},{3,7},{4,0},{5,1},{6,2},{7,3},{8,12},{9,13},{10,... | collective-permute-start | bytes 884744 | tf_op jit(solution)/shard_map/ppermute | solution.py:49
  179.3 12.3 %collective-permute-start.25 = (bf16[192,768]{1,0:T(8,128)(2,1)S(1)}, bf16[192,768]{1,0:T(8,128)(2,1)S(1)}, u32[]{:S(2)}, u32[]{:S(2)}) collective-permute-start(bf16[192,768]{1,0:T(8,128)(2,1)S(1)} %get-tuple-element.238), channel_id=1, source_target_pairs={{0,8},{1,9},{2,10},{3,11},{4,12},{5,13},{6,14},{7,15},{8,16},{9,17... | collective-permute-start | bytes 884744 | tf_op jit(solution)/shard_map/ppermute | solution.py:49
  182.9 11.7 %collective-permute-start.26 = (bf16[192,768]{1,0:T(8,128)(2,1)S(1)}, bf16[192,768]{1,0:T(8,128)(2,1)S(1)}, u32[]{:S(2)}, u32[]{:S(2)}) collective-permute-start(bf16[192,768]{1,0:T(8,128)(2,1)S(1)} %get-tuple-element.237), channel_id=1, source_target_pairs={{0,24},{1,25},{2,26},{3,27},{4,28},{5,29},{6,30},{7,31},{8,0},{9,1... | collective-permute-start | bytes 884744 | tf_op jit(solution)/shard_map/ppermute | solution.py:49
  191.5 6.4 %copy-start.10 = (f32[768,768]{1,0:T(8,128)S(1)}, f32[768,768]{1,0:T(8,128)}, u32[]{:S(2)}) copy-start(f32[768,768]{1,0:T(8,128)} %get-tuple-element.183.refs_0_) | copy-start | bytes 7077892
  194.6 3.2 %collective-permute-start.27 = (bf16[784,768]{1,0:T(8,128)(2,1)S(1)}, bf16[784,768]{1,0:T(8,128)(2,1)S(1)}, u32[]{:S(2)}, u32[]{:S(2)}) collective-permute-start(bf16[784,768]{1,0:T(8,128)(2,1)S(1)} %get-tuple-element.189), channel_id=1, source_target_pairs={{0,1},{1,0},{2,3},{3,2},{4,5},{5,4},{6,7},{7,6},{8,9},{9,8},{10,11... | collective-permute-start | bytes 3612680 | tf_op jit(solution)/shard_map/ppermute | solution.py:49
  194.6 15.7 %collective-permute-start.30 = (bf16[4,4,48,384]{3,2,1,0:T(8,128)(2,1)S(1)}, bf16[4,4,48,384]{3,2,1,0:T(8,128)(2,1)S(1)}, u32[]{:S(2)}, u32[]{:S(2)}) collective-permute-start(bf16[4,4,48,384]{3,2,1,0:T(8,128)(2,1)S(1)} %pad_maximum_fusion.5), channel_id=1, source_target_pairs={{0,4},{1,5},{2,6},{3,7},{4,0},{5,1},{6,2},{7,3},{8,12},{9,13},{10,... | collective-permute-start | bytes 1769480 | tf_op jit(solution)/shard_map/ppermute | solution.py:49
  196.4 16.2 %collective-permute-start.31 = (bf16[4,4,48,384]{3,2,1,0:T(8,128)(2,1)S(1)}, bf16[4,4,48,384]{3,2,1,0:T(8,128)(2,1)S(1)}, u32[]{:S(2)}, u32[]{:S(2)}) collective-permute-start(bf16[4,4,48,384]{3,2,1,0:T(8,128)(2,1)S(1)} %pad_maximum_fusion.6), channel_id=1, source_target_pairs={{0,2},{1,3},{2,0},{3,1},{4,6},{5,7},{6,4},{7,5},{8,10},{9,11},{10,... | collective-permute-start | bytes 1769480 | tf_op jit(solution)/shard_map/ppermute | solution.py:49
  197.2 16.1 %collective-permute-start.35 = (bf16[192,768]{1,0:T(8,128)(2,1)S(1)}, bf16[192,768]{1,0:T(8,128)(2,1)S(1)}, u32[]{:S(2)}, u32[]{:S(2)}) collective-permute-start(bf16[192,768]{1,0:T(8,128)(2,1)S(1)} %get-tuple-element.236), channel_id=1, source_target_pairs={{0,16},{1,17},{2,18},{3,19},{4,20},{5,21},{6,22},{7,23},{8,24},{9,... | collective-permute-start | bytes 884744 | tf_op jit(solution)/shard_map/ppermute | solution.py:49
  198.0 26.5 %collective-permute-start.29 = (bf16[384,768]{1,0:T(8,128)(2,1)S(1)}, bf16[384,768]{1,0:T(8,128)(2,1)S(1)}, u32[]{:S(2)}, u32[]{:S(2)}) collective-permute-start(bf16[384,768]{1,0:T(8,128)(2,1)S(1)} %add_convert_fusion), channel_id=1, source_target_pairs={{0,2},{1,3},{2,0},{3,1},{4,6},{5,7},{6,4},{7,5},{8,10},{9,11},{10,... | collective-permute-start | bytes 1769480 | tf_op jit(solution)/shard_map/ppermute | solution.py:49
  199.3 14.0 %copy-start.14 = (f32[768,768]{1,0:T(8,128)S(1)}, f32[768,768]{1,0:T(8,128)}, u32[]{:S(2)}) copy-start(f32[768,768]{1,0:T(8,128)} %get-tuple-element.190) | copy-start | bytes 7077892
  213.4 15.2 %collective-permute-start.28 = (bf16[384,768]{1,0:T(8,128)(2,1)S(1)}, bf16[384,768]{1,0:T(8,128)(2,1)S(1)}, u32[]{:S(2)}, u32[]{:S(2)}) collective-permute-start(bf16[384,768]{1,0:T(8,128)(2,1)S(1)} %fusion.12), channel_id=1, source_target_pairs={{0,1},{1,0},{2,3},{3,2},{4,5},{5,4},{6,7},{7,6},{8,9},{9,8},{10,11... | collective-permute-start | bytes 1769480 | tf_op jit(solution)/shard_map/ppermute | solution.py:49
  213.5 11.0 %copy-start.5 = (f32[1536,1]{1,0:T(8,128)S(1)}, f32[1536,1]{1,0:T(8,128)}, u32[]{:S(2)}) copy-start(f32[1536,1]{1,0:T(8,128)} %get-tuple-element.192.refs_4_) | copy-start | bytes 18436
  213.6 10.8 %copy-start.1 = (bf16[1536,768]{1,0:T(8,128)(2,1)S(1)}, bf16[1536,768]{1,0:T(8,128)(2,1)}, u32[]{:S(2)}) copy-start(bf16[1536,768]{1,0:T(8,128)(2,1)} %get-tuple-element.180.refs_7_.refs_3_) | copy-start | bytes 7077892
  213.7 3.6 %collective-permute-start.36 = (bf16[96,768]{1,0:T(8,128)(2,1)S(1)}, bf16[96,768]{1,0:T(8,128)(2,1)S(1)}, u32[]{:S(2)}, u32[]{:S(2)}) collective-permute-start(bf16[96,768]{1,0:T(8,128)(2,1)S(1)} %slice.393), channel_id=1, source_target_pairs={{0,1},{1,0},{2,3},{3,2},{4,5},{5,4},{6,7},{7,6},{8,9},{9,8},{10,11... | collective-permute-start | bytes 442376 | tf_op jit(solution)/shard_map/ppermute | solution.py:49
  214.3 15.3 %collective-permute-start.32 = (bf16[224,384]{1,0:T(8,128)(2,1)S(1)}, bf16[224,384]{1,0:T(8,128)(2,1)S(1)}, u32[]{:S(2)}, u32[]{:S(2)}) collective-permute-start(bf16[224,384]{1,0:T(8,128)(2,1)S(1)} %get-tuple-element.243), channel_id=1, source_target_pairs={{0,8},{1,9},{2,10},{3,11},{4,12},{5,13},{6,14},{7,15},{8,16},{9,17... | collective-permute-start | bytes 516104 | tf_op jit(solution)/shard_map/ppermute | solution.py:49
  214.4 15.6 %collective-permute-start.33 = (bf16[224,384]{1,0:T(8,128)(2,1)S(1)}, bf16[224,384]{1,0:T(8,128)(2,1)S(1)}, u32[]{:S(2)}, u32[]{:S(2)}) collective-permute-start(bf16[224,384]{1,0:T(8,128)(2,1)S(1)} %get-tuple-element.242), channel_id=1, source_target_pairs={{0,16},{1,17},{2,18},{3,19},{4,20},{5,21},{6,22},{7,23},{8,24},{9,... | collective-permute-start | bytes 516104 | tf_op jit(solution)/shard_map/ppermute | solution.py:49
  217.3 12.7 %collective-permute-start.34 = (bf16[224,384]{1,0:T(8,128)(2,1)S(1)}, bf16[224,384]{1,0:T(8,128)(2,1)S(1)}, u32[]{:S(2)}, u32[]{:S(2)}) collective-permute-start(bf16[224,384]{1,0:T(8,128)(2,1)S(1)} %get-tuple-element.241), channel_id=1, source_target_pairs={{0,24},{1,25},{2,26},{3,27},{4,28},{5,29},{6,30},{7,31},{8,0},{9,1... | collective-permute-start | bytes 516104 | tf_op jit(solution)/shard_map/ppermute | solution.py:49
  230.1 8.5 %collective-permute-start.37 = (bf16[4,48,384]{2,1,0:T(8,128)(2,1)S(1)}, bf16[4,48,384]{2,1,0:T(8,128)(2,1)S(1)}, u32[]{:S(2)}, u32[]{:S(2)}) collective-permute-start(bf16[4,48,384]{2,1,0:T(8,128)(2,1)S(1)} %get-tuple-element.218), channel_id=1, source_target_pairs={{0,1},{1,0},{2,3},{3,2},{4,5},{5,4},{6,7},{7,6},{8,9},{9,8},{10,11... | collective-permute-start | bytes 442376 | tf_op jit(solution)/shard_map/ppermute | solution.py:49
  230.2 4.2 %collective-permute-start.38 = (f32[32,384]{1,0:T(8,128)S(1)}, f32[32,384]{1,0:T(8,128)S(1)}, u32[]{:S(2)}, u32[]{:S(2)}) collective-permute-start(f32[32,384]{1,0:T(8,128)S(1)} %convert_add_fusion.10), channel_id=1, source_target_pairs={{0,4},{1,5},{2,6},{3,7},{4,0},{5,1},{6,2},{7,3},{8,12},{9,13},{10,... | collective-permute-start | bytes 147464 | tf_op jit(solution)/shard_map/ppermute | solution.py:49
  234.5 4.2 %collective-permute-start.39 = (f32[32,384]{1,0:T(8,128)S(1)}, f32[32,384]{1,0:T(8,128)S(1)}, u32[]{:S(2)}, u32[]{:S(2)}) collective-permute-start(f32[32,384]{1,0:T(8,128)S(1)} %add.206), channel_id=1, source_target_pairs={{0,2},{1,3},{2,0},{3,1},{4,6},{5,7},{6,4},{7,5},{8,10},{9,11},{10,... | collective-permute-start | bytes 147464 | tf_op jit(solution)/shard_map/ppermute | solution.py:49
  (15 other events, 31.2 us)
Sparse Core Ops, SparseCore 0:
  11.6 88.7 all-gather.2
